TPU v7x, 128 devices: a whole 4x4x4 slice. The times are simulated.
128 devices in a mesh: table: 64 (over z, y, x_hi, core), row: 2 (over x_lo).
Axes of the slice: x: 4 (x_hi: 2, x_lo: 2; x = x_hi * 2 + x_lo), y: 4, z: 4, core: 2. Of those that a mesh axis runs over, the one named last changes fastest.
Arguments:
- ids: int32 [4096, 512, 8], P(None, 'table'), may hold values from 0 to 511
- lengths: int32 [4096, 512], P(None, 'table'), may hold values from 1 to 8
- tables: bfloat16 [512, 512, 128], P('table', 'row'), may hold values from -5 to 5
- cross_down: bfloat16 [65536, 256], P('row'), may hold values from -0.0234375 to 0.0234375
- cross_up: bfloat16 [256, 65536], P(None, 'row'), may hold values from -0.375 to 0.375
- bias: float32 [65536], P('row'), may hold values from -4 to 4
- grad_out: bfloat16 [4096, 65536], P('table', 'row'), may hold values from -4 to 4
Outputs:
- crossed: bfloat16 [4096, 65536], P('table', 'row')
- table_grad: bfloat16 [512, 512, 128], P('table', 'row')
Inputs may be any that keep to these rules, and one draw needn't show every extreme that they name: ids index the rows of the feature's own table.
All inputs are finite; a program needn't handle non-finite values.
Results may differ from a plain program's by a relative error of at most 0.0061.
Values may be sent and summed in bfloat16 or wider, within the bound.
No kernel may reach another device: no remote copies, remote signals or barrier semaphores. Data moves between devices by JAX's collectives and lax.ppermute only.
A program may use at most 256 MiB of HBM per device.

v0:
```python
import jax
import jax.numpy as jnp
from jax import lax
from jax.sharding import PartitionSpec as P


def count_rows(local_ids, live_f, span):
    table_rows = jnp.arange(span, dtype=jnp.int32)
    total = jnp.zeros((local_ids.shape[0], span), jnp.bfloat16)
    for slot in range(local_ids.shape[1]):
        match = (local_ids[:, slot, None] == table_rows[None, :]) & live_f[:, slot, None]
        total = total + jnp.where(match, 1.0, 0.0).astype(jnp.bfloat16)
    return total


def body(ids, lengths, tables, cross_down, cross_up, bias, grad_out):
    batch, feats, bag = ids.shape
    width = tables.shape[2]
    shards = lax.axis_size("row")
    pair = feats // shards
    shard = lax.axis_index("row")
    live = jnp.arange(bag, dtype=jnp.int32)[None, None, :] < lengths[:, :, None]
    owned = lax.all_to_all(tables, "row", split_axis=0, concat_axis=1, tiled=True)
    own_ids = jnp.moveaxis(lax.dynamic_slice_in_dim(ids, shard * pair, pair, 1), 1, 0)
    own_live = jnp.moveaxis(lax.dynamic_slice_in_dim(live, shard * pair, pair, 1), 1, 0)
    counts = lax.map(
        lambda items: count_rows(items[0], items[1], owned.shape[1]), (own_ids, own_live)
    )
    pooled = jnp.einsum("kbr,kre->kbe", counts, owned, preferred_element_type=jnp.float32)
    outgoing = jnp.transpose(pooled.astype(jnp.bfloat16), (1, 0, 2)).reshape(batch, pair * width)
    x0 = lax.all_to_all(outgoing, "table", split_axis=0, concat_axis=1, tiled=True)
    low_part = jnp.dot(x0, cross_down, preferred_element_type=jnp.float32)
    low = lax.psum(low_part, "row").astype(jnp.bfloat16)
    gate = jnp.dot(low, cross_up, preferred_element_type=jnp.float32) + bias
    x0f = x0.astype(jnp.float32)
    crossed = (x0f * gate + x0f).astype(jnp.bfloat16)
    upstream = grad_out.astype(jnp.float32)
    dgate = (upstream * x0f).astype(jnp.bfloat16)
    dlow_part = lax.dot_general(
        dgate, cross_up, (((1,), (1,)), ((), ())), preferred_element_type=jnp.float32
    )
    dlow = lax.psum(dlow_part, "row").astype(jnp.bfloat16)
    spread = lax.dot_general(
        dlow, cross_down, (((1,), (1,)), ((), ())), preferred_element_type=jnp.float32
    )
    x0_grad = (upstream * gate + upstream + spread).astype(jnp.bfloat16)
    back = lax.all_to_all(x0_grad, "table", split_axis=1, concat_axis=0, tiled=True).reshape(
        batch, pair, width
    )
    full_grad = jnp.einsum("kbr,bke->kre", counts, back, preferred_element_type=jnp.float32).astype(
        jnp.bfloat16
    )
    table_grad = lax.all_to_all(full_grad, "row", split_axis=1, concat_axis=0, tiled=True)
    return (crossed, table_grad)


def solution(mesh):
    in_specs = (
        P(None, "table", None),
        P(None, "table"),
        P("table", "row", None),
        P("row", None),
        P(None, "row"),
        P("row"),
        P("table", "row"),
    )
    out_specs = (P("table", "row"), P("table", "row", None))
    return jax.shard_map(body, mesh=mesh, in_specs=in_specs, out_specs=out_specs, check_vma=False)
```

profile of v0, /device:TPU:1, one launch (start us, length us, event | category | flops | bytes accessed | tf_op | source)
XLA Modules:
  0.0 320.9 jit_solution(13985106837100581277)
XLA Ops:
  0.6 3.6 %all-to-all-start = ((bf16[8,256,128]{2,1,0:T(8,128)(2,1)}), bf16[8,256,128]{2,1,0:T(8,128)(2,1)S(1)}, u32[]{:S(2)}, u32[]{:S(2)}) async-start(bf16[8,256,128]{2,1,0:T(8,128)(2,1)} %param.11), calls=%async_computation | async-start | bytes 1048576 | tf_op jit(solution)/shard_map/all_to_all | solution.py:23
  4.4 0.9 constant_dynamic-slice_fusion
  5.4 72.8 %while.10 = (s32[]{:T(128)}, bf16[4,4096,512]{2,1,0:T(8,128)(2,1)}, s32[4,4096,8]{1,2,0:T(8,128)S(1)}, pred[4,4096,8]{1,2,0:T(8,128)(4,1)S(1)}, s32[]{:T(128)}) while((s32[]{:T(128)}, bf16[4,4096,512]{2,1,0:T(8,128)(2,1)}, s32[4,4096,8]{1,2,0:T(8,128)S(1)}, pred[4,4096,8]{1,2,0:T(8,128)(4,1)S(1)}, s32[]{:T(128)}) %tuple.41), condition=%wide.region_1.2_spmd, body=%wide.region_0.1_spmd.sunk | while | flops 100663296 | bytes 5014085 | solution.py:26
  5.4 0.1 fusion.44
  5.5 0.4 slice_reduce_fusion.9
  5.9 17.7 %fusion.45 = bf16[4,4096,512]{2,1,0:T(8,128)(2,1)} fusion(bf16[4,4096,512]{2,1,0:T(8,128)(2,1)} %get-tuple-element.116, s32[]{:T(128)} %get-tuple-element.115, s32[4096]{0:T(1024)S(1)} %bitcast.74, s32[4096]{0:T(1024)S(1)} %bitcast.75, s32[4096]{0:T(1024)S(1)} %bitcast.76, s32[4096]{0:T(1024)S(1)} %bitcast.77, s32[4096]{0:T(1024)S(1)} %bitcast.78, ...), kind=kLoop, calls=%fused_computation.31.clone.1 | loop fusion | flops 100663296 | bytes 4358656 | tf_op jit(solution)/shard_map/while/body/jit(dynamic_update_index_in_dim)/dynamic_update_slice | solution.py:26
  23.6 0.1 fusion.44
  23.7 0.4 slice_reduce_fusion.9
  24.1 17.7 %fusion.45 = bf16[4,4096,512]{2,1,0:T(8,128)(2,1)} fusion(bf16[4,4096,512]{2,1,0:T(8,128)(2,1)} %get-tuple-element.116, s32[]{:T(128)} %get-tuple-element.115, s32[4096]{0:T(1024)S(1)} %bitcast.74, s32[4096]{0:T(1024)S(1)} %bitcast.75, s32[4096]{0:T(1024)S(1)} %bitcast.76, s32[4096]{0:T(1024)S(1)} %bitcast.77, s32[4096]{0:T(1024)S(1)} %bitcast.78, ...), kind=kLoop, calls=%fused_computation.31.clone.1 | loop fusion | flops 100663296 | bytes 4358656 | tf_op jit(solution)/shard_map/while/body/jit(dynamic_update_index_in_dim)/dynamic_update_slice | solution.py:26
  41.8 0.1 fusion.44
  41.9 0.4 slice_reduce_fusion.9
  42.3 17.7 %fusion.45 = bf16[4,4096,512]{2,1,0:T(8,128)(2,1)} fusion(bf16[4,4096,512]{2,1,0:T(8,128)(2,1)} %get-tuple-element.116, s32[]{:T(128)} %get-tuple-element.115, s32[4096]{0:T(1024)S(1)} %bitcast.74, s32[4096]{0:T(1024)S(1)} %bitcast.75, s32[4096]{0:T(1024)S(1)} %bitcast.76, s32[4096]{0:T(1024)S(1)} %bitcast.77, s32[4096]{0:T(1024)S(1)} %bitcast.78, ...), kind=kLoop, calls=%fused_computation.31.clone.1 | loop fusion | flops 100663296 | bytes 4358656 | tf_op jit(solution)/shard_map/while/body/jit(dynamic_update_index_in_dim)/dynamic_update_slice | solution.py:26
  60.0 0.1 fusion.44
  60.1 0.4 slice_reduce_fusion.9
  60.5 17.7 %fusion.45 = bf16[4,4096,512]{2,1,0:T(8,128)(2,1)} fusion(bf16[4,4096,512]{2,1,0:T(8,128)(2,1)} %get-tuple-element.116, s32[]{:T(128)} %get-tuple-element.115, s32[4096]{0:T(1024)S(1)} %bitcast.74, s32[4096]{0:T(1024)S(1)} %bitcast.75, s32[4096]{0:T(1024)S(1)} %bitcast.76, s32[4096]{0:T(1024)S(1)} %bitcast.77, s32[4096]{0:T(1024)S(1)} %bitcast.78, ...), kind=kLoop, calls=%fused_computation.31.clone.1 | loop fusion | flops 100663296 | bytes 4358656 | tf_op jit(solution)/shard_map/while/body/jit(dynamic_update_index_in_dim)/dynamic_update_slice | solution.py:26
  78.2 12.3 %fusion.19 = bf16[4096,4,128]{2,0,1:T(8,128)(2,1)} fusion(bf16[4,4096,512]{2,1,0:T(8,128)(2,1)} %get-tuple-element.24, bf16[4,512,128]{2,1,0:T(8,128)(2,1)S(1)} %bitcast.82), kind=kOutput, calls=%fused_computation.51 | convolution fusion | flops 2149580800 | bytes 21495808 | tf_op jit(solution)/shard_map/kbr,kre->kbe/dot_general | solution.py:29
  90.5 7.6 %copy.20 = bf16[4096,4,128]{2,1,0:T(4,128)(2,1)} copy(bf16[4096,4,128]{2,0,1:T(8,128)(2,1)} %fusion.19) | data formatting | bytes 8388608 | tf_op jit(solution)/shard_map/convert_element_type | solution.py:30
  98.1 7.2 %all_to_all.56 = bf16[64,64,512]{2,1,0:T(8,128)(2,1)} reshape(bf16[4096,4,128]{2,1,0:T(4,128)(2,1)} %copy.20) | data formatting | bytes 8388608 | tf_op jit(solution)/shard_map/all_to_all | solution.py:31
  105.2 66.3 %all_to_all.71 = bf16[64,64,512]{2,1,0:T(8,128)(2,1)S(1)} all-to-all(bf16[64,64,512]{2,1,0:T(8,128)(2,1)} %all_to_all.56), channel_id=1, replica_groups=mesh['table'=64,'row'=2] {'table'}, dimensions={0} | all-to-all | bytes 8388608 | tf_op jit(solution)/shard_map/all_to_all | solution.py:31
  171.5 0.4 copy.29
  171.9 10.2 %fusion.20 = f32[64,256]{1,0:T(8,128)S(1)} fusion(bf16[256,32768]{1,0:T(8,128)(2,1)} %param.13, bf16[64,32768]{1,0:T(8,128)(2,1)S(1)} %bitcast.64, bf16[64,32768]{1,0:T(8,128)(2,1)S(1)} %copy-done.3), kind=kOutput, calls=%fused_computation.52 | convolution fusion | flops 1082130432 | bytes 25231360 | tf_op jit(solution)/shard_map/dot_general | solution.py:39
  182.2 8.6 %fusion.31 = f32[64,256]{1,0:T(8,128)S(1)} fusion(bf16[64,32768]{1,0:T(8,128)(2,1)S(1)} %bitcast.65, bf16[32768,256]{1,0:T(8,128)(2,1)} %param.12), kind=kOutput, calls=%fused_computation.64 | convolution fusion | flops 1073741824 | bytes 21037056 | tf_op jit(solution)/shard_map/dot_general | solution.py:32
  190.8 7.6 %all-reduce.2 = (bf16[64,256]{1,0:T(8,128)(2,1)S(1)}, bf16[64,256]{1,0:T(8,128)(2,1)S(1)}) all-reduce(f32[64,256]{1,0:T(8,128)S(1)} %fusion.31, f32[64,256]{1,0:T(8,128)S(1)} %fusion.20), channel_id=1, replica_groups=mesh['table'=64,'row'=2] {'row'}, use_global_device_ids=true, to_apply=%region_2.3 | all-reduce | flops 32768 | bytes 196608 | tf_op jit(solution)/shard_map/psum | solution.py:33
  198.4 15.6 %fusion.18 = (bf16[64,32768]{1,0:T(8,128)(2,1)}, f32[64,32768]{1,0:T(8,128)}) fusion(bf16[64,32768]{1,0:T(8,128)(2,1)} %bitcast.66, f32[32768]{0:T(1024)S(1)} %copy-done.4, bf16[64,256]{1,0:T(8,128)(2,1)S(1)} %get-tuple-element.41, bf16[256,32768]{1,0:T(8,128)(2,1)} %param.13), kind=kOutput, calls=%fused_computation.49 | convolution fusion | flops 1084227584 | bytes 33718272 | tf_op jit(solution)/shard_map/dot_general | solution.py:34
  214.0 14.2 %fusion.16 = bf16[64,32768]{1,0:T(8,128)(2,1)} fusion(bf16[32768,256]{1,0:T(8,128)(2,1)} %param.12, f32[64,32768]{1,0:T(8,128)} %get-tuple-element.52, bf16[64,32768]{1,0:T(8,128)(2,1)} %param.15, bf16[64,256]{1,0:T(8,128)(2,1)S(1)} %get-tuple-element.42), kind=kOutput, calls=%fused_computation.44 | convolution fusion | flops 1084227584 | bytes 33587200 | tf_op jit(solution)/shard_map/dot_general | solution.py:43
  228.2 2.8 copy.35
  231.0 61.0 %all_to_all.72 = bf16[64,64,512]{2,0,1:T(8,128)(2,1)} all-to-all(bf16[64,64,512]{2,0,1:T(8,128)(2,1)S(1)} %bitcast.69), channel_id=1, replica_groups=mesh['table'=64,'row'=2] {'table'}, dimensions={1} | all-to-all | bytes 8388608 | tf_op jit(solution)/shard_map/all_to_all | solution.py:47
  291.9 7.0 %reshape.639 = bf16[4096,4,128]{2,1,0:T(4,128)(2,1)} reshape(bf16[64,64,512]{2,1,0:T(8,128)(2,1)} %bitcast.70) | data formatting | bytes 8388608 | tf_op jit(solution)/shard_map/reshape | solution.py:47
  299.0 10.6 %fusion.24 = bf16[4,512,128]{2,1,0:T(8,128)(2,1)S(1)} fusion(bf16[4,4096,512]{2,1,0:T(8,128)(2,1)} %get-tuple-element.24, bf16[4096,4,128]{2,1,0:T(4,128)(2,1)} %reshape.639), kind=kOutput, calls=%fused_computation.56 | convolution fusion | flops 2147745792 | bytes 21495808 | tf_op jit(solution)/shard_map/kbr,bke->kre/dot_general | solution.py:50
  309.5 0.4 copy.25
  309.9 10.1 %all_to_all.73 = bf16[4,512,128]{2,0,1:T(4,128)(2,1)S(1)} all-to-all(bf16[4,512,128]{2,0,1:T(4,128)(2,1)S(1)} %copy.25), channel_id=1, replica_groups=mesh['table'=64,'row'=2] {'row'}, dimensions={1} | all-to-all | bytes 1048576 | tf_op jit(solution)/shard_map/all_to_all | solution.py:53
  320.0 0.9 copy.26
  (23 shorter events, 0.3 us)
Async XLA Ops:
  0.6 3.7 %copy-start = (s32[4096,8,8]{0,2,1:T(8,128)S(1)}, s32[4096,8,8]{0,2,1:T(8,128)}, u32[]{:S(2)}) copy-start(s32[4096,8,8]{0,2,1:T(8,128)} %param.9) | copy-start | bytes 3145732
  0.6 77.5 %all-to-all-start = ((bf16[8,256,128]{2,1,0:T(8,128)(2,1)}), bf16[8,256,128]{2,1,0:T(8,128)(2,1)S(1)}, u32[]{:S(2)}, u32[]{:S(2)}) async-start(bf16[8,256,128]{2,1,0:T(8,128)(2,1)} %param.11), calls=%async_computation | async-start | bytes 1048576 | tf_op jit(solution)/shard_map/all_to_all | solution.py:23
  105.2 66.7 %copy-start.3 = (bf16[64,32768]{1,0:T(8,128)(2,1)S(1)}, bf16[64,32768]{1,0:T(8,128)(2,1)}, u32[]{:S(2)}) copy-start(bf16[64,32768]{1,0:T(8,128)(2,1)} %param.15) | copy-start | bytes 12582916
  171.9 10.3 %copy-start.2 = (bf16[64,8,8,512]{3,2,0,1:T(8,128)(2,1)}, bf16[64,8,8,512]{3,2,0,1:T(8,128)(2,1)S(1)}, u32[]{:S(2)}) copy-start(bf16[64,8,8,512]{3,2,0,1:T(8,128)(2,1)S(1)} %copy.29) | copy-start | bytes 12582916
  182.2 16.2 %copy-start.4 = (f32[32768]{0:T(1024)S(1)}, f32[32768]{0:T(1024)}, u32[]{:S(2)}) copy-start(f32[32768]{0:T(1024)} %param.14) | copy-start | bytes 393220
  291.9 28.9 %copy-start.1 = (s32[4096,8,8]{0,2,1:T(8,128)S(1)}, s32[4096,8,8]{0,2,1:T(8,128)}, u32[]{:S(2)}) copy-start(s32[4096,8,8]{0,2,1:T(8,128)} %param.9) | copy-start | bytes 3145732
where the time goes:
time: 322 us; the launch traced here: 321 us
  blocking collectives  145 us (45%)
  matrix products  71.5 us (22%)
  other arithmetic  70.9 us (22%)
  local copies, waits for them, and re-layouts  29.1 us (9%)
  starting transfers between devices  3.63 us (1%)
    dynamic_update_slice x4, other arithmetic, body(): lax.map(lambda items: count_rows(items[0], items[1], owned.shape[1]), (ow...  70.8 us
    all_to_all x1, blocking collectives, body(): lax.all_to_all(outgoing, 'table', split_axis=0, concat_axis=1, tiled=True)  66.3 us
    all_to_all x1, blocking collectives, body(): lax.all_to_all(x0_grad, 'table', split_axis=1, concat_axis=0, tiled=True)  61 us
    dot_general x1, matrix products, body(): gate = jnp.dot(low, cross_up, preferred_element_type=jnp.float32) + bias  15.6 us
    dot_general x1, matrix products, body(): lax.dot_general(dlow, cross_down, (((1,), (1,)), ((), ())), preferred_ele...  14.2 us
    dot_general x1, matrix products, body(): jnp.einsum('kbr,kre->kbe', counts, owned, preferred_element_type=jnp.floa...  12.3 us
    dot_general x1, matrix products, body(): jnp.einsum('kbr,bke->kre', counts, back, preferred_element_type=jnp.float32)  10.6 us
    dot_general x1, matrix products, body(): lax.dot_general(dgate, cross_up, (((1,), (1,)), ((), ())), preferred_elem...  10.2 us
  transfers between devices with their start and end apart: 1, of which 0 were waited for; matrix products, arithmetic and copies ran while one was open for 23% of the time, Pallas kernels for 0%

commit v1 on v0

v1 whole, which is shorter than its diff:
```python
import jax
import jax.numpy as jnp
from jax import lax
from jax.experimental import pallas as pl
from jax.experimental.pallas import tpu as pltpu
from jax.sharding import PartitionSpec as P

FIELDS = 8
BITS = 4
LANES = 128


def count_kernel(shard_ref, ids_ref, lengths_ref, packed_ref):
    feat = shard_ref[0] * packed_ref.shape[0]
    tables, rows, batch = packed_ref.shape
    bag = ids_ref.shape[1]
    slot = lax.broadcasted_iota(jnp.int32, (bag, LANES), 0)
    table_row = lax.broadcasted_iota(jnp.int32, (rows, LANES), 0)
    for k in range(tables):
        for start in range(0, batch, LANES):
            cols = pl.ds(start, LANES)
            ids = ids_ref[feat + k, :, cols]
            length = lengths_ref[k : k + 1, cols]
            for other in range(1, lengths_ref.shape[0] // tables):
                at = other * tables + k
                length = jnp.where(shard_ref[0] == other, lengths_ref[at : at + 1, cols], length)
            live = slot < length
            row = jnp.where(live, ids & (rows - 1), -1)
            unit = jnp.left_shift(1, lax.shift_right_logical(ids, rows.bit_length() - 1) * BITS)
            total = jnp.zeros((rows, LANES), jnp.int32)
            for p in range(bag):
                total = total + jnp.where(table_row == row[p : p + 1], unit[p : p + 1], 0)
            packed_ref[k, :, cols] = total


def count(shard, ids, lengths, tables, vocab):
    feats, bag, batch = ids.shape
    rows = vocab // FIELDS
    chunk = 512
    return pl.pallas_call(
        count_kernel,
        grid_spec=pltpu.PrefetchScalarGridSpec(
            num_scalar_prefetch=1,
            grid=(batch // chunk,),
            in_specs=[
                pl.BlockSpec((feats, bag, chunk), lambda b, s: (0, 0, b)),
                pl.BlockSpec((feats, chunk), lambda b, s: (0, b)),
            ],
            out_specs=pl.BlockSpec((tables, rows, chunk), lambda b, s: (0, 0, b)),
        ),
        out_shape=jax.ShapeDtypeStruct((tables, rows, batch), jnp.int32),
        cost_estimate=pl.CostEstimate(
            flops=3 * tables * rows * bag * batch,
            bytes_accessed=4 * batch * (feats * bag + tables * rows),
            transcendentals=0,
        ),
        name="count",
    )(shard, ids, lengths)


def unpack(packed_ref, counts_ref):
    rows, batch = packed_ref.shape[1:]
    for start in range(0, batch, LANES):
        cols = pl.ds(start, LANES)
        packed = packed_ref[0, :, cols]
        for j in range(FIELDS):
            field = lax.shift_right_logical(packed, j * BITS) & ((1 << BITS) - 1)
            counts_ref[j * rows : (j + 1) * rows, cols] = field.astype(jnp.float32).astype(jnp.bfloat16)


def pool_kernel(packed_ref, tables_ref, pooled_ref, counts_ref):
    unpack(packed_ref, counts_ref)
    table = tables_ref[:, 0].reshape(counts_ref.shape[0], tables_ref.shape[3])
    out = lax.dot_general(
        table, counts_ref[...], (((0,), (0,)), ((), ())), preferred_element_type=jnp.float32
    )
    pooled_ref[...] = jnp.transpose(out).astype(jnp.bfloat16)


def pool(packed, tables):
    pair, rows, batch = packed.shape
    shards, _, part, width = tables.shape
    vocab = shards * part
    chunk = 1024
    return pl.pallas_call(
        pool_kernel,
        grid=(pair, batch // chunk),
        in_specs=[
            pl.BlockSpec((1, rows, chunk), lambda k, b: (k, 0, b)),
            pl.BlockSpec((shards, 1, part, width), lambda k, b: (0, k, 0, 0)),
        ],
        out_specs=pl.BlockSpec((chunk, width), lambda k, b: (b, k)),
        out_shape=jax.ShapeDtypeStruct((batch, pair * width), jnp.bfloat16),
        scratch_shapes=[pltpu.VMEM((vocab, chunk), jnp.bfloat16)],
        cost_estimate=pl.CostEstimate(
            flops=2 * pair * batch * vocab * width,
            bytes_accessed=4 * packed.size + 2 * batch * pair * width,
            transcendentals=0,
        ),
        name="pool",
    )(packed, tables)


def scatter_kernel(packed_ref, back_ref, grad_ref, counts_ref, total_ref):
    unpack(packed_ref, counts_ref)
    part = jnp.dot(counts_ref[...], back_ref[...], preferred_element_type=jnp.float32)
    step = pl.program_id(1)

    @pl.when(step == 0)
    def _():
        total_ref[...] = part

    @pl.when(step > 0)
    def _():
        total_ref[...] += part

    @pl.when(step == pl.num_programs(1) - 1)
    def _():
        shards, _, half, width = grad_ref.shape
        grad_ref[:, 0] = total_ref[...].astype(jnp.bfloat16).reshape(shards, half, width)


def scatter(packed, back, shards):
    pair, rows, batch = packed.shape
    vocab = rows * FIELDS
    width = back.shape[1] // pair
    chunk = 1024
    return pl.pallas_call(
        scatter_kernel,
        grid=(pair, batch // chunk),
        in_specs=[
            pl.BlockSpec((1, rows, chunk), lambda k, b: (k, 0, b)),
            pl.BlockSpec((chunk, width), lambda k, b: (b, k)),
        ],
        out_specs=pl.BlockSpec((shards, 1, vocab // shards, width), lambda k, b: (0, k, 0, 0)),
        out_shape=jax.ShapeDtypeStruct((shards, pair, vocab // shards, width), jnp.bfloat16),
        scratch_shapes=[
            pltpu.VMEM((vocab, chunk), jnp.bfloat16),
            pltpu.VMEM((vocab, width), jnp.float32),
        ],
        cost_estimate=pl.CostEstimate(
            flops=2 * pair * batch * vocab * width,
            bytes_accessed=4 * packed.size + 2 * back.size,
            transcendentals=0,
        ),
        name="scatter",
    )(packed, back)


def project_kernel(x0_ref, down_ref, up_ref, grad_ref, sums_ref):
    groups, samples, cols = x0_ref.shape
    low = jnp.zeros((samples, down_ref.shape[1]), jnp.float32)
    dlow = jnp.zeros((samples, down_ref.shape[1]), jnp.float32)
    for g in range(groups):
        span = slice(g * cols, (g + 1) * cols)
        x0 = x0_ref[g]
        low += jnp.dot(x0, down_ref[span, :], preferred_element_type=jnp.float32)
        dgate = (grad_ref[:, span].astype(jnp.float32) * x0.astype(jnp.float32)).astype(jnp.bfloat16)
        dlow += lax.dot_general(
            dgate, up_ref[:, span], (((1,), (1,)), ((), ())), preferred_element_type=jnp.float32
        )

    @pl.when(pl.program_id(0) == 0)
    def _():
        sums_ref[:samples] = low
        sums_ref[samples:] = dlow

    @pl.when(pl.program_id(0) > 0)
    def _():
        sums_ref[:samples] += low
        sums_ref[samples:] += dlow


def project(x0, down, up, grad):
    count_, samples, cols = x0.shape
    rank = down.shape[1]
    groups = 4
    return pl.pallas_call(
        project_kernel,
        grid=(count_ // groups,),
        in_specs=[
            pl.BlockSpec((groups, samples, cols), lambda i: (i, 0, 0)),
            pl.BlockSpec((groups * cols, rank), lambda i: (i, 0)),
            pl.BlockSpec((rank, groups * cols), lambda i: (0, i)),
            pl.BlockSpec((samples, groups * cols), lambda i: (0, i)),
        ],
        out_specs=pl.BlockSpec((2 * samples, rank), lambda i: (0, 0)),
        out_shape=jax.ShapeDtypeStruct((2 * samples, rank), jnp.float32),
        cost_estimate=pl.CostEstimate(
            flops=4 * x0.size * rank, bytes_accessed=4 * x0.size + 4 * down.size, transcendentals=0
        ),
        name="project",
    )(x0, down, up, grad)


def cross_kernel(mine_ref, other_ref, x0_ref, down_ref, up_ref, bias_ref, grad_ref, crossed_ref, back_ref):
    groups, samples, cols = x0_ref.shape
    sums = (mine_ref[...] + other_ref[...]).astype(jnp.bfloat16)
    low, dlow = sums[:samples], sums[samples:]
    for g in range(groups):
        span = slice(g * cols, (g + 1) * cols)
        gate = jnp.dot(low, up_ref[:, span], preferred_element_type=jnp.float32) + bias_ref[:, span]
        spread = lax.dot_general(
            dlow, down_ref[span, :], (((1,), (1,)), ((), ())), preferred_element_type=jnp.float32
        )
        x0 = x0_ref[g].astype(jnp.float32)
        upstream = grad_ref[:, span].astype(jnp.float32)
        crossed_ref[:, span] = (x0 * gate + x0).astype(jnp.bfloat16)
        back_ref[g] = (upstream * gate + upstream + spread).astype(jnp.bfloat16)


def cross(mine, other, x0, down, up, bias, grad):
    count_, samples, cols = x0.shape
    rank = down.shape[1]
    groups = 4
    whole = pl.BlockSpec((2 * samples, rank), lambda i: (0, 0))
    return pl.pallas_call(
        cross_kernel,
        grid=(count_ // groups,),
        in_specs=[
            whole,
            whole,
            pl.BlockSpec((groups, samples, cols), lambda i: (i, 0, 0)),
            pl.BlockSpec((groups * cols, rank), lambda i: (i, 0)),
            pl.BlockSpec((rank, groups * cols), lambda i: (0, i)),
            pl.BlockSpec((1, groups * cols), lambda i: (0, i)),
            pl.BlockSpec((samples, groups * cols), lambda i: (0, i)),
        ],
        out_specs=[
            pl.BlockSpec((samples, groups * cols), lambda i: (0, i)),
            pl.BlockSpec((groups, samples, cols), lambda i: (i, 0, 0)),
        ],
        out_shape=[
            jax.ShapeDtypeStruct((samples, count_ * cols), jnp.bfloat16),
            jax.ShapeDtypeStruct((count_, samples, cols), jnp.bfloat16),
        ],
        cost_estimate=pl.CostEstimate(
            flops=4 * x0.size * rank, bytes_accessed=8 * x0.size + 4 * down.size, transcendentals=0
        ),
        name="cross",
    )(mine, other, x0, down, up, bias, grad)


def body(ids, lengths, tables, cross_down, cross_up, bias, grad_out):
    batch, feats, bag = ids.shape
    part, width = tables.shape[1:]
    shards = lax.axis_size("row")
    owners = lax.axis_size("table")
    pair = feats // shards
    vocab = shards * part
    shard = lax.axis_index("row").astype(jnp.int32).reshape(1)
    owned = lax.all_to_all(
        tables.reshape(shards, pair, part, width), "row", split_axis=0, concat_axis=0, tiled=True
    )
    packed = count(shard, jnp.transpose(ids, (1, 2, 0)), jnp.transpose(lengths), pair, vocab)
    pooled = pool(packed, owned)
    x0 = lax.all_to_all(
        pooled.reshape(owners, batch // owners, pair * width), "table", split_axis=0, concat_axis=0, tiled=True
    )
    mine = project(x0, cross_down, cross_up, grad_out)
    other = lax.ppermute(mine, "row", [(0, 1), (1, 0)])
    crossed, x0_grad = cross(mine, other, x0, cross_down, cross_up, bias.reshape(1, -1), grad_out)
    back = lax.all_to_all(x0_grad, "table", split_axis=0, concat_axis=0, tiled=True)
    halves = scatter(packed, back.reshape(batch, pair * width), shards)
    table_grad = lax.all_to_all(halves, "row", split_axis=0, concat_axis=0, tiled=True)
    return (crossed, table_grad.reshape(feats, part, width))


def solution(mesh):
    in_specs = (
        P(None, "table", None),
        P(None, "table"),
        P("table", "row", None),
        P("row", None),
        P(None, "row"),
        P("row"),
        P("table", "row"),
    )
    out_specs = (P("table", "row"), P("table", "row", None))
    return jax.shard_map(body, mesh=mesh, in_specs=in_specs, out_specs=out_specs, check_vma=False)
```

time: 322 us -> 233 us (0.72)
  Pallas kernels: 0 us -> 82.1 us
  matrix products: 71.5 us -> 0 us
  other arithmetic: 70.9 us -> 0 us
  local copies, waits for them, and re-layouts: 29.1 us -> 2.23 us
  blocking collectives: 145 us -> 138 us
  waiting for transfers between devices: 0.01 us -> 4.6 us
    pallas_call x0 -> x5, Pallas kernels: none -> 82.1 us  [the longest x1 23.2 us: cross(): pl.pallas_call(cross_kernel, grid=(count_ // groups,), in_specs=[whole, w...]
    dot_general x6 -> x0, matrix products: 71.5 us -> none  [the longest x1 15.6 us: body(): gate = jnp.dot(low, cross_up, preferred_element_type=jnp.float32) + bias]
    dynamic_update_slice x4 -> x0, other arithmetic: 70.8 us -> none  [body(): lax.map(lambda items: count_rows(items[0], items[1], owned.shape[1]), (ow...]
    all_to_all x5 -> x0, local copies, waits for them, and re-layouts: 11.2 us -> none  [the longest x2 7.56 us: body(): lax.all_to_all(outgoing, 'table', split_axis=0, concat_axis=1, tiled=True)]
    convert_element_type x2 -> x0, local copies, waits for them, and re-layouts: 7.97 us -> none  [the longest x1 7.57 us: body(): pooled.astype(jnp.bfloat16)]
    psum x1 -> x0, blocking collectives: 7.58 us -> none  [body(): low = lax.psum(low_part, 'row').astype(jnp.bfloat16)]
    reshape x1 -> x0, local copies, waits for them, and re-layouts: 7.02 us -> none  [body(): lax.all_to_all(x0_grad, 'table', split_axis=1, concat_axis=0, tiled=True)]
    ppermute x0 -> x1, waiting for transfers between devices: none -> 4.42 us  [body(): other = lax.ppermute(mine, 'row', [(0, 1), (1, 0)])]
  transfers between devices with their start and end apart: 1 -> 2, of which waited for: 0 -> 2; matrix products, arithmetic and copies ran while one was open for 23% -> 0% of each run, Pallas kernels for 0% -> 3%
where the time goes in v1:
time: 233 us; the launch traced here: 231 us
  blocking collectives  138 us (59%)
  Pallas kernels  82.1 us (35%)
  waiting for transfers between devices  4.6 us (2%)
  starting transfers between devices  3.94 us (2%)
    all_to_all x1, blocking collectives, body(): lax.all_to_all(pooled.reshape(owners, batch // owners, pair * width), 'ta...  66.6 us
    all_to_all x1, blocking collectives, body(): lax.all_to_all(x0_grad, 'table', split_axis=0, concat_axis=0, tiled=True)  59.9 us
    pallas_call x1, Pallas kernels, cross(): pl.pallas_call(cross_kernel, grid=(count_ // groups,), in_specs=[whole, w...  23.2 us
    pallas_call x1, Pallas kernels, project(): pl.pallas_call(project_kernel, grid=(count_ // groups,), in_specs=[pl.Blo...  21 us
    pallas_call x1, Pallas kernels, pool(): pl.pallas_call(pool_kernel, grid=(pair, batch // chunk), in_specs=[pl.Blo...  15.6 us
    pallas_call x1, Pallas kernels, scatter(): pl.pallas_call(scatter_kernel, grid=(pair, batch // chunk), in_specs=[pl....  14.8 us
    all_to_all x1, blocking collectives, body(): lax.all_to_all(halves, 'row', split_axis=0, concat_axis=0, tiled=True)  11.1 us
    pallas_call x1, Pallas kernels, count(): pl.pallas_call(count_kernel, grid_spec=pltpu.PrefetchScalarGridSpec(num_s...  7.56 us
  transfers between devices with their start and end apart: 2, of which 2 were waited for; matrix products, arithmetic and copies ran while one was open for 0% of the time, Pallas kernels for 3%

profile of v1, /device:TPU:1, one launch (start us, length us, event | category | flops | bytes accessed | tf_op | source)
XLA Modules:
  0.0 231.2 jit_solution(7957109454587416957)
XLA Ops:
  0.6 3.5 %all-to-all-start = ((bf16[2,4,256,128]{3,2,1,0:T(8,128)(2,1)}), bf16[2,4,256,128]{3,2,1,0:T(8,128)(2,1)S(1)}, u32[]{:S(2)}, u32[]{:S(2)}) async-start(bf16[2,4,256,128]{3,2,1,0:T(8,128)(2,1)} %bitcast.12), calls=%async_computation | async-start | bytes 1048576 | tf_op jit(solution)/shard_map/all_to_all | solution.py:252
  4.1 7.6 %count.1.packed_ref = s32[4,64,4096]{2,1,0:T(8,128)} custom-call(s32[1]{0:T(128)} %bitcast.shard_ref, s32[8,8,4096]{2,1,0:T(8,128)} %bitcast.11, s32[8,4096]{1,0:T(8,128)} %bitcast.14), custom_call_target="tpu_custom_call" | custom-call | flops 25165824 | bytes 5242880 | tf_op jit(solution)/shard_map/count/pallas_call | solution.py:40
  11.7 0.2 all-to-all-done.tables_ref
  11.9 0.0 copy-start
  11.9 0.8 copy-done
  12.7 15.6 %pool.1 = bf16[4096,512]{1,0:T(8,128)(2,1)} custom-call(s32[4,64,4096]{2,1,0:T(8,128)} %count.1.packed_ref, bf16[2,4,256,128]{3,2,1,0:T(8,128)(2,1)} %copy-done), custom_call_target="tpu_custom_call" | custom-call | flops 2147483648 | bytes 8388608 | tf_op jit(solution)/shard_map/pool/pallas_call | solution.py:85
  28.3 66.6 %all_to_all.20.x0_ref = bf16[64,64,512]{2,1,0:T(8,128)(2,1)} all-to-all(bf16[64,64,512]{2,1,0:T(8,128)(2,1)} %bitcast.9), channel_id=1, replica_groups=mesh['table'=64,'row'=2] {'table'}, dimensions={0} | all-to-all | bytes 8388608 | tf_op jit(solution)/shard_map/all_to_all | solution.py:257
  94.8 21.0 %project.1.mine_ref = f32[128,256]{1,0:T(8,128)} custom-call(bf16[64,64,512]{2,1,0:T(8,128)(2,1)} %all_to_all.20.x0_ref, bf16[32768,256]{1,0:T(8,128)(2,1)} %down_ref.3, bf16[256,32768]{1,0:T(8,128)(2,1)} %up_ref.3, bf16[64,32768]{1,0:T(8,128)(2,1)} %grad_ref.3), custom_call_target="tpu_custom_call" | custom-call | flops 2147483648 | bytes 41943040 | tf_op jit(solution)/shard_map/project/pallas_call | solution.py:178
  115.8 0.4 collective-permute-start
  116.3 4.4 %collective-permute-done.other_ref = f32[128,256]{1,0:T(8,128)S(1)} collective-permute-done((f32[128,256]{1,0:T(8,128)}, f32[128,256]{1,0:T(8,128)S(1)}, u32[]{:S(2)}, u32[]{:S(2)}) %collective-permute-start) | collective-permute-done | bytes 131104 | tf_op jit(solution)/shard_map/ppermute | solution.py:261
  120.7 0.0 copy-start.1
  120.7 0.6 copy-done.1
  121.3 23.2 %cross.1 = (bf16[64,32768]{1,0:T(8,128)(2,1)}, bf16[64,64,512]{2,1,0:T(8,128)(2,1)}) custom-call(f32[128,256]{1,0:T(8,128)} %project.1.mine_ref, f32[128,256]{1,0:T(8,128)} %copy-done.1, bf16[64,64,512]{2,1,0:T(8,128)(2,1)} %all_to_all.20.x0_ref, bf16[32768,256]{1,0:T(8,128)(2,1)} %down_ref.3, bf16[256,32768]{1,0:T(8,128)(2,1)} %up_ref.3, ...), custom_call_target="tpu_custom_call" | custom-call | flops 2147483648 | bytes 50331648 | tf_op jit(solution)/shard_map/cross/pallas_call | solution.py:217
  144.5 59.9 %all_to_all.21 = bf16[64,64,512]{2,1,0:T(8,128)(2,1)} all-to-all(bf16[64,64,512]{2,1,0:T(8,128)(2,1)} %get-tuple-element.5), channel_id=1, replica_groups=mesh['table'=64,'row'=2] {'table'}, dimensions={0} | all-to-all | bytes 8388608 | tf_op jit(solution)/shard_map/all_to_all | solution.py:263
  204.4 14.8 %scatter.1 = bf16[2,4,256,128]{3,2,1,0:T(8,128)(2,1)} custom-call(s32[4,64,4096]{2,1,0:T(8,128)} %count.1.packed_ref, bf16[4096,512]{1,0:T(8,128)(2,1)} %bitcast.8), custom_call_target="tpu_custom_call" | custom-call | flops 2147483648 | bytes 8388608 | tf_op jit(solution)/shard_map/scatter/pallas_call | solution.py:128
  219.2 11.1 %all_to_all.22 = bf16[2,4,256,128]{3,2,1,0:T(8,128)(2,1)S(1)} all-to-all(bf16[2,4,256,128]{3,2,1,0:T(8,128)(2,1)} %scatter.1), channel_id=1, replica_groups=mesh['table'=64,'row'=2] {'row'}, dimensions={0} | all-to-all | bytes 1048576 | tf_op jit(solution)/shard_map/all_to_all | solution.py:265
  230.4 0.8 copy.10
Async XLA Ops:
  0.6 11.3 %all-to-all-start = ((bf16[2,4,256,128]{3,2,1,0:T(8,128)(2,1)}), bf16[2,4,256,128]{3,2,1,0:T(8,128)(2,1)S(1)}, u32[]{:S(2)}, u32[]{:S(2)}) async-start(bf16[2,4,256,128]{3,2,1,0:T(8,128)(2,1)} %bitcast.12), calls=%async_computation | async-start | bytes 1048576 | tf_op jit(solution)/shard_map/all_to_all | solution.py:252
  11.9 0.8 copy-start
  115.8 4.9 %collective-permute-start = (f32[128,256]{1,0:T(8,128)}, f32[128,256]{1,0:T(8,128)S(1)}, u32[]{:S(2)}, u32[]{:S(2)}) collective-permute-start(f32[128,256]{1,0:T(8,128)} %project.1.mine_ref), channel_id=1, source_target_pairs={{0,1},{1,0},{2,3},{3,2},{4,5},{5,4},{6,7},{7,6},{8,9},{9,8},{10,11... | collective-permute-start | bytes 393224 | tf_op jit(solution)/shard_map/ppermute | solution.py:261
  120.7 0.6 copy-start.1

commit v2 on v1

v2 whole, which is shorter than its diff:
```python
import jax
import jax.numpy as jnp
from jax import lax
from jax.experimental import pallas as pl
from jax.experimental.pallas import tpu as pltpu
from jax.sharding import PartitionSpec as P

FIELDS = 8
BITS = 4
LANES = 128
MIB = 1 << 20


def count_kernel(shard_ref, ids_ref, lengths_ref, counts_ref):
    tables, vocab, batch = counts_ref.shape
    bag = ids_ref.shape[1]
    rows = vocab // FIELDS
    feat = shard_ref[0] * tables
    slot = lax.broadcasted_iota(jnp.int32, (bag, LANES), 0)
    table_row = lax.broadcasted_iota(jnp.int32, (rows, LANES), 0)
    for k in range(tables):
        for start in range(0, batch, LANES):
            cols = pl.ds(start, LANES)
            ids = ids_ref[feat + k, :, cols]
            length = lengths_ref[k : k + 1, cols]
            for other in range(1, lengths_ref.shape[0] // tables):
                at = other * tables + k
                length = jnp.where(shard_ref[0] == other, lengths_ref[at : at + 1, cols], length)
            row = jnp.where(slot < length, ids & (rows - 1), -1)
            unit = jnp.left_shift(1, lax.shift_right_logical(ids, rows.bit_length() - 1) * BITS)
            total = jnp.zeros((rows, LANES), jnp.int32)
            for p in range(bag):
                total = total + jnp.where(table_row == row[p : p + 1], unit[p : p + 1], 0)
            for j in range(FIELDS):
                field = lax.shift_right_logical(total, j * BITS) & ((1 << BITS) - 1)
                counts_ref[k, j * rows : (j + 1) * rows, cols] = field.astype(jnp.float32).astype(jnp.bfloat16)


def count(shard, ids, lengths, tables, vocab):
    feats, bag, batch = ids.shape
    chunk = 512
    return pl.pallas_call(
        count_kernel,
        grid_spec=pltpu.PrefetchScalarGridSpec(
            num_scalar_prefetch=1,
            grid=(batch // chunk,),
            in_specs=[
                pl.BlockSpec((feats, bag, chunk), lambda b, s: (0, 0, b)),
                pl.BlockSpec((feats, chunk), lambda b, s: (0, b)),
            ],
            out_specs=pl.BlockSpec((tables, vocab, chunk), lambda b, s: (0, 0, b)),
        ),
        out_shape=jax.ShapeDtypeStruct((tables, vocab, batch), jnp.bfloat16),
        compiler_params=pltpu.CompilerParams(vmem_limit_bytes=12 * MIB),
        cost_estimate=pl.CostEstimate(
            flops=tables * vocab * bag * batch,
            bytes_accessed=4 * ids.size + 2 * tables * vocab * batch,
            transcendentals=0,
        ),
        name="count",
    )(shard, ids, lengths)


def pool_kernel(counts_ref, tables_ref, pooled_ref):
    shards, _, part, width = tables_ref.shape
    table = tables_ref[:, 0].reshape(shards * part, width)
    out = lax.dot_general(
        table, counts_ref[0], (((0,), (0,)), ((), ())), preferred_element_type=jnp.float32
    )
    pooled_ref[...] = jnp.transpose(out.astype(jnp.bfloat16))


def pool(counts, tables):
    pair, vocab, batch = counts.shape
    shards, _, part, width = tables.shape
    chunk = 2048
    return pl.pallas_call(
        pool_kernel,
        grid=(pair, batch // chunk),
        in_specs=[
            pl.BlockSpec((1, vocab, chunk), lambda k, b: (k, 0, b)),
            pl.BlockSpec((shards, 1, part, width), lambda k, b: (0, k, 0, 0)),
        ],
        out_specs=pl.BlockSpec((chunk, width), lambda k, b: (b, k)),
        out_shape=jax.ShapeDtypeStruct((batch, pair * width), jnp.bfloat16),
        compiler_params=pltpu.CompilerParams(vmem_limit_bytes=14 * MIB),
        cost_estimate=pl.CostEstimate(
            flops=2 * counts.size * width,
            bytes_accessed=2 * counts.size + 2 * batch * pair * width,
            transcendentals=0,
        ),
        name="pool",
    )(counts, tables)


def scatter_kernel(shard_ref, counts_ref, back_ref, grad_ref):
    grad_ref[0] = jnp.dot(counts_ref[0], back_ref[...], preferred_element_type=jnp.float32).astype(jnp.bfloat16)


def scatter(half, place, counts, back, shards, slots):
    pair, vocab, batch = counts.shape
    part = vocab // shards
    width = back.shape[1] // pair
    return pl.pallas_call(
        scatter_kernel,
        grid_spec=pltpu.PrefetchScalarGridSpec(
            num_scalar_prefetch=1,
            grid=(pair,),
            in_specs=[
                pl.BlockSpec((1, part, batch), lambda k, s: (k, s[0], 0)),
                pl.BlockSpec((batch, width), lambda k, s: (0, k)),
            ],
            out_specs=pl.BlockSpec((1, part, width), lambda k, s: (s[1] * pair + k, 0, 0)),
        ),
        out_shape=jax.ShapeDtypeStruct((slots, part, width), jnp.bfloat16),
        compiler_params=pltpu.CompilerParams(vmem_limit_bytes=14 * MIB),
        cost_estimate=pl.CostEstimate(
            flops=2 * counts.size // shards * width,
            bytes_accessed=2 * counts.size // shards + 2 * back.size,
            transcendentals=0,
        ),
        name="scatter",
    )(jnp.stack([half, place]), counts, back)


def project_kernel(x0_ref, down_ref, up_ref, grad_ref, sums_ref):
    groups, samples, cols = x0_ref.shape
    step = pl.program_id(0)
    span = pl.ds(pl.multiple_of(step * groups * cols, groups * cols), groups * cols)
    x0 = jnp.concatenate([x0_ref[g] for g in range(groups)], axis=1)
    low = jnp.dot(x0, down_ref[span, :], preferred_element_type=jnp.float32)
    dgate = (grad_ref[...].astype(jnp.float32) * x0.astype(jnp.float32)).astype(jnp.bfloat16)
    dlow = lax.dot_general(
        dgate, up_ref[:, span], (((1,), (1,)), ((), ())), preferred_element_type=jnp.float32
    )

    @pl.when(step == 0)
    def _():
        sums_ref[:samples] = low
        sums_ref[samples:] = dlow

    @pl.when(step > 0)
    def _():
        sums_ref[:samples] += low
        sums_ref[samples:] += dlow


def project(x0, down, up, grad):
    owners, samples, cols = x0.shape
    rank = down.shape[1]
    groups = 8
    held = pl.BlockSpec(memory_space=pltpu.VMEM)
    return pl.pallas_call(
        project_kernel,
        grid=(owners // groups,),
        in_specs=[
            pl.BlockSpec((groups, samples, cols), lambda i: (i, 0, 0)),
            held,
            held,
            pl.BlockSpec((samples, groups * cols), lambda i: (0, i)),
        ],
        out_specs=pl.BlockSpec((2 * samples, rank), lambda i: (0, 0)),
        out_shape=jax.ShapeDtypeStruct((2 * samples, rank), jnp.float32),
        compiler_params=pltpu.CompilerParams(vmem_limit_bytes=14 * MIB),
        cost_estimate=pl.CostEstimate(
            flops=4 * x0.size * rank, bytes_accessed=4 * x0.size, transcendentals=0
        ),
        name="project",
    )(x0, down, up, grad)


def cross_kernel(mine_ref, other_ref, x0_ref, down_ref, up_ref, bias_ref, grad_ref, crossed_ref, back_ref):
    groups, samples, cols = x0_ref.shape
    step = pl.program_id(0)
    span = pl.ds(pl.multiple_of(step * groups * cols, groups * cols), groups * cols)
    sums = (mine_ref[...] + other_ref[...]).astype(jnp.bfloat16)
    gate = jnp.dot(sums[:samples], up_ref[:, span], preferred_element_type=jnp.float32) + bias_ref[...]
    spread = lax.dot_general(
        sums[samples:], down_ref[span, :], (((1,), (1,)), ((), ())), preferred_element_type=jnp.float32
    )
    x0 = jnp.concatenate([x0_ref[g] for g in range(groups)], axis=1).astype(jnp.float32)
    upstream = grad_ref[...].astype(jnp.float32)
    crossed_ref[...] = (x0 * gate + x0).astype(jnp.bfloat16)
    back = (upstream * gate + upstream + spread).astype(jnp.bfloat16)
    for g in range(groups):
        back_ref[g] = back[:, g * cols : (g + 1) * cols]


def cross(mine, other, x0, down, up, bias, grad):
    owners, samples, cols = x0.shape
    rank = down.shape[1]
    groups = 8
    whole = pl.BlockSpec((2 * samples, rank), lambda i: (0, 0))
    held = pl.BlockSpec(memory_space=pltpu.VMEM)
    return pl.pallas_call(
        cross_kernel,
        grid=(owners // groups,),
        in_specs=[
            whole,
            whole,
            pl.BlockSpec((groups, samples, cols), lambda i: (i, 0, 0)),
            held,
            held,
            pl.BlockSpec((1, groups * cols), lambda i: (0, i)),
            pl.BlockSpec((samples, groups * cols), lambda i: (0, i)),
        ],
        out_specs=[
            pl.BlockSpec((samples, groups * cols), lambda i: (0, i)),
            pl.BlockSpec((groups, samples, cols), lambda i: (i, 0, 0)),
        ],
        out_shape=[
            jax.ShapeDtypeStruct((samples, owners * cols), jnp.bfloat16),
            jax.ShapeDtypeStruct((owners, samples, cols), jnp.bfloat16),
        ],
        compiler_params=pltpu.CompilerParams(vmem_limit_bytes=20 * MIB),
        cost_estimate=pl.CostEstimate(
            flops=4 * x0.size * rank, bytes_accessed=8 * x0.size, transcendentals=0
        ),
        name="cross",
    )(mine, other, x0, down, up, bias, grad)


def body(ids, lengths, tables, cross_down, cross_up, bias, grad_out):
    batch, feats, bag = ids.shape
    part, width = tables.shape[1:]
    shards = lax.axis_size("row")
    owners = lax.axis_size("table")
    pair = feats // shards
    vocab = shards * part
    shard = lax.axis_index("row").astype(jnp.int32)
    swap = [(0, 1), (1, 0)]
    owned = lax.all_to_all(
        tables.reshape(shards, pair, part, width), "row", split_axis=0, concat_axis=0, tiled=True
    )
    counts = count(shard.reshape(1), jnp.transpose(ids, (1, 2, 0)), jnp.transpose(lengths), pair, vocab)
    pooled = pool(counts, owned)
    x0 = lax.all_to_all(
        pooled.reshape(owners, batch // owners, pair * width), "table", split_axis=0, concat_axis=0, tiled=True
    )
    down = pltpu.with_memory_space_constraint(cross_down, pltpu.VMEM)
    up = pltpu.with_memory_space_constraint(cross_up, pltpu.VMEM)
    mine = project(x0, down, up, grad_out)
    other = lax.ppermute(mine, "row", swap)
    crossed, x0_grad = cross(mine, other, x0, down, up, bias.reshape(1, -1), grad_out)
    back = lax.all_to_all(x0_grad, "table", split_axis=0, concat_axis=0, tiled=True)
    back = back.reshape(batch, pair * width)
    outgoing = scatter(1 - shard, jnp.zeros_like(shard), counts, back, shards, pair)
    incoming = lax.ppermute(outgoing, "row", swap)
    own = scatter(shard, shard, counts, back, shards, feats)
    table_grad = lax.dynamic_update_slice_in_dim(own, incoming, (1 - shard) * pair, 0)
    return (crossed, table_grad)


def solution(mesh):
    in_specs = (
        P(None, "table", None),
        P(None, "table"),
        P("table", "row", None),
        P("row", None),
        P(None, "row"),
        P("row"),
        P("table", "row"),
    )
    out_specs = (P("table", "row"), P("table", "row", None))
    return jax.shard_map(body, mesh=mesh, in_specs=in_specs, out_specs=out_specs, check_vma=False)
```

time: 233 us -> 237 us (1.017)
  blocking collectives: 138 us -> 65.8 us
  waiting for transfers between devices: 4.6 us -> 56.7 us
  local copies, waits for them, and re-layouts: 2.23 us -> 49 us
  Pallas kernels: 82.1 us -> 49.5 us
  starting transfers between devices: 3.94 us -> 14.3 us
    all_to_all x2 -> x0, blocking collectives: 71 us -> none  [the longest x1 59.9 us: body(): lax.all_to_all(x0_grad, 'table', split_axis=0, concat_axis=0, tiled=True)]
    all_to_all x0 -> x1, waiting for transfers between devices: none -> 53.2 us  [body(): lax.all_to_all(x0_grad, 'table', split_axis=0, concat_axis=0, tiled=True)]
    unnamed x5 -> x24, local copies, waits for them, and re-layouts: 2.23 us -> 48.3 us
    pallas_call x3 -> x4, Pallas kernels: 59 us -> 33.8 us  [the longest x1 12.2 us: cross(): pl.pallas_call(cross_kernel, grid=(owners // groups,), in_specs=[whole, w...]
    pallas_call x1, Pallas kernels: 15.6 us -> 6.28 us  [pool(): pl.pallas_call(pool_kernel, grid=(pair, batch // chunk), in_specs=[pl.Blo...]
    all_to_all x0 -> x1, starting transfers between devices: none -> 6.65 us  [body(): lax.all_to_all(x0_grad, 'table', split_axis=0, concat_axis=0, tiled=True)]
    ppermute x1 -> x2, starting transfers between devices: 0.44 us -> 4.17 us  [the longest x1 2.95 us: body(): incoming = lax.ppermute(outgoing, 'row', swap)]
  transfers between devices with their start and end apart: 2 -> 4, of which waited for: 2 -> 2; matrix products, arithmetic and copies ran while one was open for 0% -> 0% of each run, Pallas kernels for 3% -> 7%
where the time goes in v2:
time: 237 us; the launch traced here: 236 us
  blocking collectives  65.8 us (28%)
  waiting for transfers between devices  56.7 us (24%)
  Pallas kernels  49.5 us (21%)
  local copies, waits for them, and re-layouts  49 us (21%)
  starting transfers between devices  14.3 us (6%)
    all_to_all x1, blocking collectives, body(): lax.all_to_all(pooled.reshape(owners, batch // owners, pair * width), 'ta...  65.8 us
    all_to_all x1, waiting for transfers between devices, body(): lax.all_to_all(x0_grad, 'table', split_axis=0, concat_axis=0, tiled=True)  53.2 us
    unnamed x24, local copies, waits for them, and re-layouts  48.3 us
    pallas_call x1, Pallas kernels, cross(): pl.pallas_call(cross_kernel, grid=(owners // groups,), in_specs=[whole, w...  12.2 us
    pallas_call x2, Pallas kernels, scatter(): pl.pallas_call(scatter_kernel, grid_spec=pltpu.PrefetchScalarGridSpec(num...  11.1 us
    pallas_call x1, Pallas kernels, project(): pl.pallas_call(project_kernel, grid=(owners // groups,), in_specs=[pl.Blo...  10.5 us
    pallas_call x1, Pallas kernels, count(): pl.pallas_call(count_kernel, grid_spec=pltpu.PrefetchScalarGridSpec(num_s...  9.48 us
    all_to_all x1, starting transfers between devices, body(): lax.all_to_all(x0_grad, 'table', split_axis=0, concat_axis=0, tiled=True)  6.65 us
  transfers between devices with their start and end apart: 4, of which 2 were waited for; matrix products, arithmetic and copies ran while one was open for 0% of the time, Pallas kernels for 7%

profile of v2, /device:TPU:1, one launch (start us, length us, event | category | flops | bytes accessed | tf_op | source)
XLA Modules:
  0.0 236.1 jit_solution(9145477704243675460)
XLA Ops:
  0.6 3.5 %all-to-all-start = ((bf16[2,4,256,128]{3,2,1,0:T(8,128)(2,1)}), bf16[2,4,256,128]{3,2,1,0:T(8,128)(2,1)S(1)}, u32[]{:S(2)}, u32[]{:S(2)}) async-start(bf16[2,4,256,128]{3,2,1,0:T(8,128)(2,1)} %bitcast.12), calls=%async_computation | async-start | bytes 1048576 | tf_op jit(solution)/shard_map/all_to_all | solution.py:232
  4.1 0.0 copy-start.9
  4.2 1.2 copy-done.9
  5.4 0.9 copy-done.11
  6.3 9.5 %count.1.counts_ref = bf16[4,512,4096]{2,1,0:T(8,128)(2,1)S(1)} custom-call(s32[1]{0:T(128)} %bitcast.shard_ref, s32[8,8,4096]{2,1,0:T(8,128)S(1)} %bitcast.9, s32[8,4096]{1,0:T(8,128)S(1)} %bitcast.11), custom_call_target="tpu_custom_call" | custom-call | flops 67108864 | bytes 17825792 | tf_op jit(solution)/shard_map/count/pallas_call | solution.py:42
  15.8 0.0 copy-start
  15.8 5.7 %copy-done = bf16[4,512,4096]{2,1,0:T(8,128)(2,1)} copy-done((bf16[4,512,4096]{2,1,0:T(8,128)(2,1)}, bf16[4,512,4096]{2,1,0:T(8,128)(2,1)S(1)}, u32[]{:S(2)}) %copy-start) | copy-done | bytes 16777240
  21.5 0.0 all-to-all-done.tables_ref
  21.5 5.8 %copy-done.1 = bf16[4,512,4096]{2,1,0:T(8,128)(2,1)S(1)} copy-done((bf16[4,512,4096]{2,1,0:T(8,128)(2,1)S(1)}, bf16[4,512,4096]{2,1,0:T(8,128)(2,1)}, u32[]{:S(2)}) %copy-start.1) | copy-done | bytes 16777240
  27.3 6.3 %pool.1 = bf16[4096,512]{1,0:T(8,128)(2,1)S(1)} custom-call(bf16[4,512,4096]{2,1,0:T(8,128)(2,1)S(1)} %copy-done.1, bf16[2,4,256,128]{3,2,1,0:T(8,128)(2,1)S(1)} %all-to-all-done.tables_ref), custom_call_target="tpu_custom_call" | custom-call | flops 2147483648 | bytes 20971520 | tf_op jit(solution)/shard_map/pool/pallas_call | solution.py:77
  33.6 65.8 %all_to_all.15.x0_ref = bf16[64,64,512]{2,1,0:T(8,128)(2,1)S(1)} all-to-all(bf16[64,64,512]{2,1,0:T(8,128)(2,1)S(1)} %bitcast.8), channel_id=1, replica_groups=mesh['table'=64,'row'=2] {'table'}, dimensions={0} | all-to-all | bytes 8388608 | tf_op jit(solution)/shard_map/all_to_all | solution.py:237
  99.3 5.8 %copy-done.4 = bf16[32768,256]{1,0:T(8,128)(2,1)S(1)} copy-done((bf16[32768,256]{1,0:T(8,128)(2,1)S(1)}, bf16[32768,256]{1,0:T(8,128)(2,1)}, u32[]{:S(2)}) %copy-start.4) | copy-done | bytes 16777240
  105.1 5.8 %copy-done.6 = bf16[256,32768]{1,0:T(8,128)(2,1)S(1)} copy-done((bf16[256,32768]{1,0:T(8,128)(2,1)S(1)}, bf16[256,32768]{1,0:T(8,128)(2,1)}, u32[]{:S(2)}) %copy-start.6) | copy-done | bytes 16777240
  110.9 10.5 %project.1.mine_ref = f32[128,256]{1,0:T(8,128)S(1)} custom-call(bf16[64,64,512]{2,1,0:T(8,128)(2,1)S(1)} %all_to_all.15.x0_ref, bf16[32768,256]{1,0:T(8,128)(2,1)S(1)} %copy-done.4, bf16[256,32768]{1,0:T(8,128)(2,1)S(1)} %copy-done.6, bf16[64,32768]{1,0:T(8,128)(2,1)} %grad_ref.3), custom_call_target="tpu_custom_call" | custom-call | flops 2147483648 | bytes 8388608 | tf_op jit(solution)/shard_map/project/pallas_call | solution.py:153
  121.4 0.0 copy-done.8
  121.4 1.2 collective-permute-start
  122.6 3.5 %collective-permute-done.other_ref = f32[128,256]{1,0:T(8,128)S(1)} collective-permute-done((f32[128,256]{1,0:T(8,128)S(1)}, f32[128,256]{1,0:T(8,128)S(1)}, u32[]{:S(2)}, u32[]{:S(2)}) %collective-permute-start) | collective-permute-done | bytes 131104 | tf_op jit(solution)/shard_map/ppermute | solution.py:243
  126.1 0.0 copy-done.10
  126.2 5.8 %copy-done.5 = bf16[32768,256]{1,0:T(8,128)(2,1)S(1)} copy-done((bf16[32768,256]{1,0:T(8,128)(2,1)S(1)}, bf16[32768,256]{1,0:T(8,128)(2,1)}, u32[]{:S(2)}) %copy-start.5) | copy-done | bytes 16777240
  131.9 5.8 %copy-done.7 = bf16[256,32768]{1,0:T(8,128)(2,1)S(1)} copy-done((bf16[256,32768]{1,0:T(8,128)(2,1)S(1)}, bf16[256,32768]{1,0:T(8,128)(2,1)}, u32[]{:S(2)}) %copy-start.7) | copy-done | bytes 16777240
  137.7 12.2 %cross.1 = (bf16[64,32768]{1,0:T(8,128)(2,1)}, bf16[64,64,512]{2,1,0:T(8,128)(2,1)}) custom-call(f32[128,256]{1,0:T(8,128)S(1)} %project.1.mine_ref, f32[128,256]{1,0:T(8,128)S(1)} %collective-permute-done.other_ref, bf16[64,64,512]{2,1,0:T(8,128)(2,1)} %copy-done.8, bf16[32768,256]{1,0:T(8,128)(2,1)S(1)} %copy-done.5, bf16[256,32768]{1,0:T(8,128)(2,1)S(1)} %copy-done.7, ...), custom_call_target="tpu_custom_call" | custom-call | flops 2147483648 | bytes 16777216 | tf_op jit(solution)/shard_map/cross/pallas_call | solution.py:195
  149.9 6.6 %all-to-all-start.2 = ((bf16[64,64,512]{2,1,0:T(8,128)(2,1)}), bf16[64,64,512]{2,1,0:T(8,128)(2,1)}, u32[]{:S(2)}, u32[]{:S(2)}) async-start(bf16[64,64,512]{2,1,0:T(8,128)(2,1)} %get-tuple-element.5), calls=%async_computation.2 | async-start | bytes 8388608 | tf_op jit(solution)/shard_map/all_to_all | solution.py:245
  156.5 0.1 pad_add_fusion.1.shard_ref
  156.6 53.2 %all-to-all-done.2 = bf16[64,64,512]{2,1,0:T(8,128)(2,1)} async-done(((bf16[64,64,512]{2,1,0:T(8,128)(2,1)}), bf16[64,64,512]{2,1,0:T(8,128)(2,1)}, u32[]{:S(2)}, u32[]{:S(2)}) %all-to-all-start.2) | async-done | bytes 4194336 | tf_op jit(solution)/shard_map/all_to_all | solution.py:245
  209.8 5.8 %copy-done.2 = bf16[4,512,4096]{2,1,0:T(8,128)(2,1)S(1)} copy-done((bf16[4,512,4096]{2,1,0:T(8,128)(2,1)S(1)}, bf16[4,512,4096]{2,1,0:T(8,128)(2,1)}, u32[]{:S(2)}) %copy-start.2) | copy-done | bytes 16777240
  215.5 5.2 %scatter.3 = bf16[4,256,128]{2,1,0:T(8,128)(2,1)S(1)} custom-call(s32[2]{0:T(128)S(1)} %pad_add_fusion.1.shard_ref, bf16[4,512,4096]{2,1,0:T(8,128)(2,1)S(1)} %copy-done.2, bf16[4096,512]{1,0:T(8,128)(2,1)} %bitcast.6.back_ref), custom_call_target="tpu_custom_call" | custom-call | flops 1073741824 | bytes 12582912 | tf_op jit(solution)/shard_map/scatter/pallas_call | solution.py:104
  220.7 3.0 %collective-permute-start.1 = (bf16[4,256,128]{2,1,0:T(8,128)(2,1)S(1)}, bf16[4,256,128]{2,1,0:T(8,128)(2,1)S(1)}, u32[]{:S(2)}, u32[]{:S(2)}) collective-permute-start(bf16[4,256,128]{2,1,0:T(8,128)(2,1)S(1)} %scatter.3), channel_id=1, source_target_pairs={{0,1},{1,0},{2,3},{3,2},{4,5},{5,4},{6,7},{7,6},{8,9},{9,8},{10,11... | collective-permute-start | bytes 786440 | tf_op jit(solution)/shard_map/ppermute | solution.py:248
  223.7 0.1 pad_add_fusion.shard_ref
  223.8 5.8 %copy-done.3 = bf16[4,512,4096]{2,1,0:T(8,128)(2,1)S(1)} copy-done((bf16[4,512,4096]{2,1,0:T(8,128)(2,1)S(1)}, bf16[4,512,4096]{2,1,0:T(8,128)(2,1)}, u32[]{:S(2)}) %copy-start.3) | copy-done | bytes 16777240
  229.5 5.9 %scatter.2 = bf16[8,256,128]{2,1,0:T(8,128)(2,1)} custom-call(s32[2]{0:T(128)S(1)} %pad_add_fusion.shard_ref, bf16[4,512,4096]{2,1,0:T(8,128)(2,1)S(1)} %copy-done.3, bf16[4096,512]{1,0:T(8,128)(2,1)} %bitcast.6.back_ref), custom_call_target="tpu_custom_call" | custom-call | flops 1073741824 | bytes 12582912 | tf_op jit(solution)/shard_map/scatter/pallas_call | solution.py:104
  235.4 0.0 collective-permute-done.1
  235.4 0.7 constant_dynamic-update-slice_fusion
  (10 shorter events, 0.0 us)
Async XLA Ops:
  0.6 20.9 %all-to-all-start = ((bf16[2,4,256,128]{3,2,1,0:T(8,128)(2,1)}), bf16[2,4,256,128]{3,2,1,0:T(8,128)(2,1)S(1)}, u32[]{:S(2)}, u32[]{:S(2)}) async-start(bf16[2,4,256,128]{3,2,1,0:T(8,128)(2,1)} %bitcast.12), calls=%async_computation | async-start | bytes 1048576 | tf_op jit(solution)/shard_map/all_to_all | solution.py:232
  4.1 1.2 copy-start.9
  5.4 0.9 copy-start.11
  15.8 5.7 %copy-start = (bf16[4,512,4096]{2,1,0:T(8,128)(2,1)}, bf16[4,512,4096]{2,1,0:T(8,128)(2,1)S(1)}, u32[]{:S(2)}) copy-start(bf16[4,512,4096]{2,1,0:T(8,128)(2,1)S(1)} %count.1.counts_ref) | copy-start | bytes 50331652
  21.5 5.8 %copy-start.1 = (bf16[4,512,4096]{2,1,0:T(8,128)(2,1)S(1)}, bf16[4,512,4096]{2,1,0:T(8,128)(2,1)}, u32[]{:S(2)}) copy-start(bf16[4,512,4096]{2,1,0:T(8,128)(2,1)} %copy-done) | copy-start | bytes 50331652
  99.3 5.8 %copy-start.4 = (bf16[32768,256]{1,0:T(8,128)(2,1)S(1)}, bf16[32768,256]{1,0:T(8,128)(2,1)}, u32[]{:S(2)}) copy-start(bf16[32768,256]{1,0:T(8,128)(2,1)} %down_ref.3) | copy-start | bytes 50331652
  105.1 5.8 %copy-start.6 = (bf16[256,32768]{1,0:T(8,128)(2,1)S(1)}, bf16[256,32768]{1,0:T(8,128)(2,1)}, u32[]{:S(2)}) copy-start(bf16[256,32768]{1,0:T(8,128)(2,1)} %up_ref.3) | copy-start | bytes 50331652
  110.9 10.5 %copy-start.8 = (bf16[64,64,512]{2,1,0:T(8,128)(2,1)}, bf16[64,64,512]{2,1,0:T(8,128)(2,1)S(1)}, u32[]{:S(2)}) copy-start(bf16[64,64,512]{2,1,0:T(8,128)(2,1)S(1)} %all_to_all.15.x0_ref) | copy-start | bytes 12582916
  110.9 15.3 %copy-start.10 = (f32[32768]{0:T(1024)S(1)}, f32[32768]{0:T(1024)}, u32[]{:S(2)}) copy-start(f32[32768]{0:T(1024)} %param.12) | copy-start | bytes 393220
  121.4 4.7 %collective-permute-start = (f32[128,256]{1,0:T(8,128)S(1)}, f32[128,256]{1,0:T(8,128)S(1)}, u32[]{:S(2)}, u32[]{:S(2)}) collective-permute-start(f32[128,256]{1,0:T(8,128)S(1)} %project.1.mine_ref), channel_id=1, source_target_pairs={{0,1},{1,0},{2,3},{3,2},{4,5},{5,4},{6,7},{7,6},{8,9},{9,8},{10,11... | collective-permute-start | bytes 393224 | tf_op jit(solution)/shard_map/ppermute | solution.py:243
  126.2 5.8 %copy-start.5 = (bf16[32768,256]{1,0:T(8,128)(2,1)S(1)}, bf16[32768,256]{1,0:T(8,128)(2,1)}, u32[]{:S(2)}) copy-start(bf16[32768,256]{1,0:T(8,128)(2,1)} %down_ref.3) | copy-start | bytes 50331652
  131.9 5.8 %copy-start.7 = (bf16[256,32768]{1,0:T(8,128)(2,1)S(1)}, bf16[256,32768]{1,0:T(8,128)(2,1)}, u32[]{:S(2)}) copy-start(bf16[256,32768]{1,0:T(8,128)(2,1)} %up_ref.3) | copy-start | bytes 50331652
  149.9 59.9 %all-to-all-start.2 = ((bf16[64,64,512]{2,1,0:T(8,128)(2,1)}), bf16[64,64,512]{2,1,0:T(8,128)(2,1)}, u32[]{:S(2)}, u32[]{:S(2)}) async-start(bf16[64,64,512]{2,1,0:T(8,128)(2,1)} %get-tuple-element.5), calls=%async_computation.2 | async-start | bytes 8388608 | tf_op jit(solution)/shard_map/all_to_all | solution.py:245
  209.8 5.8 %copy-start.2 = (bf16[4,512,4096]{2,1,0:T(8,128)(2,1)S(1)}, bf16[4,512,4096]{2,1,0:T(8,128)(2,1)}, u32[]{:S(2)}) copy-start(bf16[4,512,4096]{2,1,0:T(8,128)(2,1)} %copy-done) | copy-start | bytes 50331652
  220.7 14.7 %collective-permute-start.1 = (bf16[4,256,128]{2,1,0:T(8,128)(2,1)S(1)}, bf16[4,256,128]{2,1,0:T(8,128)(2,1)S(1)}, u32[]{:S(2)}, u32[]{:S(2)}) collective-permute-start(bf16[4,256,128]{2,1,0:T(8,128)(2,1)S(1)} %scatter.3), channel_id=1, source_target_pairs={{0,1},{1,0},{2,3},{3,2},{4,5},{5,4},{6,7},{7,6},{8,9},{9,8},{10,11... | collective-permute-start | bytes 786440 | tf_op jit(solution)/shard_map/ppermute | solution.py:248
  223.8 5.8 %copy-start.3 = (bf16[4,512,4096]{2,1,0:T(8,128)(2,1)S(1)}, bf16[4,512,4096]{2,1,0:T(8,128)(2,1)}, u32[]{:S(2)}) copy-start(bf16[4,512,4096]{2,1,0:T(8,128)(2,1)} %copy-done) | copy-start | bytes 50331652

commit v3 on v0

v3 whole, which is shorter than its diff:
```python
import jax
import jax.numpy as jnp
from jax import lax
from jax.experimental import pallas as pl
from jax.experimental.pallas import tpu as pltpu
from jax.sharding import PartitionSpec as P

FIELDS = 8
BITS = 4
LANES = 128
MIB = 1 << 20
AHEAD = 3
HELD = pl.BlockSpec(memory_space=pltpu.VMEM)
FAR = pl.BlockSpec(memory_space=pl.ANY)


def near(x):
    return pltpu.with_memory_space_constraint(x, pltpu.VMEM)


def far(x):
    return pltpu.with_memory_space_constraint(x, pltpu.HBM)


def params(mib):
    return pltpu.CompilerParams(vmem_limit_bytes=mib * MIB)


def cost(flops, moved):
    return pl.CostEstimate(flops=flops, bytes_accessed=moved, transcendentals=0)


def count_kernel(shard_ref, ids_ref, lengths_ref, counts_ref):
    tables, vocab = counts_ref.shape[:2]
    bag, batch = ids_ref.shape[1:]
    rows = vocab // FIELDS
    feat = shard_ref[0] * tables
    base = pl.program_id(0) * batch
    slot = lax.broadcasted_iota(jnp.int32, (bag, LANES), 0)
    table_row = lax.broadcasted_iota(jnp.int32, (rows, LANES), 0)
    for k in range(tables):
        for start in range(0, batch, LANES):
            cols = pl.ds(start, LANES)
            out = pl.ds(pl.multiple_of(base + start, LANES), LANES)
            ids = ids_ref[feat + k, :, cols]
            length = lengths_ref[k : k + 1, cols]
            for other in range(1, lengths_ref.shape[0] // tables):
                at = other * tables + k
                length = jnp.where(shard_ref[0] == other, lengths_ref[at : at + 1, cols], length)
            row = jnp.where(slot < length, ids & (rows - 1), -1)
            unit = jnp.left_shift(1, lax.shift_right_logical(ids, rows.bit_length() - 1) * BITS)
            total = jnp.zeros((rows, LANES), jnp.int32)
            for p in range(bag):
                total = total + jnp.where(table_row == row[p : p + 1], unit[p : p + 1], 0)
            for j in range(FIELDS):
                field = lax.shift_right_logical(total, j * BITS) & ((1 << BITS) - 1)
                counts_ref[k, j * rows : (j + 1) * rows, out] = field.astype(jnp.float32).astype(jnp.bfloat16)


def count(shard, ids, lengths, tables, vocab):
    feats, bag, batch = ids.shape
    chunk = 512
    return pl.pallas_call(
        count_kernel,
        grid_spec=pltpu.PrefetchScalarGridSpec(
            num_scalar_prefetch=1,
            grid=(batch // chunk,),
            in_specs=[
                pl.BlockSpec((feats, bag, chunk), lambda b, s: (0, 0, b)),
                pl.BlockSpec((feats, chunk), lambda b, s: (0, b)),
            ],
            out_specs=HELD,
        ),
        out_shape=pltpu.VMEM((tables, vocab, batch), jnp.bfloat16),
        compiler_params=params(8),
        cost_estimate=cost(tables * vocab * bag * batch, 4 * ids.size),
        name="count",
    )(shard, far(ids), far(lengths))


def pool_kernel(shard_ref, counts_ref, own_ref, other_ref, pooled_ref, saved_ref, sem):
    part, width = own_ref.shape[1:]
    owners, _, samples, _ = pooled_ref.shape
    chunk = owners * samples
    k, step = pl.program_id(0), pl.program_id(1)
    save = pltpu.make_async_copy(counts_ref, saved_ref, sem)

    @pl.when((k == 0) & (step == 0))
    def _():
        save.start()

    cols = pl.ds(pl.multiple_of(step * chunk, chunk), chunk)
    total = jnp.zeros((width, chunk), jnp.float32)
    for place, table_ref in ((shard_ref[0], own_ref), (1 - shard_ref[0], other_ref)):
        rows = pl.ds(pl.multiple_of(place * part, part), part)
        total += lax.dot_general(
            table_ref[0], counts_ref[k, rows, cols], (((0,), (0,)), ((), ())), preferred_element_type=jnp.float32
        )
    pooled_ref[:, 0] = jnp.transpose(total.astype(jnp.bfloat16)).reshape(owners, samples, width)

    @pl.when((k == pl.num_programs(0) - 1) & (step == pl.num_programs(1) - 1))
    def _():
        save.wait()


def pool(shard, counts, tables, other, owners):
    pair, vocab, batch = counts.shape
    part, width = tables.shape[1:]
    steps = 2
    return pl.pallas_call(
        pool_kernel,
        grid_spec=pltpu.PrefetchScalarGridSpec(
            num_scalar_prefetch=1,
            grid=(pair, steps),
            in_specs=[
                HELD,
                pl.BlockSpec((1, part, width), lambda k, b, s: (s[0] * pair + k, 0, 0)),
                pl.BlockSpec((1, part, width), lambda k, b, s: (k, 0, 0)),
            ],
            out_specs=[
                pl.BlockSpec((owners // steps, 1, batch // owners, width), lambda k, b, s: (b, k, 0, 0)),
                FAR,
            ],
            scratch_shapes=[pltpu.SemaphoreType.DMA],
        ),
        out_shape=[
            jax.ShapeDtypeStruct((owners, pair, batch // owners, width), jnp.bfloat16),
            pltpu.HBM(counts.shape, counts.dtype),
        ],
        compiler_params=params(10),
        cost_estimate=cost(2 * counts.size * width, 4 * counts.size),
        name="pool",
    )(shard, near(counts), tables, other)


def scatter_kernel(shard_ref, counts_ref, back_ref, grad_ref):
    owners, _, samples, width = back_ref.shape
    back = back_ref[:, 0].reshape(owners * samples, width)
    grad_ref[0] = jnp.dot(counts_ref[0], back, preferred_element_type=jnp.float32).astype(jnp.bfloat16)


def scatter(shard, counts, back, shards, away):
    pair, vocab, batch = counts.shape
    part = vocab // shards
    owners, _, samples, width = back.shape
    return pl.pallas_call(
        scatter_kernel,
        grid_spec=pltpu.PrefetchScalarGridSpec(
            num_scalar_prefetch=1,
            grid=(pair,),
            in_specs=[
                pl.BlockSpec((1, part, batch), lambda k, s: (k, 1 - s[0] if away else s[0], 0)),
                pl.BlockSpec((owners, 1, samples, width), lambda k, s: (0, k, 0, 0)),
            ],
            out_specs=pl.BlockSpec((1, part, width), lambda k, s: (k if away else s[0] * pair + k, 0, 0)),
        ),
        out_shape=jax.ShapeDtypeStruct((pair if away else shards * pair, part, width), jnp.bfloat16),
        compiler_params=params(12),
        cost_estimate=cost(2 * counts.size // shards * width, 2 * counts.size // shards + 2 * back.size),
        name="scatter",
    )(shard, far(counts), back)


def row_of(x0_ref):
    groups, tables = x0_ref.shape[:2]
    return jnp.concatenate([x0_ref[g, k] for g in range(groups) for k in range(tables)], axis=1)


def stream(weight_ref, held_ref, sems, piece, steps):
    step = pl.program_id(0)

    def copy(i):
        return pltpu.make_async_copy(weight_ref.at[piece(i)], held_ref.at[piece(i)], sems.at[i])

    @pl.when(step == 0)
    def _():
        for i in range(min(AHEAD, steps)):
            copy(i).start()

    @pl.when(step + AHEAD < steps)
    def _():
        copy(step + AHEAD).start()

    copy(step).wait()


def add_up(total_ref, part):
    @pl.when(pl.program_id(0) == 0)
    def _():
        total_ref[...] = part

    @pl.when(pl.program_id(0) > 0)
    def _():
        total_ref[...] += part


def dlow_kernel(x0_ref, grad_ref, up_ref, dlow_ref):
    dgate = (grad_ref[...].astype(jnp.float32) * row_of(x0_ref).astype(jnp.float32)).astype(jnp.bfloat16)
    add_up(dlow_ref, lax.dot_general(dgate, up_ref[...], (((1,), (1,)), ((), ())), preferred_element_type=jnp.float32))


def low_kernel(steps, x0_ref, down_ref, low_ref, held_ref, sems):
    groups, tables, _, cols = x0_ref.shape
    width = groups * tables * cols
    span = lambda i: pl.ds(pl.multiple_of(i * width, width), width)
    x0 = row_of(x0_ref)
    stream(down_ref, held_ref, sems, span, steps)
    add_up(low_ref, jnp.dot(x0, held_ref[span(pl.program_id(0)), :], preferred_element_type=jnp.float32))


def spread_kernel(groups_cols, mine_ref, other_ref, down_ref, spread_ref):
    span = pl.ds(pl.multiple_of(pl.program_id(0) * groups_cols, groups_cols), groups_cols)
    dlow = (mine_ref[...] + other_ref[...]).astype(jnp.bfloat16)
    spread_ref[:, span] = lax.dot_general(
        dlow, down_ref[span, :], (((1,), (1,)), ((), ())), preferred_element_type=jnp.float32
    )


def cross_kernel(mine_ref, other_ref, x0_ref, up_ref, bias_ref, grad_ref, spread_ref, crossed_ref, back_ref):
    groups, tables, _, cols = x0_ref.shape
    width = groups * tables * cols
    span = pl.ds(pl.multiple_of(pl.program_id(0) * width, width), width)
    low = (mine_ref[...] + other_ref[...]).astype(jnp.bfloat16)
    gate = jnp.dot(low, up_ref[...], preferred_element_type=jnp.float32) + bias_ref[...]
    x0 = row_of(x0_ref).astype(jnp.float32)
    crossed_ref[...] = (x0 * gate + x0).astype(jnp.bfloat16)
    upstream = grad_ref[...].astype(jnp.float32)
    back = (upstream * gate + upstream + spread_ref[:, span]).astype(jnp.bfloat16)
    for g in range(groups):
        for k in range(tables):
            at = (g * tables + k) * cols
            back_ref[g, k] = back[:, at : at + cols]


def cross_layer(x0, down, up, bias, grad):
    owners, tables, samples, cols = x0.shape
    rank = down.shape[1]
    groups = 8
    steps = owners // groups
    width = groups * tables * cols
    x0_spec = pl.BlockSpec((groups, tables, samples, cols), lambda i: (i, 0, 0, 0))
    row_spec = pl.BlockSpec((samples, width), lambda i: (0, i))
    up_spec = pl.BlockSpec((rank, width), lambda i: (0, i))
    sum_spec = pl.BlockSpec((samples, rank), lambda i: (0, 0))
    sum_shape = jax.ShapeDtypeStruct((samples, rank), jnp.float32)
    work = 2 * x0.size * rank
    swap = [(0, 1), (1, 0)]

    def call(kernel, in_specs, out_specs, out_shape, mib, moved, name, *operands, sems=0):
        return pl.pallas_call(
            kernel,
            grid=(steps,),
            in_specs=in_specs,
            out_specs=out_specs,
            out_shape=out_shape,
            scratch_shapes=[pltpu.SemaphoreType.DMA((sems,))] if sems else [],
            compiler_params=params(mib),
            cost_estimate=cost(work, moved),
            name=name,
        )(*operands)

    dlow = call(
        dlow_kernel, [x0_spec, row_spec, up_spec], sum_spec, sum_shape, 12, 2 * up.size + 4 * x0.size, "dlow",
        x0, grad, far(up),
    )
    dlow_other = lax.ppermute(dlow, "row", swap)
    low, down = call(
        lambda *refs: low_kernel(steps, *refs), [x0_spec, FAR], [sum_spec, HELD],
        [sum_shape, pltpu.VMEM(down.shape, down.dtype)], 8, 2 * down.size + 2 * x0.size, "low",
        x0, far(down), sems=steps,
    )
    low_other = lax.ppermute(low, "row", swap)
    spread = call(
        lambda *refs: spread_kernel(width, *refs), [sum_spec, sum_spec, HELD], HELD,
        pltpu.VMEM((samples, owners * tables * cols), jnp.float32), 6, 4 * x0.size, "spread",
        dlow, dlow_other, near(down),
    )
    return call(
        cross_kernel,
        [sum_spec, sum_spec, x0_spec, up_spec, pl.BlockSpec((1, width), lambda i: (0, i)), row_spec, HELD],
        [row_spec, x0_spec],
        [pltpu.HBM((samples, owners * tables * cols), jnp.bfloat16), pltpu.HBM(x0.shape, jnp.bfloat16)],
        16, 8 * x0.size, "cross",
        low, low_other, x0, far(up), bias, grad, near(spread),
    )


def body(ids, lengths, tables, cross_down, cross_up, bias, grad_out):
    batch, feats, bag = ids.shape
    part, width = tables.shape[1:]
    shards = lax.axis_size("row")
    owners = lax.axis_size("table")
    pair = feats // shards
    shard = lax.axis_index("row").astype(jnp.int32)
    mine = shard.reshape(1)
    swap = [(0, 1), (1, 0)]
    sent = lax.dynamic_slice_in_dim(tables, (1 - shard) * pair, pair, 0)
    other = lax.ppermute(sent, "row", swap)
    counts = count(mine, jnp.transpose(ids, (1, 2, 0)), jnp.transpose(lengths), pair, shards * part)
    pooled, counts = pool(mine, counts, tables, other, owners)
    x0 = lax.all_to_all(pooled, "table", split_axis=0, concat_axis=0, tiled=True)
    crossed, x0_grad = cross_layer(x0, cross_down, cross_up, bias.reshape(1, -1), grad_out)
    back = lax.all_to_all(x0_grad, "table", split_axis=0, concat_axis=0, tiled=True)
    outgoing = scatter(mine, counts, back, shards, True)
    incoming = lax.ppermute(outgoing, "row", swap)
    own = scatter(mine, counts, back, shards, False)
    table_grad = lax.dynamic_update_slice_in_dim(own, incoming, (1 - shard) * pair, 0)
    return (crossed, table_grad)


def solution(mesh):
    in_specs = (
        P(None, "table", None),
        P(None, "table"),
        P("table", "row", None),
        P("row", None),
        P(None, "row"),
        P("row"),
        P("table", "row"),
    )
    out_specs = (P("table", "row"), P("table", "row", None))
    return jax.shard_map(body, mesh=mesh, in_specs=in_specs, out_specs=out_specs, check_vma=False)
```

time: 322 us -> 200 us (0.62)
  matrix products: 71.5 us -> 0 us
  other arithmetic: 70.9 us -> 0 us
  Pallas kernels: 0 us -> 67.4 us
  local copies, waits for them, and re-layouts: 29.1 us -> 1.71 us
  blocking collectives: 145 us -> 124 us
    dot_general x6 -> x0, matrix products: 71.5 us -> none  [the longest x1 15.6 us: body(): gate = jnp.dot(low, cross_up, preferred_element_type=jnp.float32) + bias]
    dynamic_update_slice x4 -> x0, other arithmetic: 70.8 us -> none  [body(): lax.map(lambda items: count_rows(items[0], items[1], owned.shape[1]), (ow...]
    pallas_call x0 -> x8, Pallas kernels: none -> 67.4 us  [the longest x4 36.3 us: call(): pl.pallas_call(kernel, grid=(steps,), in_specs=in_specs, out_specs=out_sp...]
    all_to_all x3 -> x2, blocking collectives: 137 us -> 124 us  [the longest x1 65.2 us: body(): lax.all_to_all(pooled, 'table', split_axis=0, concat_axis=0, tiled=True)]
    all_to_all x5 -> x0, local copies, waits for them, and re-layouts: 11.2 us -> none  [the longest x2 7.56 us: body(): lax.all_to_all(outgoing, 'table', split_axis=0, concat_axis=1, tiled=True)]
    convert_element_type x2 -> x0, local copies, waits for them, and re-layouts: 7.97 us -> none  [the longest x1 7.57 us: body(): pooled.astype(jnp.bfloat16)]
    psum x1 -> x0, blocking collectives: 7.58 us -> none  [body(): low = lax.psum(low_part, 'row').astype(jnp.bfloat16)]
    reshape x1 -> x0, local copies, waits for them, and re-layouts: 7.02 us -> none  [body(): lax.all_to_all(x0_grad, 'table', split_axis=1, concat_axis=0, tiled=True)]
  transfers between devices with their start and end apart: 1 -> 4, of which waited for: 0 -> 1; matrix products, arithmetic and copies ran while one was open for 23% -> 0% of each run, Pallas kernels for 0% -> 16%
where the time goes in v3:
time: 200 us; the launch traced here: 199 us
  blocking collectives  124 us (62%)
  Pallas kernels  67.4 us (34%)
  starting transfers between devices  4.02 us (2%)
    all_to_all x1, blocking collectives, body(): lax.all_to_all(pooled, 'table', split_axis=0, concat_axis=0, tiled=True)  65.2 us
    all_to_all x1, blocking collectives, body(): lax.all_to_all(x0_grad, 'table', split_axis=0, concat_axis=0, tiled=True)  59 us
    pallas_call x4, Pallas kernels, call(): pl.pallas_call(kernel, grid=(steps,), in_specs=in_specs, out_specs=out_sp...  36.3 us
    pallas_call x1, Pallas kernels, count(): pl.pallas_call(count_kernel, grid_spec=pltpu.PrefetchScalarGridSpec(num_s...  13.5 us
    pallas_call x2, Pallas kernels, scatter(): pl.pallas_call(scatter_kernel, grid_spec=pltpu.PrefetchScalarGridSpec(num...  11.8 us
    pallas_call x1, Pallas kernels, pool(): pl.pallas_call(pool_kernel, grid_spec=pltpu.PrefetchScalarGridSpec(num_sc...  5.83 us
  transfers between devices with their start and end apart: 4, of which 1 were waited for; matrix products, arithmetic and copies ran while one was open for 0% of the time, Pallas kernels for 16%

profile of v3, /device:TPU:1, one launch (start us, length us, event | category | flops | bytes accessed | tf_op | source)
XLA Modules:
  0.0 199.1 jit_solution(6630706333660354076)
XLA Ops:
  0.6 1.0 constant_dynamic-slice_fusion
  1.6 2.1 %collective-permute-start = (bf16[4,256,128]{2,1,0:T(8,128)(2,1)S(1)}, bf16[4,256,128]{2,1,0:T(8,128)(2,1)S(1)}, u32[]{:S(2)}, u32[]{:S(2)}) collective-permute-start(bf16[4,256,128]{2,1,0:T(8,128)(2,1)S(1)} %constant_dynamic-slice_fusion), channel_id=1, source_target_pairs={{0,1},{1,0},{2,3},{3,2},{4,5},{5,4},{6,7},{7,6},{8,9},{9,8},{10,11... | collective-permute-start | bytes 786440 | tf_op jit(solution)/shard_map/ppermute | solution.py:298
  3.7 0.0 copy-start.1
  3.7 13.5 %count.1.counts_ref = bf16[4,512,4096]{2,1,0:T(8,128)(2,1)S(1)} custom-call(s32[1]{0:T(128)} %bitcast.shard_ref, s32[8,8,4096]{2,1,0:T(8,128)} %bitcast.5, s32[8,4096]{1,0:T(8,128)} %bitcast.6), custom_call_target="tpu_custom_call" | custom-call | flops 67108864 | bytes 1048576 | tf_op jit(solution)/shard_map/count/pallas_call | solution.py:63
  17.2 0.0 collective-permute-done.other_ref
  17.2 0.0 copy-done.1
  17.2 5.8 %pool.1 = (bf16[64,4,64,128]{3,2,1,0:T(8,128)(2,1)S(1)}, bf16[4,512,4096]{2,1,0:T(8,128)(2,1)}) custom-call(s32[1]{0:T(128)} %bitcast.shard_ref, bf16[4,512,4096]{2,1,0:T(8,128)(2,1)S(1)} %count.1.counts_ref, bf16[8,256,128]{2,1,0:T(8,128)(2,1)S(1)} %copy-done.1, bf16[4,256,128]{2,1,0:T(8,128)(2,1)S(1)} %collective-permute-done.other_ref), custom_call_target="tpu_custom_call" | custom-call | flops 2147483648 | bytes 33554432 | tf_op jit(solution)/shard_map/pool/pallas_call | solution.py:110
  23.1 0.0 copy-start
  23.1 65.2 %all_to_all.10.refs_0_.x0_ref = bf16[64,4,64,128]{3,2,1,0:T(8,128)(2,1)S(1)} all-to-all(bf16[64,4,64,128]{3,2,1,0:T(8,128)(2,1)S(1)} %get-tuple-element.8), channel_id=1, replica_groups=mesh['table'=64,'row'=2] {'table'}, dimensions={0} | all-to-all | bytes 8388608 | tf_op jit(solution)/shard_map/all_to_all | solution.py:301
  88.3 0.0 copy-done
  88.3 10.9 %dlow.1.refs_0_ = f32[64,256]{1,0:T(8,128)S(1)} custom-call(bf16[64,4,64,128]{3,2,1,0:T(8,128)(2,1)S(1)} %all_to_all.10.refs_0_.x0_ref, bf16[64,32768]{1,0:T(8,128)(2,1)S(1)} %copy-done, bf16[256,32768]{1,0:T(8,128)(2,1)} %up_ref.3), custom_call_target="tpu_custom_call" | custom-call | flops 1073741824 | bytes 25165824 | tf_op jit(solution)/shard_map/dlow/pallas_call | solution.py:250
  99.2 0.1 collective-permute-start.2
  99.2 6.7 %low.1 = (f32[64,256]{1,0:T(8,128)S(1)}, bf16[32768,256]{1,0:T(8,128)(2,1)S(1)}) custom-call(bf16[64,4,64,128]{3,2,1,0:T(8,128)(2,1)S(1)} %all_to_all.10.refs_0_.x0_ref, bf16[32768,256]{1,0:T(8,128)(2,1)} %refs_1_.1), custom_call_target="tpu_custom_call" | custom-call | flops 1073741824 | bytes 20971520 | tf_op jit(solution)/shard_map/low/pallas_call | solution.py:250
  105.9 1.5 collective-permute-start.1
  107.5 0.0 collective-permute-done.2.refs_1_
  107.5 0.0 copy-start.2
  107.5 6.0 %spread.1.spread_ref = f32[64,32768]{1,0:T(8,128)S(1)} custom-call(f32[64,256]{1,0:T(8,128)S(1)} %dlow.1.refs_0_, f32[64,256]{1,0:T(8,128)S(1)} %collective-permute-done.2.refs_1_, bf16[32768,256]{1,0:T(8,128)(2,1)S(1)} %get-tuple-element.10.refs_2_), custom_call_target="tpu_custom_call" | custom-call | flops 1073741824 | bytes 8388608 | tf_op jit(solution)/shard_map/spread/pallas_call | solution.py:250
  113.5 0.0 collective-permute-done.1.other_ref
  113.5 0.0 copy-done.2
  113.5 12.7 %cross.1 = (bf16[64,32768]{1,0:T(8,128)(2,1)}, bf16[64,4,64,128]{3,2,1,0:T(8,128)(2,1)}) custom-call(f32[64,256]{1,0:T(8,128)S(1)} %get-tuple-element.9.mine_ref, f32[64,256]{1,0:T(8,128)S(1)} %collective-permute-done.1.other_ref, bf16[64,4,64,128]{3,2,1,0:T(8,128)(2,1)S(1)} %all_to_all.10.refs_0_.x0_ref, bf16[256,32768]{1,0:T(8,128)(2,1)} %up_ref.3, ...), custom_call_target="tpu_custom_call" | custom-call | flops 1073741824 | bytes 16777216 | tf_op jit(solution)/shard_map/cross/pallas_call | solution.py:250
  126.3 59.0 %all_to_all.11.back_ref = bf16[64,4,64,128]{3,2,1,0:T(8,128)(2,1)S(1)} all-to-all(bf16[64,4,64,128]{3,2,1,0:T(8,128)(2,1)} %get-tuple-element.13), channel_id=1, replica_groups=mesh['table'=64,'row'=2] {'table'}, dimensions={0} | all-to-all | bytes 8388608 | tf_op jit(solution)/shard_map/all_to_all | solution.py:303
  185.3 5.6 %scatter.3 = bf16[4,256,128]{2,1,0:T(8,128)(2,1)S(1)} custom-call(s32[1]{0:T(128)} %bitcast.shard_ref, bf16[4,512,4096]{2,1,0:T(8,128)(2,1)} %get-tuple-element.12.counts_ref, bf16[64,4,64,128]{3,2,1,0:T(8,128)(2,1)S(1)} %all_to_all.11.back_ref), custom_call_target="tpu_custom_call" | custom-call | flops 1073741824 | bytes 12582912 | tf_op jit(solution)/shard_map/scatter/pallas_call | solution.py:146
  190.8 0.3 collective-permute-start.3
  191.1 6.2 %scatter.2 = bf16[8,256,128]{2,1,0:T(8,128)(2,1)} custom-call(s32[1]{0:T(128)} %bitcast.shard_ref, bf16[4,512,4096]{2,1,0:T(8,128)(2,1)} %get-tuple-element.12.counts_ref, bf16[64,4,64,128]{3,2,1,0:T(8,128)(2,1)S(1)} %all_to_all.11.back_ref), custom_call_target="tpu_custom_call" | custom-call | flops 1073741824 | bytes 12582912 | tf_op jit(solution)/shard_map/scatter/pallas_call | solution.py:146
  197.3 1.0 collective-permute-done.3
  198.4 0.7 constant_dynamic-update-slice_fusion
Async XLA Ops:
  1.6 15.6 %collective-permute-start = (bf16[4,256,128]{2,1,0:T(8,128)(2,1)S(1)}, bf16[4,256,128]{2,1,0:T(8,128)(2,1)S(1)}, u32[]{:S(2)}, u32[]{:S(2)}) collective-permute-start(bf16[4,256,128]{2,1,0:T(8,128)(2,1)S(1)} %constant_dynamic-slice_fusion), channel_id=1, source_target_pairs={{0,1},{1,0},{2,3},{3,2},{4,5},{5,4},{6,7},{7,6},{8,9},{9,8},{10,11... | collective-permute-start | bytes 786440 | tf_op jit(solution)/shard_map/ppermute | solution.py:298
  3.7 13.5 %copy-start.1 = (bf16[8,256,128]{2,1,0:T(8,128)(2,1)S(1)}, bf16[8,256,128]{2,1,0:T(8,128)(2,1)}, u32[]{:S(2)}) copy-start(bf16[8,256,128]{2,1,0:T(8,128)(2,1)} %own_ref.1) | copy-start | bytes 1572868
  23.1 65.2 %copy-start = (bf16[64,32768]{1,0:T(8,128)(2,1)S(1)}, bf16[64,32768]{1,0:T(8,128)(2,1)}, u32[]{:S(2)}) copy-start(bf16[64,32768]{1,0:T(8,128)(2,1)} %grad_ref.3) | copy-start | bytes 12582916
  99.2 8.3 %collective-permute-start.2 = (f32[64,256]{1,0:T(8,128)S(1)}, f32[64,256]{1,0:T(8,128)S(1)}, u32[]{:S(2)}, u32[]{:S(2)}) collective-permute-start(f32[64,256]{1,0:T(8,128)S(1)} %dlow.1.refs_0_), channel_id=1, source_target_pairs={{0,1},{1,0},{2,3},{3,2},{4,5},{5,4},{6,7},{7,6},{8,9},{9,8},{10,11... | collective-permute-start | bytes 196616 | tf_op jit(solution)/shard_map/ppermute | solution.py:266
  105.9 7.6 %collective-permute-start.1 = (f32[64,256]{1,0:T(8,128)S(1)}, f32[64,256]{1,0:T(8,128)S(1)}, u32[]{:S(2)}, u32[]{:S(2)}) collective-permute-start(f32[64,256]{1,0:T(8,128)S(1)} %get-tuple-element.9.mine_ref), channel_id=1, source_target_pairs={{0,1},{1,0},{2,3},{3,2},{4,5},{5,4},{6,7},{7,6},{8,9},{9,8},{10,11... | collective-permute-start | bytes 196616 | tf_op jit(solution)/shard_map/ppermute | solution.py:272
  107.5 6.1 %copy-start.2 = (f32[32768]{0:T(1024)S(1)}, f32[32768]{0:T(1024)}, u32[]{:S(2)}) copy-start(f32[32768]{0:T(1024)} %param.12) | copy-start | bytes 393220
  190.8 7.5 %collective-permute-start.3 = (bf16[4,256,128]{2,1,0:T(8,128)(2,1)S(1)}, bf16[4,256,128]{2,1,0:T(8,128)(2,1)S(1)}, u32[]{:S(2)}, u32[]{:S(2)}) collective-permute-start(bf16[4,256,128]{2,1,0:T(8,128)(2,1)S(1)} %scatter.3), channel_id=1, source_target_pairs={{0,1},{1,0},{2,3},{3,2},{4,5},{5,4},{6,7},{7,6},{8,9},{9,8},{10,11... | collective-permute-start | bytes 786440 | tf_op jit(solution)/shard_map/ppermute | solution.py:305

commit v4 on v3

v4 whole, which is shorter than its diff:
```python
import jax
import jax.numpy as jnp
from jax import lax
from jax.experimental import pallas as pl
from jax.experimental.pallas import tpu as pltpu
from jax.sharding import PartitionSpec as P

FIELDS = 8
BITS = 4
LANES = 128
MIB = 1 << 20
AHEAD = 3
HELD = pl.BlockSpec(memory_space=pltpu.VMEM)
FAR = pl.BlockSpec(memory_space=pl.ANY)


def near(x):
    return pltpu.with_memory_space_constraint(x, pltpu.VMEM)


def far(x):
    return pltpu.with_memory_space_constraint(x, pltpu.HBM)


def params(mib):
    return pltpu.CompilerParams(vmem_limit_bytes=mib * MIB)


def cost(flops, moved):
    return pl.CostEstimate(flops=flops, bytes_accessed=moved, transcendentals=0)


def count_kernel(shard_ref, ids_ref, lengths_ref, counts_ref):
    tables, vocab = counts_ref.shape[1:3]
    bag, batch = ids_ref.shape[1:]
    rows = vocab // FIELDS
    feat = shard_ref[0] * tables
    step = pl.program_id(0)
    slot = lax.broadcasted_iota(jnp.int32, (bag, LANES), 0)
    table_row = lax.broadcasted_iota(jnp.int32, (rows, LANES), 0)
    for k in range(tables):
        for start in range(0, batch, LANES):
            cols = pl.ds(start, LANES)
            ids = ids_ref[feat + k, :, cols]
            length = lengths_ref[k : k + 1, cols]
            for other in range(1, lengths_ref.shape[0] // tables):
                at = other * tables + k
                length = jnp.where(shard_ref[0] == other, lengths_ref[at : at + 1, cols], length)
            row = jnp.where(slot < length, ids & (rows - 1), -1)
            unit = jnp.left_shift(1, lax.shift_right_logical(ids, rows.bit_length() - 1) * BITS)
            total = jnp.zeros((rows, LANES), jnp.int32)
            for p in range(bag):
                total = total + jnp.where(table_row == row[p : p + 1], unit[p : p + 1], 0)
            for j in range(FIELDS):
                field = lax.shift_right_logical(total, j * BITS) & ((1 << BITS) - 1)
                counts_ref[step, k, j * rows : (j + 1) * rows, cols] = field.astype(jnp.float32).astype(jnp.bfloat16)


def count(shard, ids, lengths, tables, vocab):
    feats, bag, batch = ids.shape
    chunk = 512
    return pl.pallas_call(
        count_kernel,
        grid_spec=pltpu.PrefetchScalarGridSpec(
            num_scalar_prefetch=1,
            grid=(batch // chunk,),
            in_specs=[
                pl.BlockSpec((feats, bag, chunk), lambda b, s: (0, 0, b)),
                pl.BlockSpec((feats, chunk), lambda b, s: (0, b)),
            ],
            out_specs=HELD,
        ),
        out_shape=pltpu.VMEM((batch // chunk, tables, vocab, chunk), jnp.bfloat16),
        compiler_params=params(8),
        cost_estimate=cost(tables * vocab * bag * batch, 4 * ids.size),
        name="count",
    )(shard, far(ids), far(lengths))


def pool_kernel(shard_ref, counts_ref, own_ref, other_ref, pooled_ref, saved_ref, sem):
    part, width = own_ref.shape[1:]
    samples = pooled_ref.shape[2]
    chunk = counts_ref.shape[3]
    blocks = pooled_ref.shape[0] * samples // chunk
    k, step = pl.program_id(0), pl.program_id(1)
    save = pltpu.make_async_copy(counts_ref, saved_ref, sem)

    @pl.when((k == 0) & (step == 0))
    def _():
        save.start()

    for c in range(blocks):
        total = jnp.zeros((width, chunk), jnp.float32)
        for place, table_ref in ((shard_ref[0], own_ref), (1 - shard_ref[0], other_ref)):
            rows = pl.ds(pl.multiple_of(place * part, part), part)
            total += lax.dot_general(
                table_ref[0], counts_ref[step * blocks + c, k, rows, :], (((0,), (0,)), ((), ())),
                preferred_element_type=jnp.float32,
            )
        owned = jnp.transpose(total.astype(jnp.bfloat16)).reshape(chunk // samples, samples, width)
        pooled_ref[c * (chunk // samples) : (c + 1) * (chunk // samples), 0] = owned

    @pl.when((k == pl.num_programs(0) - 1) & (step == pl.num_programs(1) - 1))
    def _():
        save.wait()


def pool(shard, counts, tables, other, owners):
    chunks, pair, vocab, chunk = counts.shape
    batch = chunks * chunk
    part, width = tables.shape[1:]
    steps = 2
    return pl.pallas_call(
        pool_kernel,
        grid_spec=pltpu.PrefetchScalarGridSpec(
            num_scalar_prefetch=1,
            grid=(pair, steps),
            in_specs=[
                HELD,
                pl.BlockSpec((1, part, width), lambda k, b, s: (s[0] * pair + k, 0, 0)),
                pl.BlockSpec((1, part, width), lambda k, b, s: (k, 0, 0)),
            ],
            out_specs=[
                pl.BlockSpec((owners // steps, 1, batch // owners, width), lambda k, b, s: (b, k, 0, 0)),
                FAR,
            ],
            scratch_shapes=[pltpu.SemaphoreType.DMA],
        ),
        out_shape=[
            jax.ShapeDtypeStruct((owners, pair, batch // owners, width), jnp.bfloat16),
            pltpu.HBM(counts.shape, counts.dtype),
        ],
        compiler_params=params(10),
        cost_estimate=cost(2 * counts.size * width, 4 * counts.size),
        name="pool",
    )(shard, near(counts), tables, other)


def scatter_kernel(shard_ref, counts_ref, back_ref, grad_ref):
    owners, _, samples, width = back_ref.shape
    back = back_ref[:, 0].reshape(owners * samples, width)
    counts = jnp.concatenate([counts_ref[c, 0] for c in range(counts_ref.shape[0])], axis=1)
    grad_ref[0] = jnp.dot(counts, back, preferred_element_type=jnp.float32).astype(jnp.bfloat16)


def scatter(shard, counts, back, shards, away):
    chunks, pair, vocab, chunk = counts.shape
    part = vocab // shards
    owners, _, samples, width = back.shape
    return pl.pallas_call(
        scatter_kernel,
        grid_spec=pltpu.PrefetchScalarGridSpec(
            num_scalar_prefetch=1,
            grid=(pair,),
            in_specs=[
                pl.BlockSpec((chunks, 1, part, chunk), lambda k, s: (0, k, 1 - s[0] if away else s[0], 0)),
                pl.BlockSpec((owners, 1, samples, width), lambda k, s: (0, k, 0, 0)),
            ],
            out_specs=pl.BlockSpec((1, part, width), lambda k, s: (k if away else s[0] * pair + k, 0, 0)),
        ),
        out_shape=jax.ShapeDtypeStruct((pair if away else shards * pair, part, width), jnp.bfloat16),
        compiler_params=params(12),
        cost_estimate=cost(2 * counts.size // shards * width, 2 * counts.size // shards + 2 * back.size),
        name="scatter",
    )(shard, far(counts), back)


def row_of(x0_ref):
    groups, tables = x0_ref.shape[:2]
    return jnp.concatenate([x0_ref[g, k] for g in range(groups) for k in range(tables)], axis=1)


def stream(steps, copies):
    step = pl.program_id(0)

    @pl.when(step == 0)
    def _():
        for i in range(min(AHEAD, steps)):
            for copy in copies(i):
                copy.start()

    @pl.when(step + AHEAD < steps)
    def _():
        for copy in copies(step + AHEAD):
            copy.start()

    for copy in copies(step):
        copy.wait()


def project_kernel(steps, x0_ref, grad_ref, down_ref, up_ref, sums_ref, held_ref, ring_ref, down_sems, up_sems):
    samples, width = grad_ref.shape
    step = pl.program_id(0)
    span = lambda i: pl.ds(pl.multiple_of(i * width, width), width)

    def copies(i):
        slot = lax.rem(i, AHEAD + 1)
        return (
            pltpu.make_async_copy(down_ref.at[span(i), :], held_ref.at[span(i), :], down_sems.at[slot]),
            pltpu.make_async_copy(up_ref.at[:, span(i)], ring_ref.at[slot], up_sems.at[slot]),
        )

    x0 = row_of(x0_ref)
    dgate = (grad_ref[...].astype(jnp.float32) * x0.astype(jnp.float32)).astype(jnp.bfloat16)
    stream(steps, copies)
    low = jnp.dot(x0, held_ref[span(step), :], preferred_element_type=jnp.float32)
    up = ring_ref[lax.rem(step, AHEAD + 1)]
    dlow = lax.dot_general(dgate, up, (((1,), (1,)), ((), ())), preferred_element_type=jnp.float32)

    @pl.when(step == 0)
    def _():
        sums_ref[:samples] = low
        sums_ref[samples:] = dlow

    @pl.when(step > 0)
    def _():
        sums_ref[:samples] += low
        sums_ref[samples:] += dlow


def cross_kernel(
    steps, mine_ref, other_ref, x0_ref, down_ref, up_ref, bias_ref, grad_ref, crossed_ref, back_ref, ring_ref, sems
):
    groups, tables, samples, cols = x0_ref.shape
    width = groups * tables * cols
    step = pl.program_id(0)
    span = lambda i: pl.ds(pl.multiple_of(i * width, width), width)

    def copies(i):
        slot = lax.rem(i, AHEAD + 1)
        return (pltpu.make_async_copy(up_ref.at[:, span(i)], ring_ref.at[slot], sems.at[slot]),)

    sums = (mine_ref[...] + other_ref[...]).astype(jnp.bfloat16)
    spread = lax.dot_general(
        sums[samples:], down_ref[span(step), :], (((1,), (1,)), ((), ())), preferred_element_type=jnp.float32
    )
    stream(steps, copies)
    up = ring_ref[lax.rem(step, AHEAD + 1)]
    gate = jnp.dot(sums[:samples], up, preferred_element_type=jnp.float32) + bias_ref[...]
    x0 = row_of(x0_ref).astype(jnp.float32)
    crossed_ref[...] = (x0 * gate + x0).astype(jnp.bfloat16)
    upstream = grad_ref[...].astype(jnp.float32)
    back = (upstream * gate + upstream + spread).astype(jnp.bfloat16)
    for g in range(groups):
        for k in range(tables):
            at = (g * tables + k) * cols
            back_ref[g, k] = back[:, at : at + cols]


def cross_layer(x0, down, up, bias, grad):
    owners, tables, samples, cols = x0.shape
    rank = down.shape[1]
    groups = 8
    steps = owners // groups
    width = groups * tables * cols
    x0_spec = pl.BlockSpec((groups, tables, samples, cols), lambda i: (i, 0, 0, 0))
    row_spec = pl.BlockSpec((samples, width), lambda i: (0, i))
    sum_spec = pl.BlockSpec((2 * samples, rank), lambda i: (0, 0))
    ring = pltpu.VMEM((AHEAD + 1, rank, width), up.dtype)
    sems = pltpu.SemaphoreType.DMA((AHEAD + 1,))
    sums, held = pl.pallas_call(
        lambda *refs: project_kernel(steps, *refs),
        grid=(steps,),
        in_specs=[x0_spec, row_spec, FAR, FAR],
        out_specs=[sum_spec, HELD],
        out_shape=[jax.ShapeDtypeStruct((2 * samples, rank), jnp.float32), pltpu.VMEM(down.shape, down.dtype)],
        scratch_shapes=[ring, sems, sems],
        compiler_params=params(14),
        cost_estimate=cost(4 * x0.size * rank, 4 * down.size + 4 * x0.size),
        name="project",
    )(x0, grad, far(down), far(up))
    other = lax.ppermute(sums, "row", [(0, 1), (1, 0)])
    return pl.pallas_call(
        lambda *refs: cross_kernel(steps, *refs),
        grid=(steps,),
        in_specs=[sum_spec, sum_spec, x0_spec, HELD, FAR, pl.BlockSpec((1, width), lambda i: (0, i)), row_spec],
        out_specs=[row_spec, x0_spec],
        out_shape=[pltpu.HBM((samples, owners * tables * cols), jnp.bfloat16), pltpu.HBM(x0.shape, jnp.bfloat16)],
        scratch_shapes=[ring, sems],
        compiler_params=params(20),
        cost_estimate=cost(4 * x0.size * rank, 2 * up.size + 8 * x0.size),
        name="cross",
    )(sums, other, x0, near(held), far(up), bias, grad)


def body(ids, lengths, tables, cross_down, cross_up, bias, grad_out):
    batch, feats, bag = ids.shape
    part, width = tables.shape[1:]
    shards = lax.axis_size("row")
    owners = lax.axis_size("table")
    pair = feats // shards
    shard = lax.axis_index("row").astype(jnp.int32)
    mine = shard.reshape(1)
    swap = [(0, 1), (1, 0)]
    sent = lax.dynamic_slice_in_dim(tables, (1 - shard) * pair, pair, 0)
    other = lax.ppermute(sent, "row", swap)
    counts = count(mine, jnp.transpose(ids, (1, 2, 0)), jnp.transpose(lengths), pair, shards * part)
    pooled, counts = pool(mine, counts, tables, other, owners)
    x0 = lax.all_to_all(pooled, "table", split_axis=0, concat_axis=0, tiled=True)
    crossed, x0_grad = cross_layer(x0, cross_down, cross_up, bias.reshape(1, -1), grad_out)
    back = lax.all_to_all(x0_grad, "table", split_axis=0, concat_axis=0, tiled=True)
    outgoing = scatter(mine, counts, back, shards, True)
    incoming = lax.ppermute(outgoing, "row", swap)
    own = scatter(mine, counts, back, shards, False)
    table_grad = lax.dynamic_update_slice_in_dim(own, incoming, (1 - shard) * pair, 0)
    return (crossed, table_grad)


def solution(mesh):
    in_specs = (
        P(None, "table", None),
        P(None, "table"),
        P("table", "row", None),
        P("row", None),
        P(None, "row"),
        P("row"),
        P("table", "row"),
    )
    out_specs = (P("table", "row"), P("table", "row", None))
    return jax.shard_map(body, mesh=mesh, in_specs=in_specs, out_specs=out_specs, check_vma=False)
```

time: 200 us -> 190 us (0.950)
  Pallas kernels: 67.4 us -> 54.2 us
  waiting for transfers between devices: 1.04 us -> 5.56 us
    pallas_call x4 -> x2, Pallas kernels: 36.3 us -> 27.4 us  [the longest x1 13.8 us: cross_layer(): pl.pallas_call(lambda *refs: cross_kernel(steps, *refs), grid=(steps,), i...]
    ppermute x2 -> x1, waiting for transfers between devices: 0.01 us -> 4.64 us  [cross_layer(): other = lax.ppermute(sums, 'row', [(0, 1), (1, 0)])]
    pallas_call x1, Pallas kernels: 13.5 us -> 9.14 us  [count(): pl.pallas_call(count_kernel, grid_spec=pltpu.PrefetchScalarGridSpec(num_s...]
  transfers between devices with their start and end apart: 4 -> 3, of which waited for: 1 -> 2; matrix products, arithmetic and copies ran while one was open for 0% -> 0% of each run, Pallas kernels for 16% -> 8%
where the time goes in v4:
time: 190 us; the launch traced here: 189 us
  blocking collectives  125 us (66%)
  Pallas kernels  54.2 us (29%)
  waiting for transfers between devices  5.56 us (3%)
  starting transfers between devices  2.61 us (1%)
    all_to_all x1, blocking collectives, body(): lax.all_to_all(pooled, 'table', split_axis=0, concat_axis=0, tiled=True)  65.2 us
    all_to_all x1, blocking collectives, body(): lax.all_to_all(x0_grad, 'table', split_axis=0, concat_axis=0, tiled=True)  59.3 us
    pallas_call x1, Pallas kernels, cross_layer(): pl.pallas_call(lambda *refs: cross_kernel(steps, *refs), grid=(steps,), i...  13.8 us
    pallas_call x1, Pallas kernels, cross_layer(): pl.pallas_call(lambda *refs: project_kernel(steps, *refs), grid=(steps,),...  13.5 us
    pallas_call x2, Pallas kernels, scatter(): pl.pallas_call(scatter_kernel, grid_spec=pltpu.PrefetchScalarGridSpec(num...  11.8 us
    pallas_call x1, Pallas kernels, count(): pl.pallas_call(count_kernel, grid_spec=pltpu.PrefetchScalarGridSpec(num_s...  9.14 us
    pallas_call x1, Pallas kernels, pool(): pl.pallas_call(pool_kernel, grid_spec=pltpu.PrefetchScalarGridSpec(num_sc...  5.87 us
    ppermute x1, waiting for transfers between devices, cross_layer(): other = lax.ppermute(sums, 'row', [(0, 1), (1, 0)])  4.64 us
  transfers between devices with their start and end apart: 3, of which 2 were waited for; matrix products, arithmetic and copies ran while one was open for 0% of the time, Pallas kernels for 8%

profile of v4, /device:TPU:1, one launch (start us, length us, event | category | flops | bytes accessed | tf_op | source)
XLA Modules:
  0.0 189.3 jit_solution(12445103792684169529)
XLA Ops:
  0.6 1.0 constant_dynamic-slice_fusion
  1.6 2.1 %collective-permute-start = (bf16[4,256,128]{2,1,0:T(8,128)(2,1)S(1)}, bf16[4,256,128]{2,1,0:T(8,128)(2,1)S(1)}, u32[]{:S(2)}, u32[]{:S(2)}) collective-permute-start(bf16[4,256,128]{2,1,0:T(8,128)(2,1)S(1)} %constant_dynamic-slice_fusion), channel_id=1, source_target_pairs={{0,1},{1,0},{2,3},{3,2},{4,5},{5,4},{6,7},{7,6},{8,9},{9,8},{10,11... | collective-permute-start | bytes 786440 | tf_op jit(solution)/shard_map/ppermute | solution.py:296
  3.7 0.0 copy-start.1
  3.7 9.1 %count.1.counts_ref = bf16[8,4,512,512]{3,2,1,0:T(8,128)(2,1)S(1)} custom-call(s32[1]{0:T(128)} %bitcast.shard_ref, s32[8,8,4096]{2,1,0:T(8,128)} %bitcast.5, s32[8,4096]{1,0:T(8,128)} %bitcast.6), custom_call_target="tpu_custom_call" | custom-call | flops 67108864 | bytes 1048576 | tf_op jit(solution)/shard_map/count/pallas_call | solution.py:62
  12.9 0.0 collective-permute-done.other_ref
  12.9 0.0 copy-done.1
  12.9 5.9 %pool.1 = (bf16[64,4,64,128]{3,2,1,0:T(8,128)(2,1)S(1)}, bf16[8,4,512,512]{3,2,1,0:T(8,128)(2,1)}) custom-call(s32[1]{0:T(128)} %bitcast.shard_ref, bf16[8,4,512,512]{3,2,1,0:T(8,128)(2,1)S(1)} %count.1.counts_ref, bf16[8,256,128]{2,1,0:T(8,128)(2,1)S(1)} %copy-done.1, bf16[4,256,128]{2,1,0:T(8,128)(2,1)S(1)} %collective-permute-done.other_ref), custom_call_target="tpu_custom_call" | custom-call | flops 2147483648 | bytes 33554432 | tf_op jit(solution)/shard_map/pool/pallas_call | solution.py:113
  18.8 0.0 copy-start
  18.8 65.2 %all_to_all.10.refs_0_.refs_2_ = bf16[64,4,64,128]{3,2,1,0:T(8,128)(2,1)S(1)} all-to-all(bf16[64,4,64,128]{3,2,1,0:T(8,128)(2,1)S(1)} %get-tuple-element.8), channel_id=1, replica_groups=mesh['table'=64,'row'=2] {'table'}, dimensions={0} | all-to-all | bytes 8388608 | tf_op jit(solution)/shard_map/all_to_all | solution.py:299
  84.0 0.0 copy-done
  84.0 0.0 copy-start.2
  84.0 13.5 %project.1 = (f32[128,256]{1,0:T(8,128)S(1)}, bf16[32768,256]{1,0:T(8,128)(2,1)S(1)}) custom-call(bf16[64,4,64,128]{3,2,1,0:T(8,128)(2,1)S(1)} %all_to_all.10.refs_0_.refs_2_, bf16[64,32768]{1,0:T(8,128)(2,1)S(1)} %copy-done, bf16[32768,256]{1,0:T(8,128)(2,1)} %refs_2_.1, bf16[256,32768]{1,0:T(8,128)(2,1)} %refs_4_.1), custom_call_target="tpu_custom_call" | custom-call | flops 2147483648 | bytes 41943040 | tf_op jit(solution)/shard_map/project/pallas_call | solution.py:261
  97.6 0.1 collective-permute-start.1
  97.7 4.6 %collective-permute-done.1.refs_1_ = f32[128,256]{1,0:T(8,128)S(1)} collective-permute-done((f32[128,256]{1,0:T(8,128)S(1)}, f32[128,256]{1,0:T(8,128)S(1)}, u32[]{:S(2)}, u32[]{:S(2)}) %collective-permute-start.1) | collective-permute-done | bytes 131104 | tf_op jit(solution)/shard_map/ppermute | solution.py:272
  102.3 0.0 copy-done.2
  102.3 13.8 %cross.1 = (bf16[64,32768]{1,0:T(8,128)(2,1)}, bf16[64,4,64,128]{3,2,1,0:T(8,128)(2,1)}) custom-call(f32[128,256]{1,0:T(8,128)S(1)} %get-tuple-element.9.refs_0_, f32[128,256]{1,0:T(8,128)S(1)} %collective-permute-done.1.refs_1_, bf16[64,4,64,128]{3,2,1,0:T(8,128)(2,1)S(1)} %all_to_all.10.refs_0_.refs_2_, bf16[32768,256]{1,0:T(8,128)(2,1)S(1)} %get-tuple-element.10.refs_3_, ...), custom_call_target="tpu_custom_call" | custom-call | flops 2147483648 | bytes 33554432 | tf_op jit(solution)/shard_map/cross/pallas_call | solution.py:273
  116.1 59.3 %all_to_all.11.back_ref = bf16[64,4,64,128]{3,2,1,0:T(8,128)(2,1)S(1)} all-to-all(bf16[64,4,64,128]{3,2,1,0:T(8,128)(2,1)} %get-tuple-element.13), channel_id=1, replica_groups=mesh['table'=64,'row'=2] {'table'}, dimensions={0} | all-to-all | bytes 8388608 | tf_op jit(solution)/shard_map/all_to_all | solution.py:301
  175.4 5.6 %scatter.3 = bf16[4,256,128]{2,1,0:T(8,128)(2,1)S(1)} custom-call(s32[1]{0:T(128)} %bitcast.shard_ref, bf16[8,4,512,512]{3,2,1,0:T(8,128)(2,1)} %get-tuple-element.12.counts_ref, bf16[64,4,64,128]{3,2,1,0:T(8,128)(2,1)S(1)} %all_to_all.11.back_ref), custom_call_target="tpu_custom_call" | custom-call | flops 1073741824 | bytes 12582912 | tf_op jit(solution)/shard_map/scatter/pallas_call | solution.py:150
  181.0 0.4 collective-permute-start.2
  181.4 6.2 %scatter.2 = bf16[8,256,128]{2,1,0:T(8,128)(2,1)} custom-call(s32[1]{0:T(128)} %bitcast.shard_ref, bf16[8,4,512,512]{3,2,1,0:T(8,128)(2,1)} %get-tuple-element.12.counts_ref, bf16[64,4,64,128]{3,2,1,0:T(8,128)(2,1)S(1)} %all_to_all.11.back_ref), custom_call_target="tpu_custom_call" | custom-call | flops 1073741824 | bytes 12582912 | tf_op jit(solution)/shard_map/scatter/pallas_call | solution.py:150
  187.6 0.9 collective-permute-done.2
  188.6 0.7 constant_dynamic-update-slice_fusion
Async XLA Ops:
  1.6 11.3 %collective-permute-start = (bf16[4,256,128]{2,1,0:T(8,128)(2,1)S(1)}, bf16[4,256,128]{2,1,0:T(8,128)(2,1)S(1)}, u32[]{:S(2)}, u32[]{:S(2)}) collective-permute-start(bf16[4,256,128]{2,1,0:T(8,128)(2,1)S(1)} %constant_dynamic-slice_fusion), channel_id=1, source_target_pairs={{0,1},{1,0},{2,3},{3,2},{4,5},{5,4},{6,7},{7,6},{8,9},{9,8},{10,11... | collective-permute-start | bytes 786440 | tf_op jit(solution)/shard_map/ppermute | solution.py:296
  3.7 9.2 %copy-start.1 = (bf16[8,256,128]{2,1,0:T(8,128)(2,1)S(1)}, bf16[8,256,128]{2,1,0:T(8,128)(2,1)}, u32[]{:S(2)}) copy-start(bf16[8,256,128]{2,1,0:T(8,128)(2,1)} %own_ref.1) | copy-start | bytes 1572868
  18.8 65.2 %copy-start = (bf16[64,32768]{1,0:T(8,128)(2,1)S(1)}, bf16[64,32768]{1,0:T(8,128)(2,1)}, u32[]{:S(2)}) copy-start(bf16[64,32768]{1,0:T(8,128)(2,1)} %refs_6_.1) | copy-start | bytes 12582916
  84.0 18.3 %copy-start.2 = (f32[32768]{0:T(1024)S(1)}, f32[32768]{0:T(1024)}, u32[]{:S(2)}) copy-start(f32[32768]{0:T(1024)} %param.12) | copy-start | bytes 393220
  97.6 4.7 %collective-permute-start.1 = (f32[128,256]{1,0:T(8,128)S(1)}, f32[128,256]{1,0:T(8,128)S(1)}, u32[]{:S(2)}, u32[]{:S(2)}) collective-permute-start(f32[128,256]{1,0:T(8,128)S(1)} %get-tuple-element.9.refs_0_), channel_id=1, source_target_pairs={{0,1},{1,0},{2,3},{3,2},{4,5},{5,4},{6,7},{7,6},{8,9},{9,8},{10,11... | collective-permute-start | bytes 393224 | tf_op jit(solution)/shard_map/ppermute | solution.py:272
  181.0 7.5 %collective-permute-start.2 = (bf16[4,256,128]{2,1,0:T(8,128)(2,1)S(1)}, bf16[4,256,128]{2,1,0:T(8,128)(2,1)S(1)}, u32[]{:S(2)}, u32[]{:S(2)}) collective-permute-start(bf16[4,256,128]{2,1,0:T(8,128)(2,1)S(1)} %scatter.3), channel_id=1, source_target_pairs={{0,1},{1,0},{2,3},{3,2},{4,5},{5,4},{6,7},{7,6},{8,9},{9,8},{10,11... | collective-permute-start | bytes 786440 | tf_op jit(solution)/shard_map/ppermute | solution.py:303

commit v5 on v4

--- a/solution.py
+++ b/solution.py
@@ -77,18 +77,12 @@
     )(shard, far(ids), far(lengths))
 
 
-def pool_kernel(shard_ref, counts_ref, own_ref, other_ref, pooled_ref, saved_ref, sem):
+def pool_kernel(shard_ref, counts_ref, own_ref, other_ref, pooled_ref):
     part, width = own_ref.shape[1:]
     samples = pooled_ref.shape[2]
     chunk = counts_ref.shape[3]
     blocks = pooled_ref.shape[0] * samples // chunk
     k, step = pl.program_id(0), pl.program_id(1)
-    save = pltpu.make_async_copy(counts_ref, saved_ref, sem)
-
-    @pl.when((k == 0) & (step == 0))
-    def _():
-        save.start()
-
     for c in range(blocks):
         total = jnp.zeros((width, chunk), jnp.float32)
         for place, table_ref in ((shard_ref[0], own_ref), (1 - shard_ref[0], other_ref)):
@@ -99,10 +93,6 @@
             )
         owned = jnp.transpose(total.astype(jnp.bfloat16)).reshape(chunk // samples, samples, width)
         pooled_ref[c * (chunk // samples) : (c + 1) * (chunk // samples), 0] = owned
-
-    @pl.when((k == pl.num_programs(0) - 1) & (step == pl.num_programs(1) - 1))
-    def _():
-        save.wait()
 
 
 def pool(shard, counts, tables, other, owners):
@@ -120,26 +110,23 @@
                 pl.BlockSpec((1, part, width), lambda k, b, s: (s[0] * pair + k, 0, 0)),
                 pl.BlockSpec((1, part, width), lambda k, b, s: (k, 0, 0)),
             ],
-            out_specs=[
-                pl.BlockSpec((owners // steps, 1, batch // owners, width), lambda k, b, s: (b, k, 0, 0)),
-                FAR,
-            ],
-            scratch_shapes=[pltpu.SemaphoreType.DMA],
+            out_specs=pl.BlockSpec((owners // steps, 1, batch // owners, width), lambda k, b, s: (b, k, 0, 0)),
         ),
-        out_shape=[
-            jax.ShapeDtypeStruct((owners, pair, batch // owners, width), jnp.bfloat16),
-            pltpu.HBM(counts.shape, counts.dtype),
-        ],
+        out_shape=jax.ShapeDtypeStruct((owners, pair, batch // owners, width), jnp.bfloat16),
         compiler_params=params(10),
         cost_estimate=cost(2 * counts.size * width, 4 * counts.size),
         name="pool",
     )(shard, near(counts), tables, other)
 
 
-def scatter_kernel(shard_ref, counts_ref, back_ref, grad_ref):
+def scatter_kernel(away, shard_ref, counts_ref, back_ref, grad_ref):
     owners, _, samples, width = back_ref.shape
     back = back_ref[:, 0].reshape(owners * samples, width)
-    counts = jnp.concatenate([counts_ref[c, 0] for c in range(counts_ref.shape[0])], axis=1)
+    part = grad_ref.shape[1]
+    half = 1 - shard_ref[0] if away else shard_ref[0]
+    rows = pl.ds(pl.multiple_of(half * part, part), part)
+    k = pl.program_id(0)
+    counts = jnp.concatenate([counts_ref[c, k, rows, :] for c in range(counts_ref.shape[0])], axis=1)
     grad_ref[0] = jnp.dot(counts, back, preferred_element_type=jnp.float32).astype(jnp.bfloat16)
 
 
@@ -148,12 +135,12 @@
     part = vocab // shards
     owners, _, samples, width = back.shape
     return pl.pallas_call(
-        scatter_kernel,
+        lambda *refs: scatter_kernel(away, *refs),
         grid_spec=pltpu.PrefetchScalarGridSpec(
             num_scalar_prefetch=1,
             grid=(pair,),
             in_specs=[
-                pl.BlockSpec((chunks, 1, part, chunk), lambda k, s: (0, k, 1 - s[0] if away else s[0], 0)),
+                HELD,
                 pl.BlockSpec((owners, 1, samples, width), lambda k, s: (0, k, 0, 0)),
             ],
             out_specs=pl.BlockSpec((1, part, width), lambda k, s: (k if away else s[0] * pair + k, 0, 0)),
@@ -162,7 +149,7 @@
         compiler_params=params(12),
         cost_estimate=cost(2 * counts.size // shards * width, 2 * counts.size // shards + 2 * back.size),
         name="scatter",
-    )(shard, far(counts), back)
+    )(shard, near(counts), back)
 
 
 def row_of(x0_ref):
@@ -170,25 +157,25 @@
     return jnp.concatenate([x0_ref[g, k] for g in range(groups) for k in range(tables)], axis=1)
 
 
-def stream(steps, copies):
+def stream(steps, ahead, copies):
     step = pl.program_id(0)
 
     @pl.when(step == 0)
     def _():
-        for i in range(min(AHEAD, steps)):
+        for i in range(min(ahead, steps)):
             for copy in copies(i):
                 copy.start()
 
-    @pl.when(step + AHEAD < steps)
-    def _():
-        for copy in copies(step + AHEAD):
+    @pl.when(step + ahead < steps)
+    def _():
+        for copy in copies(step + ahead):
             copy.start()
 
     for copy in copies(step):
         copy.wait()
 
 
-def project_kernel(steps, x0_ref, grad_ref, down_ref, up_ref, sums_ref, held_ref, ring_ref, down_sems, up_sems):
+def project_kernel(steps, x0_ref, grad_ref, down_ref, up_ref, sums_ref, rounded_ref, held_ref, ring_ref, down_sems, up_sems):
     samples, width = grad_ref.shape
     step = pl.program_id(0)
     span = lambda i: pl.ds(pl.multiple_of(i * width, width), width)
@@ -202,7 +189,7 @@
 
     x0 = row_of(x0_ref)
     dgate = (grad_ref[...].astype(jnp.float32) * x0.astype(jnp.float32)).astype(jnp.bfloat16)
-    stream(steps, copies)
+    stream(steps, AHEAD, copies)
     low = jnp.dot(x0, held_ref[span(step), :], preferred_element_type=jnp.float32)
     up = ring_ref[lax.rem(step, AHEAD + 1)]
     dlow = lax.dot_general(dgate, up, (((1,), (1,)), ((), ())), preferred_element_type=jnp.float32)
@@ -216,6 +203,10 @@
     def _():
         sums_ref[:samples] += low
         sums_ref[samples:] += dlow
+
+    @pl.when(step == steps - 1)
+    def _():
+        rounded_ref[...] = sums_ref[...].astype(jnp.bfloat16)
 
 
 def cross_kernel(
@@ -227,15 +218,15 @@
     span = lambda i: pl.ds(pl.multiple_of(i * width, width), width)
 
     def copies(i):
-        slot = lax.rem(i, AHEAD + 1)
+        slot = lax.rem(i, 2)
         return (pltpu.make_async_copy(up_ref.at[:, span(i)], ring_ref.at[slot], sems.at[slot]),)
 
-    sums = (mine_ref[...] + other_ref[...]).astype(jnp.bfloat16)
+    sums = (mine_ref[...] + other_ref[...].astype(jnp.float32)).astype(jnp.bfloat16)
     spread = lax.dot_general(
         sums[samples:], down_ref[span(step), :], (((1,), (1,)), ((), ())), preferred_element_type=jnp.float32
     )
-    stream(steps, copies)
-    up = ring_ref[lax.rem(step, AHEAD + 1)]
+    stream(steps, 1, copies)
+    up = ring_ref[lax.rem(step, 2)]
     gate = jnp.dot(sums[:samples], up, preferred_element_type=jnp.float32) + bias_ref[...]
     x0 = row_of(x0_ref).astype(jnp.float32)
     crossed_ref[...] = (x0 * gate + x0).astype(jnp.bfloat16)
@@ -258,26 +249,30 @@
     sum_spec = pl.BlockSpec((2 * samples, rank), lambda i: (0, 0))
     ring = pltpu.VMEM((AHEAD + 1, rank, width), up.dtype)
     sems = pltpu.SemaphoreType.DMA((AHEAD + 1,))
-    sums, held = pl.pallas_call(
+    sums, rounded, held = pl.pallas_call(
         lambda *refs: project_kernel(steps, *refs),
         grid=(steps,),
         in_specs=[x0_spec, row_spec, FAR, FAR],
-        out_specs=[sum_spec, HELD],
-        out_shape=[jax.ShapeDtypeStruct((2 * samples, rank), jnp.float32), pltpu.VMEM(down.shape, down.dtype)],
+        out_specs=[sum_spec, sum_spec, HELD],
+        out_shape=[
+            jax.ShapeDtypeStruct((2 * samples, rank), jnp.float32),
+            jax.ShapeDtypeStruct((2 * samples, rank), jnp.bfloat16),
+            pltpu.VMEM(down.shape, down.dtype),
+        ],
         scratch_shapes=[ring, sems, sems],
-        compiler_params=params(14),
+        compiler_params=params(12),
         cost_estimate=cost(4 * x0.size * rank, 4 * down.size + 4 * x0.size),
         name="project",
     )(x0, grad, far(down), far(up))
-    other = lax.ppermute(sums, "row", [(0, 1), (1, 0)])
+    other = lax.ppermute(rounded, "row", [(0, 1), (1, 0)])
     return pl.pallas_call(
         lambda *refs: cross_kernel(steps, *refs),
         grid=(steps,),
         in_specs=[sum_spec, sum_spec, x0_spec, HELD, FAR, pl.BlockSpec((1, width), lambda i: (0, i)), row_spec],
         out_specs=[row_spec, x0_spec],
         out_shape=[pltpu.HBM((samples, owners * tables * cols), jnp.bfloat16), pltpu.HBM(x0.shape, jnp.bfloat16)],
-        scratch_shapes=[ring, sems],
-        compiler_params=params(20),
+        scratch_shapes=[pltpu.VMEM((2, rank, width), up.dtype), pltpu.SemaphoreType.DMA((2,))],
+        compiler_params=params(16),
         cost_estimate=cost(4 * x0.size * rank, 2 * up.size + 8 * x0.size),
         name="cross",
     )(sums, other, x0, near(held), far(up), bias, grad)
@@ -295,7 +290,7 @@
     sent = lax.dynamic_slice_in_dim(tables, (1 - shard) * pair, pair, 0)
     other = lax.ppermute(sent, "row", swap)
     counts = count(mine, jnp.transpose(ids, (1, 2, 0)), jnp.transpose(lengths), pair, shards * part)
-    pooled, counts = pool(mine, counts, tables, other, owners)
+    pooled = pool(mine, counts, tables, other, owners)
     x0 = lax.all_to_all(pooled, "table", split_axis=0, concat_axis=0, tiled=True)
     crossed, x0_grad = cross_layer(x0, cross_down, cross_up, bias.reshape(1, -1), grad_out)
     back = lax.all_to_all(x0_grad, "table", split_axis=0, concat_axis=0, tiled=True)

time: 190 us -> 185 us (0.974)
  Pallas kernels: 54.2 us -> 48.3 us
    pallas_call x2, Pallas kernels: 11.8 us -> 6.87 us  [scatter(): pl.pallas_call(lambda *refs: scatter_kernel(away, *refs), grid_spec=pltpu...]
    ppermute x1, waiting for transfers between devices: 0.92 us -> 3.48 us  [body(): incoming = lax.ppermute(outgoing, 'row', swap)]
  transfers between devices with their start and end apart: 3 -> 3, of which waited for: 2 -> 2; matrix products, arithmetic and copies ran while one was open for 0% -> 0% of each run, Pallas kernels for 8% -> 7%
where the time goes in v5:
time: 185 us
  blocking collectives  125 us (68%)
  Pallas kernels  48.3 us (26%)
  waiting for transfers between devices  6.58 us (4%)
  starting transfers between devices  2.51 us (1%)
    all_to_all x1, blocking collectives, body(): lax.all_to_all(pooled, 'table', split_axis=0, concat_axis=0, tiled=True)  65.2 us
    all_to_all x1, blocking collectives, body(): lax.all_to_all(x0_grad, 'table', split_axis=0, concat_axis=0, tiled=True)  59.6 us
    pallas_call x1, Pallas kernels, cross_layer(): pl.pallas_call(lambda *refs: cross_kernel(steps, *refs), grid=(steps,), i...  14 us
    pallas_call x1, Pallas kernels, cross_layer(): pl.pallas_call(lambda *refs: project_kernel(steps, *refs), grid=(steps,),...  13.6 us
    pallas_call x1, Pallas kernels, count(): pl.pallas_call(count_kernel, grid_spec=pltpu.PrefetchScalarGridSpec(num_s...  9.14 us
    pallas_call x2, Pallas kernels, scatter(): pl.pallas_call(lambda *refs: scatter_kernel(away, *refs), grid_spec=pltpu...  6.87 us
    pallas_call x1, Pallas kernels, pool(): pl.pallas_call(pool_kernel, grid_spec=pltpu.PrefetchScalarGridSpec(num_sc...  4.67 us
  transfers between devices with their start and end apart: 3, of which 2 were waited for; matrix products, arithmetic and copies ran while one was open for 0% of the time, Pallas kernels for 7%

profile of v5, /device:TPU:1, one launch (start us, length us, event | category | flops | bytes accessed | tf_op | source)
XLA Modules:
  0.0 184.6 jit_solution(10357346448774054338)
XLA Ops:
  0.6 1.0 constant_dynamic-slice_fusion
  1.6 2.1 %collective-permute-start = (bf16[4,256,128]{2,1,0:T(8,128)(2,1)S(1)}, bf16[4,256,128]{2,1,0:T(8,128)(2,1)S(1)}, u32[]{:S(2)}, u32[]{:S(2)}) collective-permute-start(bf16[4,256,128]{2,1,0:T(8,128)(2,1)S(1)} %constant_dynamic-slice_fusion), channel_id=1, source_target_pairs={{0,1},{1,0},{2,3},{3,2},{4,5},{5,4},{6,7},{7,6},{8,9},{9,8},{10,11... | collective-permute-start | bytes 786440 | tf_op jit(solution)/shard_map/ppermute | solution.py:291
  3.7 0.0 copy-start.1
  3.7 9.1 %count.1.counts_ref.refs_1_ = bf16[8,4,512,512]{3,2,1,0:T(8,128)(2,1)S(1)} custom-call(s32[1]{0:T(128)} %bitcast.shard_ref.refs_0_, s32[8,8,4096]{2,1,0:T(8,128)} %bitcast.5, s32[8,4096]{1,0:T(8,128)} %bitcast.6), custom_call_target="tpu_custom_call" | custom-call | flops 67108864 | bytes 1048576 | tf_op jit(solution)/shard_map/count/pallas_call | solution.py:62
  12.9 0.0 collective-permute-done.other_ref
  12.9 0.0 copy-done.1
  12.9 4.7 %pool.1 = bf16[64,4,64,128]{3,2,1,0:T(8,128)(2,1)S(1)} custom-call(s32[1]{0:T(128)} %bitcast.shard_ref.refs_0_, bf16[8,4,512,512]{3,2,1,0:T(8,128)(2,1)S(1)} %count.1.counts_ref.refs_1_, bf16[8,256,128]{2,1,0:T(8,128)(2,1)S(1)} %copy-done.1, bf16[4,256,128]{2,1,0:T(8,128)(2,1)S(1)} %collective-permute-done.other_ref), custom_call_target="tpu_custom_call" | custom-call | flops 2147483648 | bytes 33554432 | tf_op jit(solution)/shard_map/pool/pallas_call | solution.py:103
  17.6 0.0 copy-start
  17.6 65.2 %all_to_all.10.refs_0_.refs_2_ = bf16[64,4,64,128]{3,2,1,0:T(8,128)(2,1)S(1)} all-to-all(bf16[64,4,64,128]{3,2,1,0:T(8,128)(2,1)S(1)} %pool.1), channel_id=1, replica_groups=mesh['table'=64,'row'=2] {'table'}, dimensions={0} | all-to-all | bytes 8388608 | tf_op jit(solution)/shard_map/all_to_all | solution.py:294
  82.8 0.0 copy-done
  82.8 0.0 copy-start.2
  82.8 13.6 %project.1 = (f32[128,256]{1,0:T(8,128)S(1)}, bf16[128,256]{1,0:T(8,128)(2,1)S(1)}, bf16[32768,256]{1,0:T(8,128)(2,1)S(1)}) custom-call(bf16[64,4,64,128]{3,2,1,0:T(8,128)(2,1)S(1)} %all_to_all.10.refs_0_.refs_2_, bf16[64,32768]{1,0:T(8,128)(2,1)S(1)} %copy-done, bf16[32768,256]{1,0:T(8,128)(2,1)} %refs_2_.1, bf16[256,32768]{1,0:T(8,128)(2,1)} %refs_4_.1), custom_call_target="tpu_custom_call" | custom-call | flops 2147483648 | bytes 41943040 | tf_op jit(solution)/shard_map/project/pallas_call | solution.py:252
  96.4 0.1 collective-permute-start.1
  96.5 3.1 %collective-permute-done.1.refs_1_ = bf16[128,256]{1,0:T(8,128)(2,1)S(1)} collective-permute-done((bf16[128,256]{1,0:T(8,128)(2,1)S(1)}, bf16[128,256]{1,0:T(8,128)(2,1)S(1)}, u32[]{:S(2)}, u32[]{:S(2)}) %collective-permute-start.1) | collective-permute-done | bytes 65568 | tf_op jit(solution)/shard_map/ppermute | solution.py:267
  99.6 0.0 copy-done.2
  99.6 14.0 %cross.1 = (bf16[64,32768]{1,0:T(8,128)(2,1)}, bf16[64,4,64,128]{3,2,1,0:T(8,128)(2,1)}) custom-call(f32[128,256]{1,0:T(8,128)S(1)} %get-tuple-element.7.refs_0_, bf16[128,256]{1,0:T(8,128)(2,1)S(1)} %collective-permute-done.1.refs_1_, bf16[64,4,64,128]{3,2,1,0:T(8,128)(2,1)S(1)} %all_to_all.10.refs_0_.refs_2_, ...), custom_call_target="tpu_custom_call" | custom-call | flops 2147483648 | bytes 33554432 | tf_op jit(solution)/shard_map/cross/pallas_call | solution.py:268
  113.6 59.6 %all_to_all.11.refs_2_ = bf16[64,4,64,128]{3,2,1,0:T(8,128)(2,1)S(1)} all-to-all(bf16[64,4,64,128]{3,2,1,0:T(8,128)(2,1)} %get-tuple-element.11), channel_id=1, replica_groups=mesh['table'=64,'row'=2] {'table'}, dimensions={0} | all-to-all | bytes 8388608 | tf_op jit(solution)/shard_map/all_to_all | solution.py:296
  173.2 3.1 %scatter.3 = bf16[4,256,128]{2,1,0:T(8,128)(2,1)S(1)} custom-call(s32[1]{0:T(128)} %bitcast.shard_ref.refs_0_, bf16[8,4,512,512]{3,2,1,0:T(8,128)(2,1)S(1)} %count.1.counts_ref.refs_1_, bf16[64,4,64,128]{3,2,1,0:T(8,128)(2,1)S(1)} %all_to_all.11.refs_2_), custom_call_target="tpu_custom_call" | custom-call | flops 1073741824 | bytes 12582912 | tf_op jit(solution)/shard_map/scatter/pallas_call | solution.py:137
  176.3 0.3 collective-permute-start.2
  176.6 3.8 %scatter.2 = bf16[8,256,128]{2,1,0:T(8,128)(2,1)} custom-call(s32[1]{0:T(128)} %bitcast.shard_ref.refs_0_, bf16[8,4,512,512]{3,2,1,0:T(8,128)(2,1)S(1)} %count.1.counts_ref.refs_1_, bf16[64,4,64,128]{3,2,1,0:T(8,128)(2,1)S(1)} %all_to_all.11.refs_2_), custom_call_target="tpu_custom_call" | custom-call | flops 1073741824 | bytes 12582912 | tf_op jit(solution)/shard_map/scatter/pallas_call | solution.py:137
  180.4 3.5 %collective-permute-done.2 = bf16[4,256,128]{2,1,0:T(8,128)(2,1)S(1)} collective-permute-done((bf16[4,256,128]{2,1,0:T(8,128)(2,1)S(1)}, bf16[4,256,128]{2,1,0:T(8,128)(2,1)S(1)}, u32[]{:S(2)}, u32[]{:S(2)}) %collective-permute-start.2) | collective-permute-done | bytes 262176 | tf_op jit(solution)/shard_map/ppermute | solution.py:298
  183.9 0.7 constant_dynamic-update-slice_fusion
Async XLA Ops:
  1.6 11.3 %collective-permute-start = (bf16[4,256,128]{2,1,0:T(8,128)(2,1)S(1)}, bf16[4,256,128]{2,1,0:T(8,128)(2,1)S(1)}, u32[]{:S(2)}, u32[]{:S(2)}) collective-permute-start(bf16[4,256,128]{2,1,0:T(8,128)(2,1)S(1)} %constant_dynamic-slice_fusion), channel_id=1, source_target_pairs={{0,1},{1,0},{2,3},{3,2},{4,5},{5,4},{6,7},{7,6},{8,9},{9,8},{10,11... | collective-permute-start | bytes 786440 | tf_op jit(solution)/shard_map/ppermute | solution.py:291
  3.7 9.2 %copy-start.1 = (bf16[8,256,128]{2,1,0:T(8,128)(2,1)S(1)}, bf16[8,256,128]{2,1,0:T(8,128)(2,1)}, u32[]{:S(2)}) copy-start(bf16[8,256,128]{2,1,0:T(8,128)(2,1)} %own_ref.1) | copy-start | bytes 1572868
  17.6 65.2 %copy-start = (bf16[64,32768]{1,0:T(8,128)(2,1)S(1)}, bf16[64,32768]{1,0:T(8,128)(2,1)}, u32[]{:S(2)}) copy-start(bf16[64,32768]{1,0:T(8,128)(2,1)} %refs_6_.1) | copy-start | bytes 12582916
  82.8 16.8 %copy-start.2 = (f32[32768]{0:T(1024)S(1)}, f32[32768]{0:T(1024)}, u32[]{:S(2)}) copy-start(f32[32768]{0:T(1024)} %param.12) | copy-start | bytes 393220
  96.4 3.2 %collective-permute-start.1 = (bf16[128,256]{1,0:T(8,128)(2,1)S(1)}, bf16[128,256]{1,0:T(8,128)(2,1)S(1)}, u32[]{:S(2)}, u32[]{:S(2)}) collective-permute-start(bf16[128,256]{1,0:T(8,128)(2,1)S(1)} %get-tuple-element.8), channel_id=1, source_target_pairs={{0,1},{1,0},{2,3},{3,2},{4,5},{5,4},{6,7},{7,6},{8,9},{9,8},{10,11... | collective-permute-start | bytes 196616 | tf_op jit(solution)/shard_map/ppermute | solution.py:267
  176.3 7.5 %collective-permute-start.2 = (bf16[4,256,128]{2,1,0:T(8,128)(2,1)S(1)}, bf16[4,256,128]{2,1,0:T(8,128)(2,1)S(1)}, u32[]{:S(2)}, u32[]{:S(2)}) collective-permute-start(bf16[4,256,128]{2,1,0:T(8,128)(2,1)S(1)} %scatter.3), channel_id=1, source_target_pairs={{0,1},{1,0},{2,3},{3,2},{4,5},{5,4},{6,7},{7,6},{8,9},{9,8},{10,11... | collective-permute-start | bytes 786440 | tf_op jit(solution)/shard_map/ppermute | solution.py:298

commit v6 on v5

--- a/solution.py
+++ b/solution.py
@@ -119,42 +119,43 @@
     )(shard, near(counts), tables, other)
 
 
-def scatter_kernel(away, shard_ref, counts_ref, back_ref, grad_ref):
+def scatter_kernel(first, away, shard_ref, counts_ref, back_ref, grad_ref):
     owners, _, samples, width = back_ref.shape
     back = back_ref[:, 0].reshape(owners * samples, width)
     part = grad_ref.shape[1]
     half = 1 - shard_ref[0] if away else shard_ref[0]
     rows = pl.ds(pl.multiple_of(half * part, part), part)
-    k = pl.program_id(0)
+    k = first + pl.program_id(0)
     counts = jnp.concatenate([counts_ref[c, k, rows, :] for c in range(counts_ref.shape[0])], axis=1)
     grad_ref[0] = jnp.dot(counts, back, preferred_element_type=jnp.float32).astype(jnp.bfloat16)
 
 
-def scatter(shard, counts, back, shards, away):
+def scatter(shard, counts, back, shards, first, last, away):
     chunks, pair, vocab, chunk = counts.shape
     part = vocab // shards
     owners, _, samples, width = back.shape
     return pl.pallas_call(
-        lambda *refs: scatter_kernel(away, *refs),
+        lambda *refs: scatter_kernel(first, away, *refs),
         grid_spec=pltpu.PrefetchScalarGridSpec(
             num_scalar_prefetch=1,
-            grid=(pair,),
+            grid=(last - first,),
             in_specs=[
                 HELD,
-                pl.BlockSpec((owners, 1, samples, width), lambda k, s: (0, k, 0, 0)),
+                pl.BlockSpec((owners, 1, samples, width), lambda k, s: (0, first + k, 0, 0)),
             ],
-            out_specs=pl.BlockSpec((1, part, width), lambda k, s: (k if away else s[0] * pair + k, 0, 0)),
+            out_specs=pl.BlockSpec((1, part, width), lambda k, s: (k if away else s[0] * pair + first + k, 0, 0)),
         ),
-        out_shape=jax.ShapeDtypeStruct((pair if away else shards * pair, part, width), jnp.bfloat16),
+        out_shape=jax.ShapeDtypeStruct((last - first if away else shards * pair, part, width), jnp.bfloat16),
         compiler_params=params(12),
         cost_estimate=cost(2 * counts.size // shards * width, 2 * counts.size // shards + 2 * back.size),
         name="scatter",
     )(shard, near(counts), back)
 
 
-def row_of(x0_ref):
-    groups, tables = x0_ref.shape[:2]
-    return jnp.concatenate([x0_ref[g, k] for g in range(groups) for k in range(tables)], axis=1)
+def row_of(x0_ref, groups):
+    first = pl.program_id(0) * groups
+    tables = x0_ref.shape[1]
+    return jnp.concatenate([x0_ref[first + g, k] for g in range(groups) for k in range(tables)], axis=1)
 
 
 def stream(steps, ahead, copies):
@@ -175,8 +176,9 @@
         copy.wait()
 
 
-def project_kernel(steps, x0_ref, grad_ref, down_ref, up_ref, sums_ref, rounded_ref, held_ref, ring_ref, down_sems, up_sems):
-    samples, width = grad_ref.shape
+def project_kernel(steps, x0_ref, grad_ref, down_ref, up_ref, sums_ref, held_ref, ring_ref, down_sems, up_sems):
+    samples = grad_ref.shape[0]
+    width = grad_ref.shape[1] // steps
     step = pl.program_id(0)
     span = lambda i: pl.ds(pl.multiple_of(i * width, width), width)
 
@@ -187,8 +189,8 @@
             pltpu.make_async_copy(up_ref.at[:, span(i)], ring_ref.at[slot], up_sems.at[slot]),
         )
 
-    x0 = row_of(x0_ref)
-    dgate = (grad_ref[...].astype(jnp.float32) * x0.astype(jnp.float32)).astype(jnp.bfloat16)
+    x0 = row_of(x0_ref, x0_ref.shape[0] // steps)
+    dgate = (grad_ref[:, span(step)].astype(jnp.float32) * x0.astype(jnp.float32)).astype(jnp.bfloat16)
     stream(steps, AHEAD, copies)
     low = jnp.dot(x0, held_ref[span(step), :], preferred_element_type=jnp.float32)
     up = ring_ref[lax.rem(step, AHEAD + 1)]
@@ -204,15 +206,11 @@
         sums_ref[:samples] += low
         sums_ref[samples:] += dlow
 
-    @pl.when(step == steps - 1)
-    def _():
-        rounded_ref[...] = sums_ref[...].astype(jnp.bfloat16)
-
 
 def cross_kernel(
     steps, mine_ref, other_ref, x0_ref, down_ref, up_ref, bias_ref, grad_ref, crossed_ref, back_ref, ring_ref, sems
 ):
-    groups, tables, samples, cols = x0_ref.shape
+    groups, tables, samples, cols = back_ref.shape
     width = groups * tables * cols
     step = pl.program_id(0)
     span = lambda i: pl.ds(pl.multiple_of(i * width, width), width)
@@ -221,16 +219,16 @@
         slot = lax.rem(i, 2)
         return (pltpu.make_async_copy(up_ref.at[:, span(i)], ring_ref.at[slot], sems.at[slot]),)
 
-    sums = (mine_ref[...] + other_ref[...].astype(jnp.float32)).astype(jnp.bfloat16)
+    sums = (mine_ref[...] + other_ref[...]).astype(jnp.bfloat16)
     spread = lax.dot_general(
         sums[samples:], down_ref[span(step), :], (((1,), (1,)), ((), ())), preferred_element_type=jnp.float32
     )
     stream(steps, 1, copies)
     up = ring_ref[lax.rem(step, 2)]
     gate = jnp.dot(sums[:samples], up, preferred_element_type=jnp.float32) + bias_ref[...]
-    x0 = row_of(x0_ref).astype(jnp.float32)
+    x0 = row_of(x0_ref, groups).astype(jnp.float32)
     crossed_ref[...] = (x0 * gate + x0).astype(jnp.bfloat16)
-    upstream = grad_ref[...].astype(jnp.float32)
+    upstream = grad_ref[:, span(step)].astype(jnp.float32)
     back = (upstream * gate + upstream + spread).astype(jnp.bfloat16)
     for g in range(groups):
         for k in range(tables):
@@ -249,33 +247,29 @@
     sum_spec = pl.BlockSpec((2 * samples, rank), lambda i: (0, 0))
     ring = pltpu.VMEM((AHEAD + 1, rank, width), up.dtype)
     sems = pltpu.SemaphoreType.DMA((AHEAD + 1,))
-    sums, rounded, held = pl.pallas_call(
+    sums, held = pl.pallas_call(
         lambda *refs: project_kernel(steps, *refs),
         grid=(steps,),
-        in_specs=[x0_spec, row_spec, FAR, FAR],
-        out_specs=[sum_spec, sum_spec, HELD],
-        out_shape=[
-            jax.ShapeDtypeStruct((2 * samples, rank), jnp.float32),
-            jax.ShapeDtypeStruct((2 * samples, rank), jnp.bfloat16),
-            pltpu.VMEM(down.shape, down.dtype),
-        ],
+        in_specs=[HELD, HELD, FAR, FAR],
+        out_specs=[sum_spec, HELD],
+        out_shape=[jax.ShapeDtypeStruct((2 * samples, rank), jnp.float32), pltpu.VMEM(down.shape, down.dtype)],
         scratch_shapes=[ring, sems, sems],
         compiler_params=params(12),
         cost_estimate=cost(4 * x0.size * rank, 4 * down.size + 4 * x0.size),
         name="project",
-    )(x0, grad, far(down), far(up))
-    other = lax.ppermute(rounded, "row", [(0, 1), (1, 0)])
+    )(near(x0), near(grad), far(down), far(up))
+    other = lax.ppermute(sums, "row", [(0, 1), (1, 0)])
     return pl.pallas_call(
         lambda *refs: cross_kernel(steps, *refs),
         grid=(steps,),
-        in_specs=[sum_spec, sum_spec, x0_spec, HELD, FAR, pl.BlockSpec((1, width), lambda i: (0, i)), row_spec],
+        in_specs=[sum_spec, sum_spec, HELD, HELD, FAR, pl.BlockSpec((1, width), lambda i: (0, i)), HELD],
         out_specs=[row_spec, x0_spec],
         out_shape=[pltpu.HBM((samples, owners * tables * cols), jnp.bfloat16), pltpu.HBM(x0.shape, jnp.bfloat16)],
         scratch_shapes=[pltpu.VMEM((2, rank, width), up.dtype), pltpu.SemaphoreType.DMA((2,))],
         compiler_params=params(16),
         cost_estimate=cost(4 * x0.size * rank, 2 * up.size + 8 * x0.size),
         name="cross",
-    )(sums, other, x0, near(held), far(up), bias, grad)
+    )(sums, other, near(x0), near(held), far(up), bias, near(grad))
 
 
 def body(ids, lengths, tables, cross_down, cross_up, bias, grad_out):
@@ -294,10 +288,14 @@
     x0 = lax.all_to_all(pooled, "table", split_axis=0, concat_axis=0, tiled=True)
     crossed, x0_grad = cross_layer(x0, cross_down, cross_up, bias.reshape(1, -1), grad_out)
     back = lax.all_to_all(x0_grad, "table", split_axis=0, concat_axis=0, tiled=True)
-    outgoing = scatter(mine, counts, back, shards, True)
-    incoming = lax.ppermute(outgoing, "row", swap)
-    own = scatter(mine, counts, back, shards, False)
-    table_grad = lax.dynamic_update_slice_in_dim(own, incoming, (1 - shard) * pair, 0)
+    cuts = [0, pair // 2, pair]
+    incoming = []
+    for first, last in zip(cuts, cuts[1:]):
+        outgoing = scatter(mine, counts, back, shards, first, last, True)
+        incoming.append(lax.ppermute(outgoing, "row", swap))
+    table_grad = scatter(mine, counts, back, shards, 0, pair, False)
+    incoming = jnp.concatenate(incoming, axis=0)
+    table_grad = lax.dynamic_update_slice_in_dim(table_grad, incoming, (1 - shard) * pair, 0)
     return (crossed, table_grad)
 
 

time: 185 us -> 184 us (level)
    ppermute x2 -> x3, waiting for transfers between devices: 6.58 us -> 5.25 us  [the longest x1 4.64 us: cross_layer(): other = lax.ppermute(sums, 'row', [(0, 1), (1, 0)])]
    pallas_call x2 -> x3, Pallas kernels: 6.87 us -> 6.9 us  [scatter(): pl.pallas_call(lambda *refs: scatter_kernel(first, away, *refs), grid_spe...]
  transfers between devices with their start and end apart: 3 -> 4, of which waited for: 2 -> 2; matrix products, arithmetic and copies ran while one was open for 0% -> 0% of each run, Pallas kernels for 7% -> 8%
where the time goes in v6:
time: 184 us; the launch traced here: 183 us
  blocking collectives  125 us (68%)
  Pallas kernels  47.3 us (26%)
  waiting for transfers between devices  5.26 us (3%)
  starting transfers between devices  3.83 us (2%)
    all_to_all x1, blocking collectives, body(): lax.all_to_all(pooled, 'table', split_axis=0, concat_axis=0, tiled=True)  65.2 us
    all_to_all x1, blocking collectives, body(): lax.all_to_all(x0_grad, 'table', split_axis=0, concat_axis=0, tiled=True)  59.3 us
    pallas_call x1, Pallas kernels, cross_layer(): pl.pallas_call(lambda *refs: cross_kernel(steps, *refs), grid=(steps,), i...  13.8 us
    pallas_call x1, Pallas kernels, cross_layer(): pl.pallas_call(lambda *refs: project_kernel(steps, *refs), grid=(steps,),...  12.8 us
    pallas_call x1, Pallas kernels, count(): pl.pallas_call(count_kernel, grid_spec=pltpu.PrefetchScalarGridSpec(num_s...  9.14 us
    pallas_call x3, Pallas kernels, scatter(): pl.pallas_call(lambda *refs: scatter_kernel(first, away, *refs), grid_spe...  6.9 us
    pallas_call x1, Pallas kernels, pool(): pl.pallas_call(pool_kernel, grid_spec=pltpu.PrefetchScalarGridSpec(num_sc...  4.67 us
    ppermute x1, waiting for transfers between devices, cross_layer(): other = lax.ppermute(sums, 'row', [(0, 1), (1, 0)])  4.64 us
  transfers between devices with their start and end apart: 4, of which 2 were waited for; matrix products, arithmetic and copies ran while one was open for 0% of the time, Pallas kernels for 8%

profile of v6, /device:TPU:1, one launch (start us, length us, event | category | flops | bytes accessed | tf_op | source)
XLA Modules:
  0.0 183.3 jit_solution(10622552310951260490)
XLA Ops:
  0.6 1.0 constant_dynamic-slice_fusion
  1.6 2.1 %collective-permute-start = (bf16[4,256,128]{2,1,0:T(8,128)(2,1)S(1)}, bf16[4,256,128]{2,1,0:T(8,128)(2,1)S(1)}, u32[]{:S(2)}, u32[]{:S(2)}) collective-permute-start(bf16[4,256,128]{2,1,0:T(8,128)(2,1)S(1)} %constant_dynamic-slice_fusion), channel_id=1, source_target_pairs={{0,1},{1,0},{2,3},{3,2},{4,5},{5,4},{6,7},{7,6},{8,9},{9,8},{10,11... | collective-permute-start | bytes 786440 | tf_op jit(solution)/shard_map/ppermute | solution.py:285
  3.7 0.0 copy-start.1
  3.7 9.1 %count.1.counts_ref.refs_1_ = bf16[8,4,512,512]{3,2,1,0:T(8,128)(2,1)S(1)} custom-call(s32[1]{0:T(128)} %bitcast.shard_ref.refs_0_, s32[8,8,4096]{2,1,0:T(8,128)} %bitcast.5, s32[8,4096]{1,0:T(8,128)} %bitcast.6), custom_call_target="tpu_custom_call" | custom-call | flops 67108864 | bytes 1048576 | tf_op jit(solution)/shard_map/count/pallas_call | solution.py:62
  12.9 0.0 collective-permute-done.other_ref
  12.9 0.0 copy-done.1
  12.9 4.7 %pool.1 = bf16[64,4,64,128]{3,2,1,0:T(8,128)(2,1)S(1)} custom-call(s32[1]{0:T(128)} %bitcast.shard_ref.refs_0_, bf16[8,4,512,512]{3,2,1,0:T(8,128)(2,1)S(1)} %count.1.counts_ref.refs_1_, bf16[8,256,128]{2,1,0:T(8,128)(2,1)S(1)} %copy-done.1, bf16[4,256,128]{2,1,0:T(8,128)(2,1)S(1)} %collective-permute-done.other_ref), custom_call_target="tpu_custom_call" | custom-call | flops 2147483648 | bytes 33554432 | tf_op jit(solution)/shard_map/pool/pallas_call | solution.py:103
  17.6 0.0 copy-start
  17.6 65.2 %all_to_all.10.refs_0_.refs_2_ = bf16[64,4,64,128]{3,2,1,0:T(8,128)(2,1)S(1)} all-to-all(bf16[64,4,64,128]{3,2,1,0:T(8,128)(2,1)S(1)} %pool.1), channel_id=1, replica_groups=mesh['table'=64,'row'=2] {'table'}, dimensions={0} | all-to-all | bytes 8388608 | tf_op jit(solution)/shard_map/all_to_all | solution.py:288
  82.8 0.0 copy-done
  82.8 0.0 copy-start.2
  82.8 12.8 %project.1 = (f32[128,256]{1,0:T(8,128)S(1)}, bf16[32768,256]{1,0:T(8,128)(2,1)S(1)}) custom-call(bf16[64,4,64,128]{3,2,1,0:T(8,128)(2,1)S(1)} %all_to_all.10.refs_0_.refs_2_, bf16[64,32768]{1,0:T(8,128)(2,1)S(1)} %copy-done, bf16[32768,256]{1,0:T(8,128)(2,1)} %refs_2_.1, bf16[256,32768]{1,0:T(8,128)(2,1)} %refs_4_.1), custom_call_target="tpu_custom_call" | custom-call | flops 2147483648 | bytes 41943040 | tf_op jit(solution)/shard_map/project/pallas_call | solution.py:250
  95.6 0.1 collective-permute-start.1
  95.7 4.6 %collective-permute-done.1.refs_1_ = f32[128,256]{1,0:T(8,128)S(1)} collective-permute-done((f32[128,256]{1,0:T(8,128)S(1)}, f32[128,256]{1,0:T(8,128)S(1)}, u32[]{:S(2)}, u32[]{:S(2)}) %collective-permute-start.1) | collective-permute-done | bytes 131104 | tf_op jit(solution)/shard_map/ppermute | solution.py:261
  100.3 0.0 copy-done.2
  100.3 13.8 %cross.1 = (bf16[64,32768]{1,0:T(8,128)(2,1)}, bf16[64,4,64,128]{3,2,1,0:T(8,128)(2,1)}) custom-call(f32[128,256]{1,0:T(8,128)S(1)} %get-tuple-element.6.refs_0_, f32[128,256]{1,0:T(8,128)S(1)} %collective-permute-done.1.refs_1_, bf16[64,4,64,128]{3,2,1,0:T(8,128)(2,1)S(1)} %all_to_all.10.refs_0_.refs_2_, bf16[32768,256]{1,0:T(8,128)(2,1)S(1)} %get-tuple-element.7.refs_3_, ...), custom_call_target="tpu_custom_call" | custom-call | flops 2147483648 | bytes 33554432 | tf_op jit(solution)/shard_map/cross/pallas_call | solution.py:262
  114.1 59.3 %all_to_all.11.refs_2_ = bf16[64,4,64,128]{3,2,1,0:T(8,128)(2,1)S(1)} all-to-all(bf16[64,4,64,128]{3,2,1,0:T(8,128)(2,1)} %get-tuple-element.9), channel_id=1, replica_groups=mesh['table'=64,'row'=2] {'table'}, dimensions={0} | all-to-all | bytes 8388608 | tf_op jit(solution)/shard_map/all_to_all | solution.py:290
  173.5 1.6 scatter.4
  175.0 0.4 collective-permute-start.2
  175.4 1.6 scatter.5
  177.0 1.2 collective-permute-start.3
  178.2 3.8 %scatter.3 = bf16[8,256,128]{2,1,0:T(8,128)(2,1)} custom-call(s32[1]{0:T(128)} %bitcast.shard_ref.refs_0_, bf16[8,4,512,512]{3,2,1,0:T(8,128)(2,1)S(1)} %count.1.counts_ref.refs_1_, bf16[64,4,64,128]{3,2,1,0:T(8,128)(2,1)S(1)} %all_to_all.11.refs_2_), custom_call_target="tpu_custom_call" | custom-call | flops 1073741824 | bytes 12582912 | tf_op jit(solution)/shard_map/scatter/pallas_call | solution.py:137
  182.0 0.0 collective-permute-done.2
  182.0 0.6 collective-permute-done.3
  182.6 0.7 maximum_dynamic-update-slice_fusion
Async XLA Ops:
  1.6 11.3 %collective-permute-start = (bf16[4,256,128]{2,1,0:T(8,128)(2,1)S(1)}, bf16[4,256,128]{2,1,0:T(8,128)(2,1)S(1)}, u32[]{:S(2)}, u32[]{:S(2)}) collective-permute-start(bf16[4,256,128]{2,1,0:T(8,128)(2,1)S(1)} %constant_dynamic-slice_fusion), channel_id=1, source_target_pairs={{0,1},{1,0},{2,3},{3,2},{4,5},{5,4},{6,7},{7,6},{8,9},{9,8},{10,11... | collective-permute-start | bytes 786440 | tf_op jit(solution)/shard_map/ppermute | solution.py:285
  3.7 9.2 %copy-start.1 = (bf16[8,256,128]{2,1,0:T(8,128)(2,1)S(1)}, bf16[8,256,128]{2,1,0:T(8,128)(2,1)}, u32[]{:S(2)}) copy-start(bf16[8,256,128]{2,1,0:T(8,128)(2,1)} %own_ref.1) | copy-start | bytes 1572868
  17.6 65.2 %copy-start = (bf16[64,32768]{1,0:T(8,128)(2,1)S(1)}, bf16[64,32768]{1,0:T(8,128)(2,1)}, u32[]{:S(2)}) copy-start(bf16[64,32768]{1,0:T(8,128)(2,1)} %refs_6_.1) | copy-start | bytes 12582916
  82.8 17.5 %copy-start.2 = (f32[32768]{0:T(1024)S(1)}, f32[32768]{0:T(1024)}, u32[]{:S(2)}) copy-start(f32[32768]{0:T(1024)} %param.12) | copy-start | bytes 393220
  95.6 4.7 %collective-permute-start.1 = (f32[128,256]{1,0:T(8,128)S(1)}, f32[128,256]{1,0:T(8,128)S(1)}, u32[]{:S(2)}, u32[]{:S(2)}) collective-permute-start(f32[128,256]{1,0:T(8,128)S(1)} %get-tuple-element.6.refs_0_), channel_id=1, source_target_pairs={{0,1},{1,0},{2,3},{3,2},{4,5},{5,4},{6,7},{7,6},{8,9},{9,8},{10,11... | collective-permute-start | bytes 393224 | tf_op jit(solution)/shard_map/ppermute | solution.py:261
  175.0 7.0 %collective-permute-start.2 = (bf16[2,256,128]{2,1,0:T(8,128)(2,1)S(1)}, bf16[2,256,128]{2,1,0:T(8,128)(2,1)S(1)}, u32[]{:S(2)}, u32[]{:S(2)}) collective-permute-start(bf16[2,256,128]{2,1,0:T(8,128)(2,1)S(1)} %scatter.4), channel_id=1, source_target_pairs={{0,1},{1,0},{2,3},{3,2},{4,5},{5,4},{6,7},{7,6},{8,9},{9,8},{10,11... | collective-permute-start | bytes 393224 | tf_op jit(solution)/shard_map/ppermute | solution.py:295
  177.0 5.6 %collective-permute-start.3 = (bf16[2,256,128]{2,1,0:T(8,128)(2,1)S(1)}, bf16[2,256,128]{2,1,0:T(8,128)(2,1)S(1)}, u32[]{:S(2)}, u32[]{:S(2)}) collective-permute-start(bf16[2,256,128]{2,1,0:T(8,128)(2,1)S(1)} %scatter.5), channel_id=1, source_target_pairs={{0,1},{1,0},{2,3},{3,2},{4,5},{5,4},{6,7},{7,6},{8,9},{9,8},{10,11... | collective-permute-start | bytes 393224 | tf_op jit(solution)/shard_map/ppermute | solution.py:295

commit v7 on v6

--- a/solution.py
+++ b/solution.py
@@ -9,7 +9,7 @@
 BITS = 4
 LANES = 128
 MIB = 1 << 20
-AHEAD = 3
+AHEAD = 2
 HELD = pl.BlockSpec(memory_space=pltpu.VMEM)
 FAR = pl.BlockSpec(memory_space=pl.ANY)
 
@@ -71,18 +71,24 @@
             out_specs=HELD,
         ),
         out_shape=pltpu.VMEM((batch // chunk, tables, vocab, chunk), jnp.bfloat16),
-        compiler_params=params(8),
+        compiler_params=params(14),
         cost_estimate=cost(tables * vocab * bag * batch, 4 * ids.size),
         name="count",
     )(shard, far(ids), far(lengths))
 
 
-def pool_kernel(shard_ref, counts_ref, own_ref, other_ref, pooled_ref):
+def pool_kernel(shard_ref, counts_ref, own_ref, other_ref, weight_ref, pooled_ref, held_ref, sem):
     part, width = own_ref.shape[1:]
     samples = pooled_ref.shape[2]
     chunk = counts_ref.shape[3]
     blocks = pooled_ref.shape[0] * samples // chunk
     k, step = pl.program_id(0), pl.program_id(1)
+    fetch = pltpu.make_async_copy(weight_ref.at[: held_ref.shape[0]], held_ref, sem)
+
+    @pl.when((k == 0) & (step == 0))
+    def _():
+        fetch.start()
+
     for c in range(blocks):
         total = jnp.zeros((width, chunk), jnp.float32)
         for place, table_ref in ((shard_ref[0], own_ref), (1 - shard_ref[0], other_ref)):
@@ -94,8 +100,12 @@
         owned = jnp.transpose(total.astype(jnp.bfloat16)).reshape(chunk // samples, samples, width)
         pooled_ref[c * (chunk // samples) : (c + 1) * (chunk // samples), 0] = owned
 
-
-def pool(shard, counts, tables, other, owners):
+    @pl.when((k == pl.num_programs(0) - 1) & (step == pl.num_programs(1) - 1))
+    def _():
+        fetch.wait()
+
+
+def pool(shard, counts, tables, other, weight, owners):
     chunks, pair, vocab, chunk = counts.shape
     batch = chunks * chunk
     part, width = tables.shape[1:]
@@ -109,14 +119,22 @@
                 HELD,
                 pl.BlockSpec((1, part, width), lambda k, b, s: (s[0] * pair + k, 0, 0)),
                 pl.BlockSpec((1, part, width), lambda k, b, s: (k, 0, 0)),
+                FAR,
             ],
-            out_specs=pl.BlockSpec((owners // steps, 1, batch // owners, width), lambda k, b, s: (b, k, 0, 0)),
+            out_specs=[
+                pl.BlockSpec((owners // steps, 1, batch // owners, width), lambda k, b, s: (b, k, 0, 0)),
+                HELD,
+            ],
+            scratch_shapes=[pltpu.SemaphoreType.DMA],
         ),
-        out_shape=jax.ShapeDtypeStruct((owners, pair, batch // owners, width), jnp.bfloat16),
-        compiler_params=params(10),
+        out_shape=[
+            jax.ShapeDtypeStruct((owners, pair, batch // owners, width), jnp.bfloat16),
+            pltpu.VMEM((weight.shape[0] // 2, weight.shape[1]), weight.dtype),
+        ],
+        compiler_params=params(14),
         cost_estimate=cost(2 * counts.size * width, 4 * counts.size),
         name="pool",
-    )(shard, near(counts), tables, other)
+    )(shard, near(counts), tables, other, far(weight))
 
 
 def scatter_kernel(first, away, shard_ref, counts_ref, back_ref, grad_ref):
@@ -176,39 +194,68 @@
         copy.wait()
 
 
-def project_kernel(steps, x0_ref, grad_ref, down_ref, up_ref, sums_ref, held_ref, ring_ref, down_sems, up_sems):
+def in_halves(steps, work, first_ref, second_ref):
+    step = pl.program_id(0)
+    half = steps // 2
+    rows = first_ref.shape[0] // half
+
+    @pl.when(step < half)
+    def _():
+        work(first_ref.at[pl.ds(pl.multiple_of(step * rows, rows), rows)])
+
+    @pl.when(step >= half)
+    def _():
+        work(second_ref.at[pl.ds(pl.multiple_of((step - half) * rows, rows), rows)])
+
+
+def project_kernel(
+    steps, x0_ref, grad_ref, first_ref, down_ref, up_ref, sums_ref, second_ref, ring_ref, down_sems, sems
+):
     samples = grad_ref.shape[0]
     width = grad_ref.shape[1] // steps
+    half = steps // 2
     step = pl.program_id(0)
     span = lambda i: pl.ds(pl.multiple_of(i * width, width), width)
 
     def copies(i):
         slot = lax.rem(i, AHEAD + 1)
-        return (
-            pltpu.make_async_copy(down_ref.at[span(i), :], held_ref.at[span(i), :], down_sems.at[slot]),
-            pltpu.make_async_copy(up_ref.at[:, span(i)], ring_ref.at[slot], up_sems.at[slot]),
-        )
-
-    x0 = row_of(x0_ref, x0_ref.shape[0] // steps)
-    dgate = (grad_ref[:, span(step)].astype(jnp.float32) * x0.astype(jnp.float32)).astype(jnp.bfloat16)
+        return (pltpu.make_async_copy(up_ref.at[:, span(i)], ring_ref.at[slot], sems.at[slot]),)
+
+    def second(i):
+        return pltpu.make_async_copy(down_ref.at[span(half + i), :], second_ref.at[span(i), :], down_sems.at[i])
+
     stream(steps, AHEAD, copies)
-    low = jnp.dot(x0, held_ref[span(step), :], preferred_element_type=jnp.float32)
-    up = ring_ref[lax.rem(step, AHEAD + 1)]
-    dlow = lax.dot_general(dgate, up, (((1,), (1,)), ((), ())), preferred_element_type=jnp.float32)
-
-    @pl.when(step == 0)
-    def _():
-        sums_ref[:samples] = low
-        sums_ref[samples:] = dlow
-
-    @pl.when(step > 0)
-    def _():
-        sums_ref[:samples] += low
-        sums_ref[samples:] += dlow
+
+    @pl.when(step < half)
+    def _():
+        second(step).start()
+
+    @pl.when(step >= half)
+    def _():
+        second(step - half).wait()
+
+    def work(weight_ref):
+        x0 = row_of(x0_ref, x0_ref.shape[0] // steps)
+        dgate = (grad_ref[:, span(step)].astype(jnp.float32) * x0.astype(jnp.float32)).astype(jnp.bfloat16)
+        low = jnp.dot(x0, weight_ref[...], preferred_element_type=jnp.float32)
+        up = ring_ref[lax.rem(step, AHEAD + 1)]
+        dlow = lax.dot_general(dgate, up, (((1,), (1,)), ((), ())), preferred_element_type=jnp.float32)
+
+        @pl.when(step == 0)
+        def _():
+            sums_ref[:samples] = low
+            sums_ref[samples:] = dlow
+
+        @pl.when(step > 0)
+        def _():
+            sums_ref[:samples] += low
+            sums_ref[samples:] += dlow
+
+    in_halves(steps, work, first_ref, second_ref)
 
 
 def cross_kernel(
-    steps, mine_ref, other_ref, x0_ref, down_ref, up_ref, bias_ref, grad_ref, crossed_ref, back_ref, ring_ref, sems
+    steps, mine_ref, other_ref, x0_ref, first_ref, second_ref, up_ref, bias_ref, grad_ref, crossed_ref, back_ref, ring_ref, sems
 ):
     groups, tables, samples, cols = back_ref.shape
     width = groups * tables * cols
@@ -219,24 +266,28 @@
         slot = lax.rem(i, 2)
         return (pltpu.make_async_copy(up_ref.at[:, span(i)], ring_ref.at[slot], sems.at[slot]),)
 
-    sums = (mine_ref[...] + other_ref[...]).astype(jnp.bfloat16)
-    spread = lax.dot_general(
-        sums[samples:], down_ref[span(step), :], (((1,), (1,)), ((), ())), preferred_element_type=jnp.float32
-    )
-    stream(steps, 1, copies)
-    up = ring_ref[lax.rem(step, 2)]
-    gate = jnp.dot(sums[:samples], up, preferred_element_type=jnp.float32) + bias_ref[...]
-    x0 = row_of(x0_ref, groups).astype(jnp.float32)
-    crossed_ref[...] = (x0 * gate + x0).astype(jnp.bfloat16)
-    upstream = grad_ref[:, span(step)].astype(jnp.float32)
-    back = (upstream * gate + upstream + spread).astype(jnp.bfloat16)
-    for g in range(groups):
-        for k in range(tables):
-            at = (g * tables + k) * cols
-            back_ref[g, k] = back[:, at : at + cols]
-
-
-def cross_layer(x0, down, up, bias, grad):
+    def work(weight_ref):
+        sums = (mine_ref[...] + other_ref[...]).astype(jnp.bfloat16)
+        spread = lax.dot_general(
+            sums[samples:], weight_ref[...], (((1,), (1,)), ((), ())), preferred_element_type=jnp.float32
+        )
+        stream(steps, 1, copies)
+        up = ring_ref[lax.rem(step, 2)]
+        gate = jnp.dot(sums[:samples], up, preferred_element_type=jnp.float32)
+        scale = gate + (bias_ref[...] + 1.0)
+        x0 = row_of(x0_ref, groups).astype(jnp.float32)
+        crossed_ref[...] = (x0 * scale).astype(jnp.bfloat16)
+        upstream = grad_ref[:, span(step)].astype(jnp.float32)
+        back = (upstream * scale + spread).astype(jnp.bfloat16)
+        for g in range(groups):
+            for k in range(tables):
+                at = (g * tables + k) * cols
+                back_ref[g, k] = back[:, at : at + cols]
+
+    in_halves(steps, work, first_ref, second_ref)
+
+
+def cross_layer(x0, first, down, up, bias, grad):
     owners, tables, samples, cols = x0.shape
     rank = down.shape[1]
     groups = 8
@@ -247,29 +298,29 @@
     sum_spec = pl.BlockSpec((2 * samples, rank), lambda i: (0, 0))
     ring = pltpu.VMEM((AHEAD + 1, rank, width), up.dtype)
     sems = pltpu.SemaphoreType.DMA((AHEAD + 1,))
-    sums, held = pl.pallas_call(
+    sums, second = pl.pallas_call(
         lambda *refs: project_kernel(steps, *refs),
         grid=(steps,),
-        in_specs=[HELD, HELD, FAR, FAR],
+        in_specs=[HELD, HELD, HELD, FAR, FAR],
         out_specs=[sum_spec, HELD],
-        out_shape=[jax.ShapeDtypeStruct((2 * samples, rank), jnp.float32), pltpu.VMEM(down.shape, down.dtype)],
-        scratch_shapes=[ring, sems, sems],
-        compiler_params=params(12),
-        cost_estimate=cost(4 * x0.size * rank, 4 * down.size + 4 * x0.size),
+        out_shape=[jax.ShapeDtypeStruct((2 * samples, rank), jnp.float32), pltpu.VMEM(first.shape, first.dtype)],
+        scratch_shapes=[ring, pltpu.SemaphoreType.DMA((steps // 2,)), sems],
+        compiler_params=params(14),
+        cost_estimate=cost(4 * x0.size * rank, 2 * up.size + 4 * x0.size),
         name="project",
-    )(near(x0), near(grad), far(down), far(up))
+    )(near(x0), near(grad), near(first), far(down), far(up))
     other = lax.ppermute(sums, "row", [(0, 1), (1, 0)])
     return pl.pallas_call(
         lambda *refs: cross_kernel(steps, *refs),
         grid=(steps,),
-        in_specs=[sum_spec, sum_spec, HELD, HELD, FAR, pl.BlockSpec((1, width), lambda i: (0, i)), HELD],
+        in_specs=[sum_spec, sum_spec, HELD, HELD, HELD, FAR, pl.BlockSpec((1, width), lambda i: (0, i)), HELD],
         out_specs=[row_spec, x0_spec],
         out_shape=[pltpu.HBM((samples, owners * tables * cols), jnp.bfloat16), pltpu.HBM(x0.shape, jnp.bfloat16)],
         scratch_shapes=[pltpu.VMEM((2, rank, width), up.dtype), pltpu.SemaphoreType.DMA((2,))],
-        compiler_params=params(16),
+        compiler_params=params(14),
         cost_estimate=cost(4 * x0.size * rank, 2 * up.size + 8 * x0.size),
         name="cross",
-    )(sums, other, near(x0), near(held), far(up), bias, near(grad))
+    )(sums, other, near(x0), near(first), near(second), far(up), bias, near(grad))
 
 
 def body(ids, lengths, tables, cross_down, cross_up, bias, grad_out):
@@ -283,10 +334,11 @@
     swap = [(0, 1), (1, 0)]
     sent = lax.dynamic_slice_in_dim(tables, (1 - shard) * pair, pair, 0)
     other = lax.ppermute(sent, "row", swap)
-    counts = count(mine, jnp.transpose(ids, (1, 2, 0)), jnp.transpose(lengths), pair, shards * part)
-    pooled = pool(mine, counts, tables, other, owners)
+    ids, lengths = jnp.transpose(ids, (1, 2, 0)), jnp.transpose(lengths)
+    counts = count(mine, ids, lengths, pair, shards * part)
+    pooled, first = pool(mine, counts, tables, other, cross_down, owners)
     x0 = lax.all_to_all(pooled, "table", split_axis=0, concat_axis=0, tiled=True)
-    crossed, x0_grad = cross_layer(x0, cross_down, cross_up, bias.reshape(1, -1), grad_out)
+    crossed, x0_grad = cross_layer(x0, first, cross_down, cross_up, bias.reshape(1, -1), grad_out)
     back = lax.all_to_all(x0_grad, "table", split_axis=0, concat_axis=0, tiled=True)
     cuts = [0, pair // 2, pair]
     incoming = []

time: 184 us -> 182 us (0.989)
    pallas_call x1, Pallas kernels: 12.8 us -> 10.9 us  [cross_layer(): pl.pallas_call(lambda *refs: project_kernel(steps, *refs), grid=(steps,),...]
where the time goes in v7:
time: 182 us
  blocking collectives  125 us (69%)
  Pallas kernels  45.5 us (25%)
  waiting for transfers between devices  5.21 us (3%)
  starting transfers between devices  3.83 us (2%)
    all_to_all x1, blocking collectives, body(): lax.all_to_all(pooled, 'table', split_axis=0, concat_axis=0, tiled=True)  65.2 us
    all_to_all x1, blocking collectives, body(): lax.all_to_all(x0_grad, 'table', split_axis=0, concat_axis=0, tiled=True)  59.3 us
    pallas_call x1, Pallas kernels, cross_layer(): pl.pallas_call(lambda *refs: cross_kernel(steps, *refs), grid=(steps,), i...  13.7 us
    pallas_call x1, Pallas kernels, cross_layer(): pl.pallas_call(lambda *refs: project_kernel(steps, *refs), grid=(steps,),...  10.9 us
    pallas_call x1, Pallas kernels, count(): pl.pallas_call(count_kernel, grid_spec=pltpu.PrefetchScalarGridSpec(num_s...  9.14 us
    pallas_call x3, Pallas kernels, scatter(): pl.pallas_call(lambda *refs: scatter_kernel(first, away, *refs), grid_spe...  7.02 us
    pallas_call x1, Pallas kernels, pool(): pl.pallas_call(pool_kernel, grid_spec=pltpu.PrefetchScalarGridSpec(num_sc...  4.79 us
    ppermute x1, waiting for transfers between devices, cross_layer(): other = lax.ppermute(sums, 'row', [(0, 1), (1, 0)])  4.64 us
  transfers between devices with their start and end apart: 4, of which 2 were waited for; matrix products, arithmetic and copies ran while one was open for 0% of the time, Pallas kernels for 8%

profile of v7, /device:TPU:1, one launch (start us, length us, event | category | flops | bytes accessed | tf_op | source)
XLA Modules:
  0.0 181.5 jit_solution(2961161474215865087)
XLA Ops:
  0.6 1.0 constant_dynamic-slice_fusion
  1.6 2.1 %collective-permute-start = (bf16[4,256,128]{2,1,0:T(8,128)(2,1)S(1)}, bf16[4,256,128]{2,1,0:T(8,128)(2,1)S(1)}, u32[]{:S(2)}, u32[]{:S(2)}) collective-permute-start(bf16[4,256,128]{2,1,0:T(8,128)(2,1)S(1)} %constant_dynamic-slice_fusion), channel_id=1, source_target_pairs={{0,1},{1,0},{2,3},{3,2},{4,5},{5,4},{6,7},{7,6},{8,9},{9,8},{10,11... | collective-permute-start | bytes 786440 | tf_op jit(solution)/shard_map/ppermute | solution.py:336
  3.7 0.0 copy-start.1
  3.7 9.1 %count.1.counts_ref.refs_1_ = bf16[8,4,512,512]{3,2,1,0:T(8,128)(2,1)S(1)} custom-call(s32[1]{0:T(128)} %bitcast.shard_ref.refs_0_, s32[8,8,4096]{2,1,0:T(8,128)} %bitcast.5, s32[8,4096]{1,0:T(8,128)} %bitcast.6), custom_call_target="tpu_custom_call" | custom-call | flops 67108864 | bytes 1048576 | tf_op jit(solution)/shard_map/count/pallas_call | solution.py:62
  12.9 0.0 collective-permute-done.other_ref
  12.9 0.0 copy-done.1
  12.9 4.8 %pool.1 = (bf16[64,4,64,128]{3,2,1,0:T(8,128)(2,1)S(1)}, bf16[16384,256]{1,0:T(8,128)(2,1)S(1)}) custom-call(s32[1]{0:T(128)} %bitcast.shard_ref.refs_0_, bf16[8,4,512,512]{3,2,1,0:T(8,128)(2,1)S(1)} %count.1.counts_ref.refs_1_, bf16[8,256,128]{2,1,0:T(8,128)(2,1)S(1)} %copy-done.1, bf16[4,256,128]{2,1,0:T(8,128)(2,1)S(1)} %collective-permute-done.other_ref, ...), custom_call_target="tpu_custom_call" | custom-call | flops 2147483648 | bytes 33554432 | tf_op jit(solution)/shard_map/pool/pallas_call | solution.py:113
  17.7 0.0 copy-start
  17.7 65.2 %all_to_all.10.refs_0_.refs_2_ = bf16[64,4,64,128]{3,2,1,0:T(8,128)(2,1)S(1)} all-to-all(bf16[64,4,64,128]{3,2,1,0:T(8,128)(2,1)S(1)} %get-tuple-element.8), channel_id=1, replica_groups=mesh['table'=64,'row'=2] {'table'}, dimensions={0} | all-to-all | bytes 8388608 | tf_op jit(solution)/shard_map/all_to_all | solution.py:340
  82.9 0.0 copy-done
  82.9 0.0 copy-start.2
  82.9 10.9 %project.1 = (f32[128,256]{1,0:T(8,128)S(1)}, bf16[16384,256]{1,0:T(8,128)(2,1)S(1)}) custom-call(bf16[64,4,64,128]{3,2,1,0:T(8,128)(2,1)S(1)} %all_to_all.10.refs_0_.refs_2_, bf16[64,32768]{1,0:T(8,128)(2,1)S(1)} %copy-done, bf16[16384,256]{1,0:T(8,128)(2,1)S(1)} %get-tuple-element.9.refs_2_.refs_3_, bf16[32768,256]{1,0:T(8,128)(2,1)} %refs_3_.1, ...), custom_call_target="tpu_custom_call" | custom-call | flops 2147483648 | bytes 25165824 | tf_op jit(solution)/shard_map/project/pallas_call | solution.py:301
  93.8 0.1 collective-permute-start.1
  93.9 4.6 %collective-permute-done.1.refs_1_ = f32[128,256]{1,0:T(8,128)S(1)} collective-permute-done((f32[128,256]{1,0:T(8,128)S(1)}, f32[128,256]{1,0:T(8,128)S(1)}, u32[]{:S(2)}, u32[]{:S(2)}) %collective-permute-start.1) | collective-permute-done | bytes 131104 | tf_op jit(solution)/shard_map/ppermute | solution.py:312
  98.5 0.0 copy-done.2
  98.5 13.7 %cross.1 = (bf16[64,32768]{1,0:T(8,128)(2,1)}, bf16[64,4,64,128]{3,2,1,0:T(8,128)(2,1)}) custom-call(f32[128,256]{1,0:T(8,128)S(1)} %get-tuple-element.10.refs_0_, f32[128,256]{1,0:T(8,128)S(1)} %collective-permute-done.1.refs_1_, bf16[64,4,64,128]{3,2,1,0:T(8,128)(2,1)S(1)} %all_to_all.10.refs_0_.refs_2_, ...), custom_call_target="tpu_custom_call" | custom-call | flops 2147483648 | bytes 33554432 | tf_op jit(solution)/shard_map/cross/pallas_call | solution.py:313
  112.2 59.3 %all_to_all.11.refs_2_ = bf16[64,4,64,128]{3,2,1,0:T(8,128)(2,1)S(1)} all-to-all(bf16[64,4,64,128]{3,2,1,0:T(8,128)(2,1)} %get-tuple-element.13), channel_id=1, replica_groups=mesh['table'=64,'row'=2] {'table'}, dimensions={0} | all-to-all | bytes 8388608 | tf_op jit(solution)/shard_map/all_to_all | solution.py:342
  171.6 1.6 scatter.4
  173.2 0.4 collective-permute-start.2
  173.6 1.6 scatter.5
  175.2 1.2 collective-permute-start.3
  176.4 3.8 %scatter.3 = bf16[8,256,128]{2,1,0:T(8,128)(2,1)} custom-call(s32[1]{0:T(128)} %bitcast.shard_ref.refs_0_, bf16[8,4,512,512]{3,2,1,0:T(8,128)(2,1)S(1)} %count.1.counts_ref.refs_1_, bf16[64,4,64,128]{3,2,1,0:T(8,128)(2,1)S(1)} %all_to_all.11.refs_2_), custom_call_target="tpu_custom_call" | custom-call | flops 1073741824 | bytes 12582912 | tf_op jit(solution)/shard_map/scatter/pallas_call | solution.py:155
  180.2 0.0 collective-permute-done.2
  180.2 0.6 collective-permute-done.3
  180.8 0.7 maximum_dynamic-update-slice_fusion
Async XLA Ops:
  1.6 11.3 %collective-permute-start = (bf16[4,256,128]{2,1,0:T(8,128)(2,1)S(1)}, bf16[4,256,128]{2,1,0:T(8,128)(2,1)S(1)}, u32[]{:S(2)}, u32[]{:S(2)}) collective-permute-start(bf16[4,256,128]{2,1,0:T(8,128)(2,1)S(1)} %constant_dynamic-slice_fusion), channel_id=1, source_target_pairs={{0,1},{1,0},{2,3},{3,2},{4,5},{5,4},{6,7},{7,6},{8,9},{9,8},{10,11... | collective-permute-start | bytes 786440 | tf_op jit(solution)/shard_map/ppermute | solution.py:336
  3.7 9.2 %copy-start.1 = (bf16[8,256,128]{2,1,0:T(8,128)(2,1)S(1)}, bf16[8,256,128]{2,1,0:T(8,128)(2,1)}, u32[]{:S(2)}) copy-start(bf16[8,256,128]{2,1,0:T(8,128)(2,1)} %own_ref.1) | copy-start | bytes 1572868
  17.7 65.2 %copy-start = (bf16[64,32768]{1,0:T(8,128)(2,1)S(1)}, bf16[64,32768]{1,0:T(8,128)(2,1)}, u32[]{:S(2)}) copy-start(bf16[64,32768]{1,0:T(8,128)(2,1)} %refs_7_.1) | copy-start | bytes 12582916
  82.9 15.6 %copy-start.2 = (f32[32768]{0:T(1024)S(1)}, f32[32768]{0:T(1024)}, u32[]{:S(2)}) copy-start(f32[32768]{0:T(1024)} %param.12) | copy-start | bytes 393220
  93.8 4.7 %collective-permute-start.1 = (f32[128,256]{1,0:T(8,128)S(1)}, f32[128,256]{1,0:T(8,128)S(1)}, u32[]{:S(2)}, u32[]{:S(2)}) collective-permute-start(f32[128,256]{1,0:T(8,128)S(1)} %get-tuple-element.10.refs_0_), channel_id=1, source_target_pairs={{0,1},{1,0},{2,3},{3,2},{4,5},{5,4},{6,7},{7,6},{8,9},{9,8},{10,11... | collective-permute-start | bytes 393224 | tf_op jit(solution)/shard_map/ppermute | solution.py:312
  173.2 7.1 %collective-permute-start.2 = (bf16[2,256,128]{2,1,0:T(8,128)(2,1)S(1)}, bf16[2,256,128]{2,1,0:T(8,128)(2,1)S(1)}, u32[]{:S(2)}, u32[]{:S(2)}) collective-permute-start(bf16[2,256,128]{2,1,0:T(8,128)(2,1)S(1)} %scatter.4), channel_id=1, source_target_pairs={{0,1},{1,0},{2,3},{3,2},{4,5},{5,4},{6,7},{7,6},{8,9},{9,8},{10,11... | collective-permute-start | bytes 393224 | tf_op jit(solution)/shard_map/ppermute | solution.py:347
  175.2 5.6 %collective-permute-start.3 = (bf16[2,256,128]{2,1,0:T(8,128)(2,1)S(1)}, bf16[2,256,128]{2,1,0:T(8,128)(2,1)S(1)}, u32[]{:S(2)}, u32[]{:S(2)}) collective-permute-start(bf16[2,256,128]{2,1,0:T(8,128)(2,1)S(1)} %scatter.5), channel_id=1, source_target_pairs={{0,1},{1,0},{2,3},{3,2},{4,5},{5,4},{6,7},{7,6},{8,9},{9,8},{10,11... | collective-permute-start | bytes 393224 | tf_op jit(solution)/shard_map/ppermute | solution.py:347

commit v8 on v7

--- a/solution.py
+++ b/solution.py
@@ -10,6 +10,8 @@
 LANES = 128
 MIB = 1 << 20
 AHEAD = 2
+STEPS = 8
+EARLY = 2
 HELD = pl.BlockSpec(memory_space=pltpu.VMEM)
 FAR = pl.BlockSpec(memory_space=pl.ANY)
 
@@ -77,17 +79,21 @@
     )(shard, far(ids), far(lengths))
 
 
-def pool_kernel(shard_ref, counts_ref, own_ref, other_ref, weight_ref, pooled_ref, held_ref, sem):
+def pool_kernel(shard_ref, counts_ref, own_ref, other_ref, down_ref, up_ref, pooled_ref, first_ref, lead_ref, sems):
     part, width = own_ref.shape[1:]
     samples = pooled_ref.shape[2]
     chunk = counts_ref.shape[3]
     blocks = pooled_ref.shape[0] * samples // chunk
     k, step = pl.program_id(0), pl.program_id(1)
-    fetch = pltpu.make_async_copy(weight_ref.at[: held_ref.shape[0]], held_ref, sem)
+    fetches = [
+        pltpu.make_async_copy(down_ref.at[: first_ref.shape[0]], first_ref, sems.at[0]),
+        pltpu.make_async_copy(up_ref.at[:, : lead_ref.shape[1]], lead_ref, sems.at[1]),
+    ]
 
     @pl.when((k == 0) & (step == 0))
     def _():
-        fetch.start()
+        for fetch in fetches:
+            fetch.start()
 
     for c in range(blocks):
         total = jnp.zeros((width, chunk), jnp.float32)
@@ -102,14 +108,15 @@
 
     @pl.when((k == pl.num_programs(0) - 1) & (step == pl.num_programs(1) - 1))
     def _():
-        fetch.wait()
-
-
-def pool(shard, counts, tables, other, weight, owners):
+        for fetch in fetches:
+            fetch.wait()
+
+
+def pool(shard, counts, tables, other, down, up, owners):
     chunks, pair, vocab, chunk = counts.shape
     batch = chunks * chunk
     part, width = tables.shape[1:]
-    steps = 2
+    steps = 1
     return pl.pallas_call(
         pool_kernel,
         grid_spec=pltpu.PrefetchScalarGridSpec(
@@ -120,21 +127,24 @@
                 pl.BlockSpec((1, part, width), lambda k, b, s: (s[0] * pair + k, 0, 0)),
                 pl.BlockSpec((1, part, width), lambda k, b, s: (k, 0, 0)),
                 FAR,
+                FAR,
             ],
             out_specs=[
                 pl.BlockSpec((owners // steps, 1, batch // owners, width), lambda k, b, s: (b, k, 0, 0)),
                 HELD,
+                HELD,
             ],
-            scratch_shapes=[pltpu.SemaphoreType.DMA],
+            scratch_shapes=[pltpu.SemaphoreType.DMA((2,))],
         ),
         out_shape=[
             jax.ShapeDtypeStruct((owners, pair, batch // owners, width), jnp.bfloat16),
-            pltpu.VMEM((weight.shape[0] // 2, weight.shape[1]), weight.dtype),
+            pltpu.VMEM((down.shape[0] // STEPS * EARLY, down.shape[1]), down.dtype),
+            pltpu.VMEM((up.shape[0], up.shape[1] // STEPS), up.dtype),
         ],
         compiler_params=params(14),
         cost_estimate=cost(2 * counts.size * width, 4 * counts.size),
         name="pool",
-    )(shard, near(counts), tables, other, far(weight))
+    )(shard, near(counts), tables, other, far(down), far(up))
 
 
 def scatter_kernel(first, away, shard_ref, counts_ref, back_ref, grad_ref):
@@ -176,70 +186,77 @@
     return jnp.concatenate([x0_ref[first + g, k] for g in range(groups) for k in range(tables)], axis=1)
 
 
-def stream(steps, ahead, copies):
+def stream(steps, ahead, copy):
     step = pl.program_id(0)
 
     @pl.when(step == 0)
     def _():
-        for i in range(min(ahead, steps)):
-            for copy in copies(i):
-                copy.start()
-
-    @pl.when(step + ahead < steps)
-    def _():
-        for copy in copies(step + ahead):
-            copy.start()
-
-    for copy in copies(step):
-        copy.wait()
-
-
-def in_halves(steps, work, first_ref, second_ref):
-    step = pl.program_id(0)
-    half = steps // 2
-    rows = first_ref.shape[0] // half
-
-    @pl.when(step < half)
-    def _():
-        work(first_ref.at[pl.ds(pl.multiple_of(step * rows, rows), rows)])
-
-    @pl.when(step >= half)
-    def _():
-        work(second_ref.at[pl.ds(pl.multiple_of((step - half) * rows, rows), rows)])
+        for i in range(1, min(ahead + 1, steps)):
+            copy(i).start()
+
+    @pl.when((step > 0) & (step + ahead < steps))
+    def _():
+        copy(step + ahead).start()
+
+    @pl.when(step > 0)
+    def _():
+        copy(step).wait()
+
+
+def in_parts(steps, work, first_ref, second_ref, lead_ref, piece_ref):
+    step = pl.program_id(0)
+    rows = first_ref.shape[0] // EARLY
+
+    @pl.when(step == 0)
+    def _():
+        work(first_ref.at[:rows], lead_ref)
+
+    @pl.when((step > 0) & (step < EARLY))
+    def _():
+        work(first_ref.at[pl.ds(pl.multiple_of(step * rows, rows), rows)], piece_ref)
+
+    @pl.when(step >= EARLY)
+    def _():
+        work(second_ref.at[pl.ds(pl.multiple_of((step - EARLY) * rows, rows), rows)], piece_ref)
 
 
 def project_kernel(
-    steps, x0_ref, grad_ref, first_ref, down_ref, up_ref, sums_ref, second_ref, ring_ref, down_sems, sems
+    steps, x0_ref, grad_ref, first_ref, lead_ref, down_ref, up_ref, sums_ref, second_ref, ring_ref, down_sems, sems
 ):
     samples = grad_ref.shape[0]
     width = grad_ref.shape[1] // steps
-    half = steps // 2
     step = pl.program_id(0)
     span = lambda i: pl.ds(pl.multiple_of(i * width, width), width)
 
-    def copies(i):
+    def copy(i):
         slot = lax.rem(i, AHEAD + 1)
-        return (pltpu.make_async_copy(up_ref.at[:, span(i)], ring_ref.at[slot], sems.at[slot]),)
+        return pltpu.make_async_copy(up_ref.at[:, span(i)], ring_ref.at[slot], sems.at[slot])
 
     def second(i):
-        return pltpu.make_async_copy(down_ref.at[span(half + i), :], second_ref.at[span(i), :], down_sems.at[i])
-
-    stream(steps, AHEAD, copies)
-
-    @pl.when(step < half)
-    def _():
-        second(step).start()
-
-    @pl.when(step >= half)
-    def _():
-        second(step - half).wait()
-
-    def work(weight_ref):
+        return pltpu.make_async_copy(down_ref.at[span(EARLY + i), :], second_ref.at[span(i), :], down_sems.at[i])
+
+    stream(steps, AHEAD, copy)
+
+    @pl.when(step == 0)
+    def _():
+        for i in range(min(EARLY, steps - EARLY)):
+            second(i).start()
+
+    @pl.when((step > 0) & (step + EARLY - 1 < steps - EARLY))
+    def _():
+        second(step + EARLY - 1).start()
+
+    @pl.when(step >= EARLY)
+    def _():
+        second(step - EARLY).wait()
+
+    def work(down_part, up_part):
         x0 = row_of(x0_ref, x0_ref.shape[0] // steps)
-        dgate = (grad_ref[:, span(step)].astype(jnp.float32) * x0.astype(jnp.float32)).astype(jnp.bfloat16)
-        low = jnp.dot(x0, weight_ref[...], preferred_element_type=jnp.float32)
-        up = ring_ref[lax.rem(step, AHEAD + 1)]
-        dlow = lax.dot_general(dgate, up, (((1,), (1,)), ((), ())), preferred_element_type=jnp.float32)
+        dgate = grad_ref[:, span(step)] * x0
+        low = jnp.dot(x0, down_part[...], preferred_element_type=jnp.float32)
+        dlow = lax.dot_general(
+            dgate, up_part[...], (((1,), (1,)), ((), ())), preferred_element_type=jnp.float32
+        )
 
         @pl.when(step == 0)
         def _():
@@ -251,29 +268,27 @@
             sums_ref[:samples] += low
             sums_ref[samples:] += dlow
 
-    in_halves(steps, work, first_ref, second_ref)
+    in_parts(steps, work, first_ref, second_ref, lead_ref, ring_ref.at[lax.rem(step, AHEAD + 1)])
 
 
 def cross_kernel(
-    steps, mine_ref, other_ref, x0_ref, first_ref, second_ref, up_ref, bias_ref, grad_ref, crossed_ref, back_ref, ring_ref, sems
+    steps, mine_ref, other_ref, x0_ref, first_ref, second_ref, lead_ref, up_ref, bias_ref, grad_ref, crossed_ref, back_ref, ring_ref, sems
 ):
     groups, tables, samples, cols = back_ref.shape
     width = groups * tables * cols
     step = pl.program_id(0)
     span = lambda i: pl.ds(pl.multiple_of(i * width, width), width)
 
-    def copies(i):
+    def copy(i):
         slot = lax.rem(i, 2)
-        return (pltpu.make_async_copy(up_ref.at[:, span(i)], ring_ref.at[slot], sems.at[slot]),)
-
-    def work(weight_ref):
+        return pltpu.make_async_copy(up_ref.at[:, span(i)], ring_ref.at[slot], sems.at[slot])
+
+    def work(down_part, up_part):
         sums = (mine_ref[...] + other_ref[...]).astype(jnp.bfloat16)
         spread = lax.dot_general(
-            sums[samples:], weight_ref[...], (((1,), (1,)), ((), ())), preferred_element_type=jnp.float32
+            sums[samples:], down_part[...], (((1,), (1,)), ((), ())), preferred_element_type=jnp.float32
         )
-        stream(steps, 1, copies)
-        up = ring_ref[lax.rem(step, 2)]
-        gate = jnp.dot(sums[:samples], up, preferred_element_type=jnp.float32)
+        gate = jnp.dot(sums[:samples], up_part[...], preferred_element_type=jnp.float32)
         scale = gate + (bias_ref[...] + 1.0)
         x0 = row_of(x0_ref, groups).astype(jnp.float32)
         crossed_ref[...] = (x0 * scale).astype(jnp.bfloat16)
@@ -284,14 +299,15 @@
                 at = (g * tables + k) * cols
                 back_ref[g, k] = back[:, at : at + cols]
 
-    in_halves(steps, work, first_ref, second_ref)
-
-
-def cross_layer(x0, first, down, up, bias, grad):
+    stream(steps, 1, copy)
+    in_parts(steps, work, first_ref, second_ref, lead_ref, ring_ref.at[lax.rem(step, 2)])
+
+
+def cross_layer(x0, first, lead, down, up, bias, grad):
     owners, tables, samples, cols = x0.shape
     rank = down.shape[1]
-    groups = 8
-    steps = owners // groups
+    steps = STEPS
+    groups = owners // steps
     width = groups * tables * cols
     x0_spec = pl.BlockSpec((groups, tables, samples, cols), lambda i: (i, 0, 0, 0))
     row_spec = pl.BlockSpec((samples, width), lambda i: (0, i))
@@ -301,26 +317,26 @@
     sums, second = pl.pallas_call(
         lambda *refs: project_kernel(steps, *refs),
         grid=(steps,),
-        in_specs=[HELD, HELD, HELD, FAR, FAR],
+        in_specs=[HELD, HELD, HELD, HELD, FAR, FAR],
         out_specs=[sum_spec, HELD],
-        out_shape=[jax.ShapeDtypeStruct((2 * samples, rank), jnp.float32), pltpu.VMEM(first.shape, first.dtype)],
-        scratch_shapes=[ring, pltpu.SemaphoreType.DMA((steps // 2,)), sems],
+        out_shape=[jax.ShapeDtypeStruct((2 * samples, rank), jnp.float32), pltpu.VMEM((down.shape[0] - first.shape[0], rank), down.dtype)],
+        scratch_shapes=[ring, pltpu.SemaphoreType.DMA((steps - EARLY,)), sems],
         compiler_params=params(14),
         cost_estimate=cost(4 * x0.size * rank, 2 * up.size + 4 * x0.size),
         name="project",
-    )(near(x0), near(grad), near(first), far(down), far(up))
+    )(near(x0), near(grad), near(first), near(lead), far(down), far(up))
     other = lax.ppermute(sums, "row", [(0, 1), (1, 0)])
     return pl.pallas_call(
         lambda *refs: cross_kernel(steps, *refs),
         grid=(steps,),
-        in_specs=[sum_spec, sum_spec, HELD, HELD, HELD, FAR, pl.BlockSpec((1, width), lambda i: (0, i)), HELD],
+        in_specs=[sum_spec, sum_spec, HELD, HELD, HELD, HELD, FAR, pl.BlockSpec((1, width), lambda i: (0, i)), HELD],
         out_specs=[row_spec, x0_spec],
         out_shape=[pltpu.HBM((samples, owners * tables * cols), jnp.bfloat16), pltpu.HBM(x0.shape, jnp.bfloat16)],
         scratch_shapes=[pltpu.VMEM((2, rank, width), up.dtype), pltpu.SemaphoreType.DMA((2,))],
         compiler_params=params(14),
         cost_estimate=cost(4 * x0.size * rank, 2 * up.size + 8 * x0.size),
         name="cross",
-    )(sums, other, near(x0), near(first), near(second), far(up), bias, near(grad))
+    )(sums, other, near(x0), near(first), near(second), near(lead), far(up), bias, near(grad))
 
 
 def body(ids, lengths, tables, cross_down, cross_up, bias, grad_out):
@@ -336,9 +352,9 @@
     other = lax.ppermute(sent, "row", swap)
     ids, lengths = jnp.transpose(ids, (1, 2, 0)), jnp.transpose(lengths)
     counts = count(mine, ids, lengths, pair, shards * part)
-    pooled, first = pool(mine, counts, tables, other, cross_down, owners)
+    pooled, first, lead = pool(mine, counts, tables, other, cross_down, cross_up, owners)
     x0 = lax.all_to_all(pooled, "table", split_axis=0, concat_axis=0, tiled=True)
-    crossed, x0_grad = cross_layer(x0, first, cross_down, cross_up, bias.reshape(1, -1), grad_out)
+    crossed, x0_grad = cross_layer(x0, first, lead, cross_down, cross_up, bias.reshape(1, -1), grad_out)
     back = lax.all_to_all(x0_grad, "table", split_axis=0, concat_axis=0, tiled=True)
     cuts = [0, pair // 2, pair]
     incoming = []

time: 182 us -> 180 us (0.989)
  Pallas kernels: 45.5 us -> 43.6 us
where the time goes in v8:
time: 180 us
  blocking collectives  125 us (69%)
  Pallas kernels  43.6 us (24%)
  waiting for transfers between devices  5.26 us (3%)
  starting transfers between devices  3.83 us (2%)
    all_to_all x1, blocking collectives, body(): lax.all_to_all(pooled, 'table', split_axis=0, concat_axis=0, tiled=True)  65.2 us
    all_to_all x1, blocking collectives, body(): lax.all_to_all(x0_grad, 'table', split_axis=0, concat_axis=0, tiled=True)  59.3 us
    pallas_call x1, Pallas kernels, cross_layer(): pl.pallas_call(lambda *refs: cross_kernel(steps, *refs), grid=(steps,), i...  13.6 us
    pallas_call x1, Pallas kernels, cross_layer(): pl.pallas_call(lambda *refs: project_kernel(steps, *refs), grid=(steps,),...  10.3 us
    pallas_call x1, Pallas kernels, count(): pl.pallas_call(count_kernel, grid_spec=pltpu.PrefetchScalarGridSpec(num_s...  9.14 us
    pallas_call x3, Pallas kernels, scatter(): pl.pallas_call(lambda *refs: scatter_kernel(first, away, *refs), grid_spe...  6.9 us
    ppermute x1, waiting for transfers between devices, cross_layer(): other = lax.ppermute(sums, 'row', [(0, 1), (1, 0)])  4.64 us
    pallas_call x1, Pallas kernels, pool(): pl.pallas_call(pool_kernel, grid_spec=pltpu.PrefetchScalarGridSpec(num_sc...  3.64 us
  transfers between devices with their start and end apart: 4, of which 2 were waited for; matrix products, arithmetic and copies ran while one was open for 0% of the time, Pallas kernels for 8%

profile of v8, /device:TPU:1, one launch (start us, length us, event | category | flops | bytes accessed | tf_op | source)
XLA Modules:
  0.0 179.7 jit_solution(13775012813323137126)
XLA Ops:
  0.6 1.0 constant_dynamic-slice_fusion
  1.6 2.1 %collective-permute-start = (bf16[4,256,128]{2,1,0:T(8,128)(2,1)S(1)}, bf16[4,256,128]{2,1,0:T(8,128)(2,1)S(1)}, u32[]{:S(2)}, u32[]{:S(2)}) collective-permute-start(bf16[4,256,128]{2,1,0:T(8,128)(2,1)S(1)} %constant_dynamic-slice_fusion), channel_id=1, source_target_pairs={{0,1},{1,0},{2,3},{3,2},{4,5},{5,4},{6,7},{7,6},{8,9},{9,8},{10,11... | collective-permute-start | bytes 786440 | tf_op jit(solution)/shard_map/ppermute | solution.py:352
  3.7 0.0 copy-start.1
  3.7 9.1 %count.1.counts_ref.refs_1_ = bf16[8,4,512,512]{3,2,1,0:T(8,128)(2,1)S(1)} custom-call(s32[1]{0:T(128)} %bitcast.shard_ref.refs_0_, s32[8,8,4096]{2,1,0:T(8,128)} %bitcast.5, s32[8,4096]{1,0:T(8,128)} %bitcast.6), custom_call_target="tpu_custom_call" | custom-call | flops 67108864 | bytes 1048576 | tf_op jit(solution)/shard_map/count/pallas_call | solution.py:64
  12.9 0.0 collective-permute-done.other_ref
  12.9 0.0 copy-done.1
  12.9 3.6 %pool.1 = (bf16[64,4,64,128]{3,2,1,0:T(8,128)(2,1)S(1)}, bf16[8192,256]{1,0:T(8,128)(2,1)S(1)}, bf16[256,4096]{1,0:T(8,128)(2,1)S(1)}) custom-call(s32[1]{0:T(128)} %bitcast.shard_ref.refs_0_, bf16[8,4,512,512]{3,2,1,0:T(8,128)(2,1)S(1)} %count.1.counts_ref.refs_1_, bf16[8,256,128]{2,1,0:T(8,128)(2,1)S(1)} %copy-done.1, ...), custom_call_target="tpu_custom_call" | custom-call | flops 2147483648 | bytes 33554432 | tf_op jit(solution)/shard_map/pool/pallas_call | solution.py:120
  16.6 0.0 copy-start
  16.6 65.2 %all_to_all.10.refs_0_.refs_2_ = bf16[64,4,64,128]{3,2,1,0:T(8,128)(2,1)S(1)} all-to-all(bf16[64,4,64,128]{3,2,1,0:T(8,128)(2,1)S(1)} %get-tuple-element.9), channel_id=1, replica_groups=mesh['table'=64,'row'=2] {'table'}, dimensions={0} | all-to-all | bytes 8388608 | tf_op jit(solution)/shard_map/all_to_all | solution.py:356
  81.8 0.0 copy-done
  81.8 0.0 copy-start.2
  81.8 10.3 %project.1 = (f32[128,256]{1,0:T(8,128)S(1)}, bf16[24576,256]{1,0:T(8,128)(2,1)S(1)}) custom-call(bf16[64,4,64,128]{3,2,1,0:T(8,128)(2,1)S(1)} %all_to_all.10.refs_0_.refs_2_, bf16[64,32768]{1,0:T(8,128)(2,1)S(1)} %copy-done, bf16[8192,256]{1,0:T(8,128)(2,1)S(1)} %get-tuple-element.10.refs_2_.refs_3_, ...), custom_call_target="tpu_custom_call" | custom-call | flops 2147483648 | bytes 25165824 | tf_op jit(solution)/shard_map/project/pallas_call | solution.py:317
  92.1 0.1 collective-permute-start.1
  92.2 4.6 %collective-permute-done.1.refs_1_ = f32[128,256]{1,0:T(8,128)S(1)} collective-permute-done((f32[128,256]{1,0:T(8,128)S(1)}, f32[128,256]{1,0:T(8,128)S(1)}, u32[]{:S(2)}, u32[]{:S(2)}) %collective-permute-start.1) | collective-permute-done | bytes 131104 | tf_op jit(solution)/shard_map/ppermute | solution.py:328
  96.8 0.0 copy-done.2
  96.8 13.6 %cross.1 = (bf16[64,32768]{1,0:T(8,128)(2,1)}, bf16[64,4,64,128]{3,2,1,0:T(8,128)(2,1)}) custom-call(f32[128,256]{1,0:T(8,128)S(1)} %get-tuple-element.12.refs_0_, f32[128,256]{1,0:T(8,128)S(1)} %collective-permute-done.1.refs_1_, bf16[64,4,64,128]{3,2,1,0:T(8,128)(2,1)S(1)} %all_to_all.10.refs_0_.refs_2_, ...), custom_call_target="tpu_custom_call" | custom-call | flops 2147483648 | bytes 33554432 | tf_op jit(solution)/shard_map/cross/pallas_call | solution.py:329
  110.5 59.3 %all_to_all.11.refs_2_ = bf16[64,4,64,128]{3,2,1,0:T(8,128)(2,1)S(1)} all-to-all(bf16[64,4,64,128]{3,2,1,0:T(8,128)(2,1)} %get-tuple-element.15), channel_id=1, replica_groups=mesh['table'=64,'row'=2] {'table'}, dimensions={0} | all-to-all | bytes 8388608 | tf_op jit(solution)/shard_map/all_to_all | solution.py:358
  169.8 1.6 scatter.4
  171.4 0.4 collective-permute-start.2
  171.8 1.6 scatter.5
  173.4 1.2 collective-permute-start.3
  174.6 3.8 %scatter.3 = bf16[8,256,128]{2,1,0:T(8,128)(2,1)} custom-call(s32[1]{0:T(128)} %bitcast.shard_ref.refs_0_, bf16[8,4,512,512]{3,2,1,0:T(8,128)(2,1)S(1)} %count.1.counts_ref.refs_1_, bf16[64,4,64,128]{3,2,1,0:T(8,128)(2,1)S(1)} %all_to_all.11.refs_2_), custom_call_target="tpu_custom_call" | custom-call | flops 1073741824 | bytes 12582912 | tf_op jit(solution)/shard_map/scatter/pallas_call | solution.py:165
  178.3 0.0 collective-permute-done.2
  178.3 0.6 collective-permute-done.3
  179.0 0.7 maximum_dynamic-update-slice_fusion
Async XLA Ops:
  1.6 11.3 %collective-permute-start = (bf16[4,256,128]{2,1,0:T(8,128)(2,1)S(1)}, bf16[4,256,128]{2,1,0:T(8,128)(2,1)S(1)}, u32[]{:S(2)}, u32[]{:S(2)}) collective-permute-start(bf16[4,256,128]{2,1,0:T(8,128)(2,1)S(1)} %constant_dynamic-slice_fusion), channel_id=1, source_target_pairs={{0,1},{1,0},{2,3},{3,2},{4,5},{5,4},{6,7},{7,6},{8,9},{9,8},{10,11... | collective-permute-start | bytes 786440 | tf_op jit(solution)/shard_map/ppermute | solution.py:352
  3.7 9.2 %copy-start.1 = (bf16[8,256,128]{2,1,0:T(8,128)(2,1)S(1)}, bf16[8,256,128]{2,1,0:T(8,128)(2,1)}, u32[]{:S(2)}) copy-start(bf16[8,256,128]{2,1,0:T(8,128)(2,1)} %own_ref.1) | copy-start | bytes 1572868
  16.6 65.2 %copy-start = (bf16[64,32768]{1,0:T(8,128)(2,1)S(1)}, bf16[64,32768]{1,0:T(8,128)(2,1)}, u32[]{:S(2)}) copy-start(bf16[64,32768]{1,0:T(8,128)(2,1)} %refs_8_.1) | copy-start | bytes 12582916
  81.8 15.1 %copy-start.2 = (f32[32768]{0:T(1024)S(1)}, f32[32768]{0:T(1024)}, u32[]{:S(2)}) copy-start(f32[32768]{0:T(1024)} %param.12) | copy-start | bytes 393220
  92.1 4.7 %collective-permute-start.1 = (f32[128,256]{1,0:T(8,128)S(1)}, f32[128,256]{1,0:T(8,128)S(1)}, u32[]{:S(2)}, u32[]{:S(2)}) collective-permute-start(f32[128,256]{1,0:T(8,128)S(1)} %get-tuple-element.12.refs_0_), channel_id=1, source_target_pairs={{0,1},{1,0},{2,3},{3,2},{4,5},{5,4},{6,7},{7,6},{8,9},{9,8},{10,11... | collective-permute-start | bytes 393224 | tf_op jit(solution)/shard_map/ppermute | solution.py:328
  171.4 7.0 %collective-permute-start.2 = (bf16[2,256,128]{2,1,0:T(8,128)(2,1)S(1)}, bf16[2,256,128]{2,1,0:T(8,128)(2,1)S(1)}, u32[]{:S(2)}, u32[]{:S(2)}) collective-permute-start(bf16[2,256,128]{2,1,0:T(8,128)(2,1)S(1)} %scatter.4), channel_id=1, source_target_pairs={{0,1},{1,0},{2,3},{3,2},{4,5},{5,4},{6,7},{7,6},{8,9},{9,8},{10,11... | collective-permute-start | bytes 393224 | tf_op jit(solution)/shard_map/ppermute | solution.py:363
  173.4 5.6 %collective-permute-start.3 = (bf16[2,256,128]{2,1,0:T(8,128)(2,1)S(1)}, bf16[2,256,128]{2,1,0:T(8,128)(2,1)S(1)}, u32[]{:S(2)}, u32[]{:S(2)}) collective-permute-start(bf16[2,256,128]{2,1,0:T(8,128)(2,1)S(1)} %scatter.5), channel_id=1, source_target_pairs={{0,1},{1,0},{2,3},{3,2},{4,5},{5,4},{6,7},{7,6},{8,9},{9,8},{10,11... | collective-permute-start | bytes 393224 | tf_op jit(solution)/shard_map/ppermute | solution.py:363

commit v9 on v8

--- a/solution.py
+++ b/solution.py
@@ -148,30 +148,35 @@
 
 
 def scatter_kernel(first, away, shard_ref, counts_ref, back_ref, grad_ref):
-    owners, _, samples, width = back_ref.shape
-    back = back_ref[:, 0].reshape(owners * samples, width)
+    owners, together, samples, width = back_ref.shape
     part = grad_ref.shape[1]
     half = 1 - shard_ref[0] if away else shard_ref[0]
     rows = pl.ds(pl.multiple_of(half * part, part), part)
-    k = first + pl.program_id(0)
-    counts = jnp.concatenate([counts_ref[c, k, rows, :] for c in range(counts_ref.shape[0])], axis=1)
-    grad_ref[0] = jnp.dot(counts, back, preferred_element_type=jnp.float32).astype(jnp.bfloat16)
+    for t in range(together):
+        k = first + pl.program_id(0) * together + t
+        back = back_ref[:, t].reshape(owners * samples, width)
+        counts = jnp.concatenate([counts_ref[c, k, rows, :] for c in range(counts_ref.shape[0])], axis=1)
+        grad_ref[t] = jnp.dot(counts, back, preferred_element_type=jnp.float32).astype(jnp.bfloat16)
 
 
 def scatter(shard, counts, back, shards, first, last, away):
     chunks, pair, vocab, chunk = counts.shape
     part = vocab // shards
     owners, _, samples, width = back.shape
+    together = pair // 2
     return pl.pallas_call(
         lambda *refs: scatter_kernel(first, away, *refs),
         grid_spec=pltpu.PrefetchScalarGridSpec(
             num_scalar_prefetch=1,
-            grid=(last - first,),
+            grid=((last - first) // together,),
             in_specs=[
                 HELD,
-                pl.BlockSpec((owners, 1, samples, width), lambda k, s: (0, first + k, 0, 0)),
+                pl.BlockSpec((owners, together, samples, width), lambda k, s: (0, first // together + k, 0, 0)),
             ],
-            out_specs=pl.BlockSpec((1, part, width), lambda k, s: (k if away else s[0] * pair + first + k, 0, 0)),
+            out_specs=pl.BlockSpec(
+                (together, part, width),
+                lambda k, s: (k if away else (s[0] * pair + first) // together + k, 0, 0),
+            ),
         ),
         out_shape=jax.ShapeDtypeStruct((last - first if away else shards * pair, part, width), jnp.bfloat16),
         compiler_params=params(12),

time: 180 us -> 180 us (level)
  no operation moved by 1% of the time
where the time goes in v9:
time: 180 us
  blocking collectives  125 us (69%)
  Pallas kernels  42.7 us (24%)
  waiting for transfers between devices  5.82 us (3%)
  starting transfers between devices  4.01 us (2%)
    all_to_all x1, blocking collectives, body(): lax.all_to_all(pooled, 'table', split_axis=0, concat_axis=0, tiled=True)  65.2 us
    all_to_all x1, blocking collectives, body(): lax.all_to_all(x0_grad, 'table', split_axis=0, concat_axis=0, tiled=True)  59.3 us
    pallas_call x1, Pallas kernels, cross_layer(): pl.pallas_call(lambda *refs: cross_kernel(steps, *refs), grid=(steps,), i...  13.6 us
    pallas_call x1, Pallas kernels, cross_layer(): pl.pallas_call(lambda *refs: project_kernel(steps, *refs), grid=(steps,),...  10.3 us
    pallas_call x1, Pallas kernels, count(): pl.pallas_call(count_kernel, grid_spec=pltpu.PrefetchScalarGridSpec(num_s...  9.14 us
    pallas_call x3, Pallas kernels, scatter(): pl.pallas_call(lambda *refs: scatter_kernel(first, away, *refs), grid_spe...  6 us
    ppermute x1, waiting for transfers between devices, cross_layer(): other = lax.ppermute(sums, 'row', [(0, 1), (1, 0)])  4.64 us
    pallas_call x1, Pallas kernels, pool(): pl.pallas_call(pool_kernel, grid_spec=pltpu.PrefetchScalarGridSpec(num_sc...  3.64 us
  transfers between devices with their start and end apart: 4, of which 2 were waited for; matrix products, arithmetic and copies ran while one was open for 0% of the time, Pallas kernels for 8%

profile of v9, /device:TPU:1, one launch (start us, length us, event | category | flops | bytes accessed | tf_op | source)
XLA Modules:
  0.0 179.5 jit_solution(8311401731638529310)
XLA Ops:
  0.6 1.0 constant_dynamic-slice_fusion
  1.6 2.1 %collective-permute-start = (bf16[4,256,128]{2,1,0:T(8,128)(2,1)S(1)}, bf16[4,256,128]{2,1,0:T(8,128)(2,1)S(1)}, u32[]{:S(2)}, u32[]{:S(2)}) collective-permute-start(bf16[4,256,128]{2,1,0:T(8,128)(2,1)S(1)} %constant_dynamic-slice_fusion), channel_id=1, source_target_pairs={{0,1},{1,0},{2,3},{3,2},{4,5},{5,4},{6,7},{7,6},{8,9},{9,8},{10,11... | collective-permute-start | bytes 786440 | tf_op jit(solution)/shard_map/ppermute | solution.py:357
  3.7 0.0 copy-start.1
  3.7 9.1 %count.1.counts_ref.refs_1_ = bf16[8,4,512,512]{3,2,1,0:T(8,128)(2,1)S(1)} custom-call(s32[1]{0:T(128)} %bitcast.shard_ref.refs_0_, s32[8,8,4096]{2,1,0:T(8,128)} %bitcast.5, s32[8,4096]{1,0:T(8,128)} %bitcast.6), custom_call_target="tpu_custom_call" | custom-call | flops 67108864 | bytes 1048576 | tf_op jit(solution)/shard_map/count/pallas_call | solution.py:64
  12.9 0.0 collective-permute-done.other_ref
  12.9 0.0 copy-done.1
  12.9 3.6 %pool.1 = (bf16[64,4,64,128]{3,2,1,0:T(8,128)(2,1)S(1)}, bf16[8192,256]{1,0:T(8,128)(2,1)S(1)}, bf16[256,4096]{1,0:T(8,128)(2,1)S(1)}) custom-call(s32[1]{0:T(128)} %bitcast.shard_ref.refs_0_, bf16[8,4,512,512]{3,2,1,0:T(8,128)(2,1)S(1)} %count.1.counts_ref.refs_1_, bf16[8,256,128]{2,1,0:T(8,128)(2,1)S(1)} %copy-done.1, ...), custom_call_target="tpu_custom_call" | custom-call | flops 2147483648 | bytes 33554432 | tf_op jit(solution)/shard_map/pool/pallas_call | solution.py:120
  16.6 0.0 copy-start
  16.6 65.2 %all_to_all.10.refs_0_.refs_2_ = bf16[64,4,64,128]{3,2,1,0:T(8,128)(2,1)S(1)} all-to-all(bf16[64,4,64,128]{3,2,1,0:T(8,128)(2,1)S(1)} %get-tuple-element.9), channel_id=1, replica_groups=mesh['table'=64,'row'=2] {'table'}, dimensions={0} | all-to-all | bytes 8388608 | tf_op jit(solution)/shard_map/all_to_all | solution.py:361
  81.8 0.0 copy-done
  81.8 0.0 copy-start.2
  81.8 10.3 %project.1 = (f32[128,256]{1,0:T(8,128)S(1)}, bf16[24576,256]{1,0:T(8,128)(2,1)S(1)}) custom-call(bf16[64,4,64,128]{3,2,1,0:T(8,128)(2,1)S(1)} %all_to_all.10.refs_0_.refs_2_, bf16[64,32768]{1,0:T(8,128)(2,1)S(1)} %copy-done, bf16[8192,256]{1,0:T(8,128)(2,1)S(1)} %get-tuple-element.10.refs_2_.refs_3_, ...), custom_call_target="tpu_custom_call" | custom-call | flops 2147483648 | bytes 25165824 | tf_op jit(solution)/shard_map/project/pallas_call | solution.py:322
  92.1 0.1 collective-permute-start.1
  92.2 4.6 %collective-permute-done.1.refs_1_ = f32[128,256]{1,0:T(8,128)S(1)} collective-permute-done((f32[128,256]{1,0:T(8,128)S(1)}, f32[128,256]{1,0:T(8,128)S(1)}, u32[]{:S(2)}, u32[]{:S(2)}) %collective-permute-start.1) | collective-permute-done | bytes 131104 | tf_op jit(solution)/shard_map/ppermute | solution.py:333
  96.8 0.0 copy-done.2
  96.8 13.6 %cross.1 = (bf16[64,32768]{1,0:T(8,128)(2,1)}, bf16[64,4,64,128]{3,2,1,0:T(8,128)(2,1)}) custom-call(f32[128,256]{1,0:T(8,128)S(1)} %get-tuple-element.12.refs_0_, f32[128,256]{1,0:T(8,128)S(1)} %collective-permute-done.1.refs_1_, bf16[64,4,64,128]{3,2,1,0:T(8,128)(2,1)S(1)} %all_to_all.10.refs_0_.refs_2_, ...), custom_call_target="tpu_custom_call" | custom-call | flops 2147483648 | bytes 33554432 | tf_op jit(solution)/shard_map/cross/pallas_call | solution.py:334
  110.5 59.3 %all_to_all.11.refs_2_ = bf16[64,4,64,128]{3,2,1,0:T(8,128)(2,1)S(1)} all-to-all(bf16[64,4,64,128]{3,2,1,0:T(8,128)(2,1)} %get-tuple-element.15), channel_id=1, replica_groups=mesh['table'=64,'row'=2] {'table'}, dimensions={0} | all-to-all | bytes 8388608 | tf_op jit(solution)/shard_map/all_to_all | solution.py:363
  169.8 1.3 scatter.4
  171.1 0.6 collective-permute-start.2
  171.7 1.3 scatter.5
  172.9 1.2 collective-permute-start.3
  174.1 3.5 %scatter.3 = bf16[8,256,128]{2,1,0:T(8,128)(2,1)} custom-call(s32[1]{0:T(128)} %bitcast.shard_ref.refs_0_, bf16[8,4,512,512]{3,2,1,0:T(8,128)(2,1)S(1)} %count.1.counts_ref.refs_1_, bf16[64,4,64,128]{3,2,1,0:T(8,128)(2,1)S(1)} %all_to_all.11.refs_2_), custom_call_target="tpu_custom_call" | custom-call | flops 1073741824 | bytes 12582912 | tf_op jit(solution)/shard_map/scatter/pallas_call | solution.py:167
  177.6 0.0 collective-permute-done.2
  177.6 1.2 collective-permute-done.3
  178.8 0.7 maximum_dynamic-update-slice_fusion
Async XLA Ops:
  1.6 11.3 %collective-permute-start = (bf16[4,256,128]{2,1,0:T(8,128)(2,1)S(1)}, bf16[4,256,128]{2,1,0:T(8,128)(2,1)S(1)}, u32[]{:S(2)}, u32[]{:S(2)}) collective-permute-start(bf16[4,256,128]{2,1,0:T(8,128)(2,1)S(1)} %constant_dynamic-slice_fusion), channel_id=1, source_target_pairs={{0,1},{1,0},{2,3},{3,2},{4,5},{5,4},{6,7},{7,6},{8,9},{9,8},{10,11... | collective-permute-start | bytes 786440 | tf_op jit(solution)/shard_map/ppermute | solution.py:357
  3.7 9.2 %copy-start.1 = (bf16[8,256,128]{2,1,0:T(8,128)(2,1)S(1)}, bf16[8,256,128]{2,1,0:T(8,128)(2,1)}, u32[]{:S(2)}) copy-start(bf16[8,256,128]{2,1,0:T(8,128)(2,1)} %own_ref.1) | copy-start | bytes 1572868
  16.6 65.2 %copy-start = (bf16[64,32768]{1,0:T(8,128)(2,1)S(1)}, bf16[64,32768]{1,0:T(8,128)(2,1)}, u32[]{:S(2)}) copy-start(bf16[64,32768]{1,0:T(8,128)(2,1)} %refs_8_.1) | copy-start | bytes 12582916
  81.8 15.1 %copy-start.2 = (f32[32768]{0:T(1024)S(1)}, f32[32768]{0:T(1024)}, u32[]{:S(2)}) copy-start(f32[32768]{0:T(1024)} %param.12) | copy-start | bytes 393220
  92.1 4.7 %collective-permute-start.1 = (f32[128,256]{1,0:T(8,128)S(1)}, f32[128,256]{1,0:T(8,128)S(1)}, u32[]{:S(2)}, u32[]{:S(2)}) collective-permute-start(f32[128,256]{1,0:T(8,128)S(1)} %get-tuple-element.12.refs_0_), channel_id=1, source_target_pairs={{0,1},{1,0},{2,3},{3,2},{4,5},{5,4},{6,7},{7,6},{8,9},{9,8},{10,11... | collective-permute-start | bytes 393224 | tf_op jit(solution)/shard_map/ppermute | solution.py:333
  171.1 6.5 %collective-permute-start.2 = (bf16[2,256,128]{2,1,0:T(8,128)(2,1)S(1)}, bf16[2,256,128]{2,1,0:T(8,128)(2,1)S(1)}, u32[]{:S(2)}, u32[]{:S(2)}) collective-permute-start(bf16[2,256,128]{2,1,0:T(8,128)(2,1)S(1)} %scatter.4), channel_id=1, source_target_pairs={{0,1},{1,0},{2,3},{3,2},{4,5},{5,4},{6,7},{7,6},{8,9},{9,8},{10,11... | collective-permute-start | bytes 393224 | tf_op jit(solution)/shard_map/ppermute | solution.py:368
  172.9 5.9 %collective-permute-start.3 = (bf16[2,256,128]{2,1,0:T(8,128)(2,1)S(1)}, bf16[2,256,128]{2,1,0:T(8,128)(2,1)S(1)}, u32[]{:S(2)}, u32[]{:S(2)}) collective-permute-start(bf16[2,256,128]{2,1,0:T(8,128)(2,1)S(1)} %scatter.5), channel_id=1, source_target_pairs={{0,1},{1,0},{2,3},{3,2},{4,5},{5,4},{6,7},{7,6},{8,9},{9,8},{10,11... | collective-permute-start | bytes 393224 | tf_op jit(solution)/shard_map/ppermute | solution.py:368
